TPU v7x, 32 devices: a whole 2x2x4 slice. The times are simulated.
32 devices in a mesh: gx: 2 (over x), gy: 4 (over z), gz: 4 (over y, core).
Axes of the slice: x: 2, y: 2, z: 4, core: 2. Of those that a mesh axis runs over, the one named last changes fastest.
Arguments:
- field: float32 [16, 512, 1024], P('gz', 'gx', 'gy'), may hold values from -6 to 6
Outputs:
- coefficients: float32 [16, 512, 1024], P('gz', 'gx', 'gy')
- coarse_values: float32 [8, 256, 512], P('gz', 'gx', 'gy')
All inputs are finite; a program needn't handle non-finite values.
Results may differ from a plain program's by a relative error of at most 0.00022.
Values sent between devices are 32-bit elements; how exact they have to be, the bound alone decides.
No kernel may reach another device: no remote copies, remote signals or barrier semaphores. Data moves between devices by JAX's collectives and lax.ppermute only.
A program may use at most 64 MiB of HBM per device.

v0:
```python
import jax
import jax.numpy as jnp
from jax import lax
from jax.sharding import PartitionSpec as P


def padded(cells, sides, width):
    for axis, dim in sides:
        count = lax.axis_size(axis)
        ends = count - 1
        head = lax.slice_in_dim(cells, 0, width, axis=dim)
        tail = lax.slice_in_dim(cells, cells.shape[dim] - width, cells.shape[dim], axis=dim)
        cells = jnp.concatenate(
            [
                lax.ppermute(tail, axis, [(i, (i + 1) % count) for i in range(ends)]),
                cells,
                lax.ppermute(head, axis, [((i + 1) % count, i) for i in range(ends)]),
            ],
            axis=dim,
        )
    return cells


def lift_rim(values, along, margin):
    extent = values.shape[along]
    center = lax.slice_in_dim(values, 1, extent - 1, axis=along)
    before = lax.slice_in_dim(values, 0, extent - 2, axis=along)
    behind = lax.slice_in_dim(values, 2, extent, axis=along)
    offsets = jnp.arange(extent - 2) + 1 - margin
    layout = [1, 1, 1]
    layout[along] = extent - 2
    is_odd = (offsets % 2 == 1).reshape(layout)
    return jnp.where(is_odd, 0.5 * (before + behind), center)


def inside_mask(extent, along, margin, device, count, shard):
    offsets = jnp.arange(extent) - margin
    global_index = device * shard + offsets
    layout = [1, 1, 1]
    layout[along] = extent
    return ((global_index >= 0) & (global_index < count * shard)).reshape(layout)


def restrict_rim(values, along, leading):
    extent = values.shape[along]
    before = lax.slice_in_dim(values, 0, extent - 2, axis=along)
    center = lax.slice_in_dim(values, 1, extent - 1, axis=along)
    behind = lax.slice_in_dim(values, 2, extent, axis=along)
    weighted = (before + 4.0 * center + behind) / 6.0
    layout = [1, 1, 1]
    layout[along] = extent - 2
    zeroed = ((jnp.arange(extent - 2) == 0) & leading).reshape(layout)
    weighted = jnp.where(zeroed, 0.0, weighted)
    count_all = extent - 2
    even_nodes = lax.slice_in_dim(weighted, 1, count_all, stride=2, axis=along)
    left_side = lax.slice_in_dim(weighted, 0, count_all - 1, stride=2, axis=along)
    right_side = lax.slice_in_dim(weighted, 2, count_all, stride=2, axis=along)
    return even_nodes + 0.5 * (left_side + right_side)


def solve_lines(loads, along):
    rotated = jnp.moveaxis(loads, along, 1)
    length = rotated.shape[1]
    position = jnp.arange(length)
    one_third = jnp.ones((length,), rotated.dtype) / 3.0
    below_diag = jnp.broadcast_to(
        jnp.where(position == 0, 0.0, one_third).astype(rotated.dtype), rotated.shape[:-1]
    )
    above_diag = jnp.broadcast_to(
        jnp.where(position == length - 1, 0.0, one_third).astype(rotated.dtype), rotated.shape[:-1]
    )
    middle = jnp.broadcast_to(4.0 * one_third, rotated.shape[:-1])
    solved = lax.linalg.tridiagonal_solve(below_diag, middle, above_diag, rotated)
    return jnp.moveaxis(solved, 1, along)


def on_device(field):
    depth, height, breadth = field.shape
    extended = padded(field, (("gz", 0), ("gx", 1), ("gy", 2)), 3)
    interpolant = lift_rim(lift_rim(lift_rim(extended, 1, 3), 2, 3), 0, 3)
    interior = extended[1:-1, 1:-1, 1:-1]
    coeff_rim = interior - interpolant
    coefficients = coeff_rim[2:-2, 2:-2, 2:-2]
    usable = coeff_rim[:-1, :-1, :-1]
    inside = inside_mask(depth + 3, 0, 2, lax.axis_index("gz"), lax.axis_size("gz"), depth)
    inside = inside & inside_mask(
        height + 3, 1, 2, lax.axis_index("gx"), lax.axis_size("gx"), height
    )
    inside = inside & inside_mask(
        breadth + 3, 2, 2, lax.axis_index("gy"), lax.axis_size("gy"), breadth
    )
    usable = jnp.where(inside, usable, 0.0)
    loads = restrict_rim(usable, 1, lax.axis_index("gx") == 0)
    loads = restrict_rim(loads, 2, lax.axis_index("gy") == 0)
    loads = restrict_rim(loads, 0, lax.axis_index("gz") == 0)
    owned_lines = lax.all_to_all(loads, "gx", split_axis=2, concat_axis=1, tiled=True)
    solved = lax.all_to_all(
        solve_lines(owned_lines, 1), "gx", split_axis=1, concat_axis=2, tiled=True
    )
    owned_lines = lax.all_to_all(solved, "gy", split_axis=1, concat_axis=2, tiled=True)
    solved = lax.all_to_all(
        solve_lines(owned_lines, 2), "gy", split_axis=2, concat_axis=1, tiled=True
    )
    owned_lines = lax.all_to_all(solved, "gz", split_axis=2, concat_axis=0, tiled=True)
    solved = lax.all_to_all(
        solve_lines(owned_lines, 0), "gz", split_axis=0, concat_axis=2, tiled=True
    )
    coarse_values = field[::2, ::2, ::2] + solved
    return (coefficients, coarse_values)


def solution(mesh):
    return jax.shard_map(
        on_device,
        mesh=mesh,
        in_specs=(P("gz", "gx", "gy"),),
        out_specs=(P("gz", "gx", "gy"), P("gz", "gx", "gy")),
        check_vma=False,
    )
```

profile of v0, /device:TPU:0, one launch (start us, length us, event | category | flops | bytes accessed | tf_op | source)
XLA Modules:
  0.0 522.2 jit_solution(3342938523679267538)
XLA Ops:
  3.0 3.2 collective-permute-start
  13.9 4.2 collective-permute-start.2
  19.8 4.2 collective-permute-done.3
  28.2 3.5 collective-permute-start.4
  41.3 3.4 pad_maximum_fusion
  51.4 3.2 slice.3921
  54.6 3.1 slice.3922
  57.7 3.1 slice.3923
  64.0 17.8 %slice.3927 = f32[7,128,128]{2,1,0:T(8,128)S(1)} slice(f32[7,128,257]{2,1,0:T(8,128)S(1)} %fusion.488), slice={[0:7:1], [0:128:1], [1:257:2]} | slice | bytes 917504 | tf_op jit(solution)/shard_map/slice | solution.py:55
  81.8 17.8 %slice.3928 = f32[7,128,128]{2,1,0:T(8,128)S(1)} slice(f32[7,128,257]{2,1,0:T(8,128)S(1)} %fusion.488), slice={[0:7:1], [0:128:1], [0:256:2]} | slice | bytes 917504 | tf_op jit(solution)/shard_map/slice | solution.py:56
  99.6 18.2 %slice.3929 = f32[7,128,128]{2,1,0:T(8,128)S(1)} slice(f32[7,128,257]{2,1,0:T(8,128)S(1)} %fusion.488), slice={[0:7:1], [0:128:1], [2:257:2]} | slice | bytes 917504 | tf_op jit(solution)/shard_map/slice | solution.py:57
  118.7 3.4 all-to-all-start
  122.8 3.7 all-to-all-done
  128.5 45.5 %while.64 = (s32[]{:T(128)}, f32[2]{0:T(128)S(1)}, f32[2,64]{1,0:T(2,128)S(1)}, f32[7,32,2]{1,0,2:T(8,128)S(1)}, f32[7,32,2,64]{3,2,1,0:T(2,128)S(1)}, /*index=5...) while((s32[]{:T(128)}, f32[2]{0:T(128)S(1)}, ...), condition=%wide.region_1.2_spmd, body=%wide.region_0.1_spmd.sunk | while | flops 12513 | bytes 263941 | solution.py:73
  175.0 38.0 %multiply_subtract_fusion.131 = (f32[2]{0:T(128)S(1)}, f32[2]{0:T(128)S(1)}, f32[2]{0:T(128)S(1)}, f32[2]{0:T(128)S(1)}, f32[2]{0:T(128)S(1)}, /*index=5*/f32[2]...) fusion(f32[]{:T(128)} %bitcast.556, ...), kind=kLoop, calls=%fused_computation.1558 | loop fusion | flops 184 | bytes 740 | tf_op jit(solution)/shard_map/vmap()/eval_jaxpr/sub | solution.py:73
  237.9 11.7 %while.65 = (s32[]{:T(128)}, f32[2,64]{1,0:T(2,128)S(1)}, f32[7,32,2,64]{3,2,1,0:T(2,128)S(1)}, f32[7,32,2,64]{3,2,1,0:T(2,128)S(1)}, f32[7,32,2]{2,1,0:T(8,128)...) while((s32[]{:T(128)}, f32[2,64]{1,0:T(2,128)S(1)}, ...), condition=%wide.region_3.4_spmd, body=%wide.region_2.3_spmd.sunk | while | flops 12065 | bytes 188245 | solution.py:73
  252.2 3.4 all-to-all-start.1
  256.3 3.7 all-to-all-done.1
  262.8 4.9 all-to-all-start.2
  268.4 5.2 all-to-all-done.2
  275.4 97.6 %while.66 = (s32[]{:T(128)}, f32[2]{0:T(128)S(1)}, f32[2,32]{1,0:T(2,128)S(1)}, f32[15,32,2]{1,0,2:T(8,128)S(1)}, f32[15,32,2,32]{3,2,1,0:T(2,128)S(1)}, /*index...) while((s32[]{:T(128)}, f32[2]{0:T(128)S(1)}, ...), condition=%wide.region_5.6_spmd, body=%wide.region_4.5_spmd.sunk | while | flops 6685 | bytes 231797 | solution.py:73
  374.9 38.2 %multiply_subtract_fusion.100 = (f32[2]{0:T(128)S(1)}, f32[2]{0:T(128)S(1)}, f32[2]{0:T(128)S(1)}, f32[2]{0:T(128)S(1)}, f32[2]{0:T(128)S(1)}, /*index=5*/f32[2]...) fusion(f32[]{:T(128)} %bitcast.725, ...), kind=kLoop, calls=%fused_computation.1527 | loop fusion | flops 184 | bytes 740 | tf_op jit(solution)/shard_map/vmap()/eval_jaxpr/sub | solution.py:73
  416.3 19.5 %subtract_divide_fusion.38 = (f32[2,32]{1,0:T(2,128)S(1)}, f32[2,32]{1,0:T(2,128)S(1)}, f32[2,32]{1,0:T(2,128)S(1)}, f32[2,32]{1,0:T(2,128)S(1)}, f32[2,32]{1,0:...) fusion(f32[2,32]{1,0:T(2,128)S(1)} %get-tuple-element.597, ...), kind=kLoop, calls=%fused_computation.1463 | loop fusion | flops 5952 | bytes 16500 | tf_op jit(solution)/shard_map/vmap()/eval_jaxpr/div | solution.py:73
  439.7 25.1 %while.67 = (s32[]{:T(128)}, f32[2,32]{1,0:T(2,128)S(1)}, f32[15,32,2,32]{3,2,1,0:T(2,128)S(1)}, f32[15,32,2,32]{3,2,1,0:T(2,128)S(1)}, f32[15,32,2]{2,1,0:T(8,1...) while((s32[]{:T(128)}, f32[2,32]{1,0:T(2,128)S(1)}, ...), condition=%wide.region_7.8_spmd, body=%wide.region_6.7_spmd.sunk | while | flops 6049 | bytes 179029 | solution.py:73
  470.6 3.3 all-to-all-start.3
  475.3 5.1 all-to-all-done.3
  482.8 7.9 %all-to-all-start.4 = ((f32[2,128,128]{1,0,2:T(2,128)}), f32[2,128,128]{1,0,2:T(2,128)S(1)}, u32[]{:S(2)}, u32[]{:S(2)}) async-start(f32[2,128,128]{1,0,2:T(2,128)} %copy.1623), calls=%async_computation.4 | async-start | bytes 262144 | tf_op jit(solution)/shard_map/all_to_all | solution.py:104
  500.1 3.6 constant_dynamic-update-slice_fusion.201
  503.8 3.6 multiply_subtract_fusion.69
  509.2 3.3 all-to-all-start.5
  512.6 5.5 %slice.3914 = f32[2,128,128]{2,1,0:T(8,128)S(1)} slice(f32[4,256,256]{2,1,0:T(8,128)} %param.9), slice={[0:4:2], [0:256:2], [0:256:2]} | slice | bytes 262144 | tf_op jit(solution)/shard_map/slice | solution.py:108
  518.2 2.7 slice.4363
  (2929 shorter events, 270.2 us)
Async XLA Ops:
  3.0 8.3 %collective-permute-start = (f32[3,256,256]{2,1,0:T(8,128)S(1)}, f32[3,256,256]{2,1,0:T(8,128)}, u32[]{:S(2)}, u32[]{:S(2)}) collective-permute-start(f32[3,256,256]{2,1,0:T(8,128)S(1)} %get-tuple-element.1454), channel_id=1, source_target_pairs={{0,1},{1,2},{2,3},{4,5},{5,6},{6,7},{8,9},{9,10},{10,11},{12,13},{... | collective-permute-start | bytes 2359304 | tf_op jit(solution)/shard_map/ppermute | solution.py:15
  6.3 7.6 %collective-permute-start.1 = (f32[3,256,256]{2,1,0:T(8,128)}, f32[3,256,256]{2,1,0:T(8,128)S(1)}, u32[]{:S(2)}, u32[]{:S(2)}) collective-permute-start(f32[3,256,256]{2,1,0:T(8,128)} %get-tuple-element.1453), channel_id=1, source_target_pairs={{1,0},{2,1},{3,2},{5,4},{6,5},{7,6},{9,8},{10,9},{11,10},{13,12},{... | collective-permute-start | bytes 2359304 | tf_op jit(solution)/shard_map/ppermute | solution.py:17
  13.9 5.9 %collective-permute-start.2 = (f32[10,3,256]{2,1,0:T(4,128)S(1)}, f32[10,3,256]{2,1,0:T(4,128)S(1)}, u32[]{:S(2)}, u32[]{:S(2)}) collective-permute-start(f32[10,3,256]{2,1,0:T(4,128)S(1)} %get-tuple-element.1451), channel_id=1, source_target_pairs={{0,16},{1,17},{2,18},{3,19},{4,20},{5,21},{6,22},{7,23},{8,24},{9,... | collective-permute-start | bytes 92168 | tf_op jit(solution)/shard_map/ppermute | solution.py:15
  18.2 5.9 %collective-permute-start.3 = (f32[10,3,256]{2,1,0:T(4,128)S(1)}, f32[10,3,256]{2,1,0:T(4,128)S(1)}, u32[]{:S(2)}, u32[]{:S(2)}) collective-permute-start(f32[10,3,256]{2,1,0:T(4,128)S(1)} %get-tuple-element.1452), channel_id=1, source_target_pairs={{16,0},{17,1},{18,2},{19,3},{20,4},{21,5},{22,6},{23,7},{24,8},{25... | collective-permute-start | bytes 92168 | tf_op jit(solution)/shard_map/ppermute | solution.py:17
  28.2 8.6 %collective-permute-start.4 = (f32[10,262,3]{1,2,0:T(4,128)S(1)}, f32[10,262,3]{1,2,0:T(4,128)S(1)}, u32[]{:S(2)}, u32[]{:S(2)}) collective-permute-start(f32[10,262,3]{1,2,0:T(4,128)S(1)} %copy.1472), channel_id=1, source_target_pairs={{0,4},{4,8},{8,12},{1,5},{5,9},{9,13},{2,6},{6,10},{10,14},{3,7},{... | collective-permute-start | bytes 94328 | tf_op jit(solution)/shard_map/ppermute | solution.py:15
  33.7 6.1 %collective-permute-start.5 = (f32[10,262,3]{1,2,0:T(4,128)S(1)}, f32[10,262,3]{1,2,0:T(4,128)S(1)}, u32[]{:S(2)}, u32[]{:S(2)}) collective-permute-start(f32[10,262,3]{1,2,0:T(4,128)S(1)} %copy.1473), channel_id=1, source_target_pairs={{4,0},{8,4},{12,8},{5,1},{9,5},{13,9},{6,2},{10,6},{14,10},{7,3},{... | collective-permute-start | bytes 94328 | tf_op jit(solution)/shard_map/ppermute | solution.py:17
  48.9 1.7 copy-start
  118.7 7.8 %all-to-all-start = ((f32[2,128,128]{1,0,2:T(2,128)}), f32[2,128,128]{1,0,2:T(2,128)S(1)}, u32[]{:S(2)}, u32[]{:S(2)}) async-start(f32[2,128,128]{1,0,2:T(2,128)} %copy.1477), calls=%async_computation | async-start | bytes 262144 | tf_op jit(solution)/shard_map/all_to_all | solution.py:96
  252.2 7.8 %all-to-all-start.1 = ((f32[2,1,16384]{2,1,0:T(1,128)}), f32[2,1,16384]{2,1,0:T(1,128)S(1)}, u32[]{:S(2)}, u32[]{:S(2)}) async-start(f32[2,1,16384]{2,1,0:T(1,128)} %reshape.2723), calls=%async_computation.1 | async-start | bytes 262144 | tf_op jit(solution)/shard_map/all_to_all | solution.py:97
  262.8 10.8 %all-to-all-start.2 = ((f32[2,128,128]{2,0,1:T(2,128)}), f32[2,128,128]{2,0,1:T(2,128)S(1)}, u32[]{:S(2)}, u32[]{:S(2)}) async-start(f32[2,128,128]{2,0,1:T(2,128)} %copy.1517), calls=%async_computation.2 | async-start | bytes 262144 | tf_op jit(solution)/shard_map/all_to_all | solution.py:100
  470.6 9.8 %all-to-all-start.3 = ((f32[4,1,8192]{2,1,0:T(1,128)}), f32[4,1,8192]{2,1,0:T(1,128)S(1)}, u32[]{:S(2)}, u32[]{:S(2)}) async-start(f32[4,1,8192]{2,1,0:T(1,128)} %reshape.2725), calls=%async_computation.3 | async-start | bytes 262144 | tf_op jit(solution)/shard_map/all_to_all | solution.py:101
  482.8 17.2 %all-to-all-start.4 = ((f32[2,128,128]{1,0,2:T(2,128)}), f32[2,128,128]{1,0,2:T(2,128)S(1)}, u32[]{:S(2)}, u32[]{:S(2)}) async-start(f32[2,128,128]{1,0,2:T(2,128)} %copy.1623), calls=%async_computation.4 | async-start | bytes 262144 | tf_op jit(solution)/shard_map/all_to_all | solution.py:104
  509.2 11.7 %all-to-all-start.5 = ((f32[8,128,32]{1,2,0:T(8,128)}), f32[8,128,32]{1,2,0:T(8,128)S(1)}, u32[]{:S(2)}, u32[]{:S(2)}) async-start(f32[8,128,32]{1,2,0:T(8,128)} %maximum_bitcast_fusion.1), calls=%async_computation.5 | async-start | bytes 262144 | tf_op jit(solution)/shard_map/all_to_all | solution.py:105
where the time goes:
time: 532 us; the launch traced here: 522 us
  other arithmetic  244 us (46%)
  local copies, waits for them, and re-layouts  198 us (37%)
  starting transfers between devices  41 us (8%)
  waiting for transfers between devices  23.7 us (4%)
  between operations  12.5 us (2%)
    sub x265, other arithmetic, solve_lines(): lax.linalg.tridiagonal_solve(below_diag, middle, above_diag, rotated)  90.8 us
    while x990, other arithmetic  82 us
    broadcast_in_dim x829, local copies, waits for them, and re-layouts, solve_lines(): lax.linalg.tridiagonal_solve(below_diag, middle, above_diag, rotated)  76.5 us
    div x48, other arithmetic, solve_lines(): lax.linalg.tridiagonal_solve(below_diag, middle, above_diag, rotated)  26.3 us
    unnamed x49, other arithmetic  25.6 us
    slice x2, local copies, waits for them, and re-layouts, restrict_rim(): right_side = lax.slice_in_dim(weighted, 2, count_all, stride=2, axis=along)  21.3 us
    slice x2, local copies, waits for them, and re-layouts, restrict_rim(): even_nodes = lax.slice_in_dim(weighted, 1, count_all, stride=2, axis=along)  21 us
    slice x2, local copies, waits for them, and re-layouts, restrict_rim(): lax.slice_in_dim(weighted, 0, count_all - 1, stride=2, axis=along)  20.8 us
  transfers between devices with their start and end apart: 12, of which 7 were waited for; matrix products, arithmetic and copies ran while one was open for 4% of the time, Pallas kernels for 0%

commit v1 on v0

v1 whole, which is shorter than its diff:
```python
import functools

import jax
import jax.numpy as jnp
import numpy as np
from jax import lax
from jax.experimental import pallas as pl
from jax.experimental.pallas import tpu as pltpu
from jax.sharding import PartitionSpec as P

RATIO = 2.0 - np.sqrt(3.0)
VMEM_LIMIT = 48 * 1024 * 1024


def inverse_mass(i, j, n):
    low, high = np.minimum(i, j), np.maximum(i, j)
    sign = np.where((high - low) % 2 == 0, 1.0, -1.0)
    value = RATIO ** (high - low + 1.0) * (1.0 - RATIO ** (2.0 * (low + 1))) * (1.0 - RATIO ** (2.0 * (n - high)))
    return 3.0 * sign * value / ((1.0 - RATIO**2) * (1.0 - RATIO ** (2.0 * (n + 1))))


def line_operator(i, k, n):
    a = k // 2
    odd = k % 2 == 1

    def at(j):
        inside = (j >= 0) & (j < n)
        return np.where(inside, inverse_mass(i, np.clip(j, 0, n - 1), n), 0.0)

    even_part = np.where(a == 0, 9.0, 10.0) * at(a) + at(a - 1) + at(a + 1)
    odd_part = 6.0 * at(a) + 6.0 * at(a + 1)
    return np.where(odd, odd_part, even_part) / 12.0


def line_tables(parts, m):
    n = parts * m
    node, fine = np.arange(m), np.arange(2 * m)
    block = np.zeros((parts, m, 2 * m))
    to_right, to_left = np.zeros((parts, 2 * m)), np.zeros((parts, 2 * m))
    from_left, from_right = np.zeros((parts, m)), np.zeros((parts, m))
    weight_left, weight_right = np.zeros((parts, parts)), np.zeros((parts, parts))
    first = np.zeros((parts, m))
    first_right = np.zeros((parts,))
    for p in range(parts):
        k = p * 2 * m + fine
        block[p] = line_operator((p * m + node)[:, None], k[None, :], n)
        if p + 1 < parts:
            to_right[p] = line_operator(np.full_like(k, (p + 1) * m), k, n)
        if p > 0:
            to_left[p] = line_operator(np.full_like(k, p * m - 1), k, n)
        from_left[p] = (-RATIO) ** node * (1 - RATIO ** (2.0 * (n - p * m - node))) / (1 - RATIO ** (2.0 * (n - p * m)))
        from_right[p] = (
            (-RATIO) ** (m - 1 - node) * (1 - RATIO ** (2.0 * (p * m + node + 1))) / (1 - RATIO ** (2.0 * (p + 1) * m))
        )
        for q in range(parts):
            if q < p:
                weight_left[p, q] = (
                    (-RATIO) ** ((p - q - 1) * m)
                    * (1 - RATIO ** (2.0 * (n - p * m)))
                    / (1 - RATIO ** (2.0 * (n - (q + 1) * m)))
                )
            if q > p:
                weight_right[p, q] = (
                    (-RATIO) ** ((q - p - 1) * m) * (1 - RATIO ** (2.0 * (p + 1) * m)) / (1 - RATIO ** (2.0 * q * m))
                )
    first[0] = inverse_mass(node, np.zeros_like(node), n) / 3.0
    if parts > 1:
        first_right[0] = -inverse_mass(np.array(m), np.array(0), n) / 3.0
    return {
        "block": block,
        "to_right": to_right,
        "to_left": to_left,
        "from_left": from_left,
        "from_right": from_right,
        "weight_left": weight_left,
        "weight_right": weight_right,
        "first": first,
        "first_right": first_right,
    }


def even_selector(m):
    pick = np.zeros((2 * m, m))
    pick[2 * np.arange(m), np.arange(m)] = 1.0
    return pick


def lift_matrix(m):
    up = np.zeros((2 * m, m + 1))
    up[2 * np.arange(m), np.arange(m)] = 1.0
    up[2 * np.arange(m) + 1, np.arange(m)] = 0.5
    up[2 * np.arange(m) + 1, np.arange(m) + 1] = 0.5
    return up


def f32(values):
    return np.asarray(values, np.float32)


def combine_tables(sizes, tx, ty, tz, mz):
    gx, gy, gz = sizes
    count = gx * gy * gz
    sender = np.arange(count)
    qx, qy, qz = sender // (gy * gz), (sender // gz) % gy, sender % gz
    rows = 32
    wx, wy, wz = (np.zeros((parts, rows, count, 4)) for parts in sizes)

    def side(t, p, q, which):
        if which == 0:
            return (q == p) * 1.0
        return (t["weight_left"] if which == 1 else t["weight_right"])[p][q]

    for sx in range(3):
        for sy in range(3):
            if sx == 0 and sy == 0:
                continue
            for z in range(mz):
                row = (sx * 3 + sy) * mz + z
                for p in range(gx):
                    wx[p, row] = side(tx, p, qx, sx)[:, None]
                for p in range(gy):
                    wy[p, row] = side(ty, p, qy, sy)[:, None]
                for p in range(gz):
                    wz[p, row, :, z] += qz == p
                    wz[p, row, :, 0] += tz["weight_left"][p][qz] * tz["from_left"][p, z]
                    wz[p, row, :, 0] += tz["weight_right"][p][qz] * tz["from_right"][p, z]
    for case, (ox, oy) in enumerate(((1, 0), (0, 1), (1, 1))):
        for layer in range(mz + 1):
            row = 9 * mz + case * (mz + 1) + layer
            for p in range(gx):
                wx[p, row] = (qx == p + ox)[:, None]
            for p in range(gy):
                wy[p, row] = (qy == p + oy)[:, None]
            for p in range(gz):
                if layer < mz:
                    wz[p, row, :, mz + layer] = qz == p
                else:
                    wz[p, row, :, mz] = qz == p + 1
    return tuple(f32(w.reshape(w.shape[0], rows, count * 4)) for w in (wx, wy, wz))


def dot(a, b, contract=((1,), (0,))):
    return lax.dot_general(
        a, b, (contract, ((), ())), precision=lax.Precision.HIGHEST, preferred_element_type=jnp.float32
    )


def start_all(copies):
    for copy in copies:
        copy.start()


def edges_kernel(
    sizes, scalars, field, row_x, row_y, right_y, right_x, send, f, ax, ay, ry, rx, kinds, sem
):
    gx, gy, gz = sizes
    px, py, pz = lax.axis_index("gx"), lax.axis_index("gy"), lax.axis_index("gz")
    depth = f.shape[0]
    planes = [pltpu.make_async_copy(field.at[z], f.at[z], sem.at[z]) for z in range(depth)]
    others = [
        pltpu.make_async_copy(row_x.at[px], ax, sem.at[depth]),
        pltpu.make_async_copy(row_y.at[py], ay, sem.at[depth + 1]),
        pltpu.make_async_copy(right_y.at[py], ry, sem.at[depth + 2]),
        pltpu.make_async_copy(right_x.at[px], rx, sem.at[depth + 3]),
    ]
    start_all(others[:2] + planes + others[2:])
    others[0].wait()
    others[1].wait()
    along_y, along_x = [], []
    for z in range(depth):
        planes[z].wait()
        along_y.append(dot(ax[0:8, :], f[z]))
        along_x.append(dot(ay[0:8, :], f[z], ((1,), (1,))))
    others[2].wait()
    others[3].wait()
    my, mx = ry.shape[1] // 4, rx.shape[1] // 2
    by_y = dot(jnp.concatenate(along_y, axis=0), ry[...])
    by_x = dot(jnp.concatenate(along_x, axis=0), rx[...])
    first_y, first_x = ay[8:9, :my], ax[8:9, :mx]
    kappa_x, kappa_y = scalars[gz, px], scalars[gz + 1, py]

    kinds[...] = jnp.zeros_like(kinds)
    mz = depth // 2
    for out in range(mz + 2):
        tile_y = sum(scalars[pz, out * depth + z] * by_y[8 * z : 8 * z + 8] for z in range(depth))
        tile_x = sum(scalars[pz, out * depth + z] * by_x[8 * z : 8 * z + 8] for z in range(depth))
        base = (mz + 2) * depth + out * mz
        first_row = sum(scalars[pz, base + j] * by_y[16 * j + 2 : 16 * j + 3, my : 2 * my] for j in range(mz))
        first_col = sum(scalars[pz, base + j] * by_x[16 * j + 2 : 16 * j + 3, mx:] for j in range(mz))
        corner = first_row[:, 0:1]
        lane = lax.broadcasted_iota(jnp.int32, (1, my), 1)
        chunks = {
            (1, 0): tile_y[0:1, :my] - kappa_x * (first_row - first_y * corner),
            (2, 0): tile_y[1:2, :my],
            (0, 1): tile_x[0:1, :mx] - kappa_y * (first_col - first_x * corner),
            (0, 2): tile_x[1:2, :mx],
            (1, 1): tile_y[0:1, 2 * my : 3 * my] - jnp.where(lane == 0, kappa_x * kappa_y * corner, 0.0),
            (1, 2): tile_y[0:1, 3 * my :],
            (2, 1): tile_y[1:2, 2 * my : 3 * my],
            (2, 2): tile_y[1:2, 3 * my :],
        }
        for (sx, sy), row in chunks.items():
            kind = (sx * 3 + sy) * 3
            if out < mz:
                kinds[kind, out : out + 1, :] = row
            else:
                kinds[kind + out - mz + 1, 0:1, :] = row
    for j in range(mz):
        row = by_y[16 * j + 2 : 16 * j + 3, my : 2 * my]
        col = by_x[16 * j + 2 : 16 * j + 3, mx:]
        for sx in range(3):
            for sy in range(3):
                for sz in range(3):
                    kinds[(sx * 3 + sy) * 3 + sz, mz + j : mz + j + 1, :] = col if sx == 0 else row

    def side(there, here):
        return jnp.where(there == here, 0, jnp.where(there > here, 1, 2))

    def scatter(tx, ty, tz, at):
        send[pl.ds(at, 1)] = kinds[pl.ds((side(tx, px) * 3 + side(ty, py)) * 3 + side(tz, pz), 1)]

    if gx * gy * gz <= 32:
        for at in range(gx * gy * gz):
            scatter(at // (gy * gz), (at // gz) % gy, at % gz, at)
    else:

        @pl.loop(0, gx * gy * gz)
        def _(at):
            scatter(at // (gy * gz), (at // gz) % gy, at % gz, at)


def bulk_kernel(sizes, hops, scalars, field, sx_all, sy_all, pick, row_x, row_y, own, even, *rest):
    gz = sizes[2]
    pays, (f, sx, sy, sel, ax, ay, picked, sem) = rest[: len(hops)], rest[len(hops) :]
    px, py, pz = lax.axis_index("gx"), lax.axis_index("gy"), lax.axis_index("gz")
    depth = f.shape[0]
    mz, mx, my = own.shape
    planes = [pltpu.make_async_copy(field.at[z], f.at[z], sem.at[z]) for z in range(depth)]
    others = [
        pltpu.make_async_copy(sx_all.at[px], sx, sem.at[depth]),
        pltpu.make_async_copy(sy_all.at[py], sy, sem.at[depth + 1]),
        pltpu.make_async_copy(pick, sel, sem.at[depth + 2]),
        pltpu.make_async_copy(row_x.at[px], ax, sem.at[depth + 3]),
        pltpu.make_async_copy(row_y.at[py], ay, sem.at[depth + 4]),
    ]
    start_all(others[:1] + planes + others[1:])
    others[0].wait()
    solved, evens = [], []
    for copy in others[1:]:
        copy.wait()
    for z in range(depth):
        planes[z].wait()
        solved.append(dot(dot(sx[...], f[z]), sy[...]))
        if z % 2 == 0:
            picked[z // 2] = dot(f[z], sel[...])
            evens.append(picked[z // 2, pl.ds(0, mx, stride=2), :])
    for j in range(mz):
        even[j] = evens[j]
    first_y = ay[8:9, :my]
    first_x = jnp.transpose(jnp.broadcast_to(ax[8:9, :mx], (8, mx)))[:, 0:1]
    outs = []
    for out in range(mz + 2):
        value = sum(scalars[pz, out * depth + z] * solved[z] for z in range(depth))
        base = (mz + 2) * depth + out * mz
        part = sum(scalars[pz, base + j] * evens[j] for j in range(mz))
        part = part - first_x * part[0:1, :]
        part = part - part[:, 0:1] * first_y
        outs.append(value - part)
    for j in range(mz):
        own[j] = evens[j] + outs[j]
    for pay, hop in zip(pays, hops, strict=True):
        right = (pz ^ hop) > pz
        pay[0] = jnp.where(right, outs[mz], outs[mz + 1])
        if pay.shape[0] > 1:
            pay[1] = evens[0]


def inner_kernel(hops, scalars, field, even, own, up_x, up_y, *rest):
    gets, (coefficients, coarse) = rest[: len(hops)], rest[len(hops) :]
    gz = lax.axis_size("gz")
    pz = lax.axis_index("gz")
    depth = field.shape[0]
    mz = even.shape[0]
    base = (mz + 2) * (depth + mz)
    ahead = jnp.zeros(even.shape[1:], jnp.float32)
    left, right = ahead, ahead
    for get, hop in zip(gets, hops, strict=True):
        q = pz ^ hop
        left = left + scalars[pz, base + q] * get[0]
        right = right + scalars[pz, base + gz + q] * get[0]
        if get.shape[0] > 1:
            ahead = ahead + jnp.where(q == pz + 1, 1.0, 0.0) * get[1]
    base = base + 2 * gz
    for j in range(mz):
        coarse[j] = own[j] + scalars[pz, base + j] * left + scalars[pz, base + mz + j] * right
    lifted = []
    for j in range(mz + 1):
        layer = even[j] if j < mz else ahead
        lifted.append(dot(dot(up_x[...], layer), up_y[...]))
    for j in range(mz):
        coefficients[2 * j] = field[2 * j] - lifted[j]
        coefficients[2 * j + 1] = field[2 * j + 1] - 0.5 * (lifted[j] + lifted[j + 1])


def finish_kernel(
    sizes, received, wx, wy, wz, row_x, row_y, up_y, up_x, inner, before, coefficients, coarse, w, ax, ay, c, sem
):
    px, py, pz = lax.axis_index("gx"), lax.axis_index("gy"), lax.axis_index("gz")
    mz, mx, my = coarse.shape
    depth = c.shape[0]
    copies = [
        pltpu.make_async_copy(wx.at[px], w.at[0], sem.at[0]),
        pltpu.make_async_copy(wy.at[py], w.at[1], sem.at[1]),
        pltpu.make_async_copy(wz.at[pz], w.at[2], sem.at[2]),
        pltpu.make_async_copy(row_x.at[px], ax, sem.at[3]),
        pltpu.make_async_copy(row_y.at[py], ay, sem.at[4]),
    ]
    fetch = pltpu.make_async_copy(inner, c, sem.at[5])
    start_all(copies + [fetch])
    for copy in copies:
        copy.wait()
    got = dot(w[0] * w[1] * w[2], received[...])
    ux, vx, uy, vy = ax[9:10, :mx], ax[10:11, :mx], ay[9:10, :my], ay[10:11, :my]

    def part(sx, sy, z):
        at = (sx * 3 + sy) * mz + z
        return got[at : at + 1]

    for z in range(mz):
        a, b = [], []
        for sy, end in ((1, uy), (2, vy)):
            a.append(part(0, sy, z) + ux * part(1, sy, z)[:, 0:1] + vx * part(2, sy, z)[:, 0:1])
            b.append(end)
        for sx, end in ((1, ux), (2, vx)):
            a.append(end)
            b.append(part(sx, 0, z))
        zero = jnp.zeros((4, mx), jnp.float32)
        coarse[z] = before[z] + dot(
            jnp.concatenate(a + [zero], axis=0), jnp.concatenate(b + [zero], axis=0), ((0,), (0,))
        )

    base = 9 * mz
    halo_x = got[base : base + mz + 1]
    halo_y = got[base + mz + 1 : base + 2 * (mz + 1)]
    halo_xy = got[base + 2 * (mz + 1) : base + 3 * (mz + 1)]
    lane = lax.broadcasted_iota(jnp.int32, (1, 2 * my), 1)
    last = jnp.where(lane == 2 * my - 1, 1.0, 0.0)
    pad = jnp.zeros((8 - mz - 1, halo_x.shape[1]), jnp.float32)
    row = dot(jnp.concatenate([halo_x, pad], axis=0), up_y[...])
    col = dot(jnp.concatenate([halo_y, pad], axis=0), up_x[...])
    fetch.wait()
    for z in range(depth):
        j = z // 2
        if z % 2 == 0:
            r, s, k = row[j : j + 1], col[j : j + 1], halo_xy[j : j + 1, 0:1]
        else:
            r = 0.5 * (row[j : j + 1] + row[j + 1 : j + 2])
            s = 0.5 * (col[j : j + 1] + col[j + 1 : j + 2])
            k = 0.5 * (halo_xy[j : j + 1, 0:1] + halo_xy[j + 1 : j + 2, 0:1])
        r = 0.5 * r + 0.25 * last * k
        s = jnp.concatenate([0.5 * s, jnp.zeros((7, 2 * mx), jnp.float32)], axis=0)
        e = jnp.concatenate([last, jnp.zeros((7, 2 * my), jnp.float32)], axis=0)
        c[z, :, my:] = c[z, :, my:] - dot(s, e[:, my:], ((0,), (0,)))
        c[z, 2 * mx - 1 : 2 * mx, :] = c[z, 2 * mx - 1 : 2 * mx, :] - r
    store = pltpu.make_async_copy(c, coefficients, sem.at[6])
    store.start()
    store.wait()


def params():
    return pltpu.CompilerParams(vmem_limit_bytes=VMEM_LIMIT)


ANY = pl.BlockSpec(memory_space=pl.ANY)
SMEM = pl.BlockSpec(memory_space=pltpu.SMEM)
VMEM = pl.BlockSpec(memory_space=pltpu.VMEM)


def on_device(sizes, field):
    gx, gy, gz = sizes
    depth, height, breadth = field.shape
    mz, mx, my = depth // 2, height // 2, breadth // 2
    count = gx * gy * gz
    axes = ("gx", "gy", "gz")
    tx, ty, tz = line_tables(gx, mx), line_tables(gy, my), line_tables(gz, mz)

    def rows(t, parts, m):
        table = np.zeros((parts, 16, 2 * m))
        table[:, 0], table[:, 1], table[:, 2, 0] = t["to_right"], t["to_left"], 1.0
        table[:, 8, :m], table[:, 9, :m], table[:, 10, :m] = t["first"], t["from_left"], t["from_right"]
        return f32(table)

    row_x, row_y = rows(tx, gx, mx), rows(ty, gy, my)
    right_y = np.zeros((gy, 2 * my, 4 * my))
    right_y[:, :, :my] = t_block = ty["block"].transpose(0, 2, 1)
    right_y[:, :, my : 2 * my] = even_selector(my)
    right_y[:, :, 2 * my], right_y[:, :, 3 * my] = ty["to_right"], ty["to_left"]
    right_x = np.zeros((gx, 2 * mx, 2 * mx))
    right_x[:, :, :mx] = tx["block"].transpose(0, 2, 1)
    right_x[:, :, mx:] = even_selector(mx)

    width = max((mz + 2) * (depth + mz) + 2 * gz + 2 * mz, gx, gy)
    scalars = np.zeros((gz + 2, width))
    for p in range(gz):
        full = np.concatenate([tz["block"][p], tz["to_right"][p : p + 1], tz["to_left"][p : p + 1]], axis=0)
        nodes = np.zeros((mz + 2, mz))
        nodes[:mz] = np.eye(mz)
        nodes[:mz, 0] -= tz["first"][p]
        nodes[mz, 0] = tz["first_right"][p]
        line = np.concatenate(
            [
                full.reshape(-1),
                nodes.reshape(-1),
                tz["weight_left"][p],
                tz["weight_right"][p],
                tz["from_left"][p],
                tz["from_right"][p],
            ]
        )
        scalars[p, : line.size] = line
    scalars[gz, :gx], scalars[gz + 1, :gy] = tx["first_right"], ty["first_right"]
    scalars = f32(scalars)

    vmem = pltpu.VMEM
    send = pl.pallas_call(
        functools.partial(edges_kernel, sizes),
        out_shape=jax.ShapeDtypeStruct((count, 4, my), jnp.float32),
        in_specs=[SMEM] + [ANY] * 5,
        out_specs=VMEM,
        scratch_shapes=[
            vmem(field.shape, jnp.float32),
            vmem((16, 2 * mx), jnp.float32),
            vmem((16, 2 * my), jnp.float32),
            vmem((2 * my, 4 * my), jnp.float32),
            vmem((2 * mx, 2 * mx), jnp.float32),
            vmem((27, 4, my), jnp.float32),
            pltpu.SemaphoreType.DMA((depth + 4,)),
        ],
        compiler_params=params(),
        name="edges",
    )(scalars, field, row_x, row_y, f32(right_y), f32(right_x))
    received = lax.all_to_all(send, axes, 0, 0, tiled=True).reshape(count * 4, my)

    hops = tuple(range(1, gz))
    plane = (mx, my)
    pay_shapes = [jax.ShapeDtypeStruct((2 if hop & (hop + 1) == 0 else 1, *plane), jnp.float32) for hop in hops]
    own, even, *pays = pl.pallas_call(
        functools.partial(bulk_kernel, sizes, hops),
        out_shape=[jax.ShapeDtypeStruct((mz, *plane), jnp.float32)] * 2 + pay_shapes,
        in_specs=[SMEM] + [ANY] * 6,
        out_specs=[VMEM] * (2 + len(hops)),
        scratch_shapes=[
            vmem(field.shape, jnp.float32),
            vmem((mx, 2 * mx), jnp.float32),
            vmem((2 * my, my), jnp.float32),
            vmem((2 * my, my), jnp.float32),
            vmem((16, 2 * mx), jnp.float32),
            vmem((16, 2 * my), jnp.float32),
            vmem((mz, 2 * mx, my), jnp.float32),
            pltpu.SemaphoreType.DMA((depth + 5,)),
        ],
        compiler_params=params(),
        name="bulk",
    )(scalars, field, f32(tx["block"]), f32(t_block), f32(even_selector(my)), row_x, row_y)
    gets = [lax.ppermute(pay, "gz", [(i, i ^ hop) for i in range(gz)]) for pay, hop in zip(pays, hops, strict=True)]

    up_x, up_y = lift_matrix(mx)[:, :mx], lift_matrix(my)[:, :my].T
    inner, before = pl.pallas_call(
        functools.partial(inner_kernel, hops),
        out_shape=[jax.ShapeDtypeStruct(field.shape, jnp.float32), jax.ShapeDtypeStruct(own.shape, jnp.float32)],
        in_specs=[SMEM] + [VMEM] * (5 + len(hops)),
        out_specs=[VMEM] * 2,
        compiler_params=params(),
        name="inner",
    )(scalars, field, even, own, f32(up_x), f32(up_y), *gets)

    wx, wy, wz = combine_tables(sizes, tx, ty, tz, mz)
    return pl.pallas_call(
        functools.partial(finish_kernel, sizes),
        out_shape=[jax.ShapeDtypeStruct(field.shape, jnp.float32), jax.ShapeDtypeStruct(own.shape, jnp.float32)],
        in_specs=[VMEM] + [ANY] * 5 + [VMEM, VMEM, ANY, VMEM],
        out_specs=[ANY, VMEM],
        scratch_shapes=[
            vmem((3, wx.shape[1], count * 4), jnp.float32),
            vmem((16, 2 * mx), jnp.float32),
            vmem((16, 2 * my), jnp.float32),
            vmem(field.shape, jnp.float32),
            pltpu.SemaphoreType.DMA((7,)),
        ],
        compiler_params=params(),
        name="finish",
    )(received, wx, wy, wz, row_x, row_y, f32(up_y), f32(up_x.T), inner, before)


def solution(mesh):
    sizes = tuple(mesh.shape[axis] for axis in ("gx", "gy", "gz"))
    return jax.shard_map(
        functools.partial(on_device, sizes),
        mesh=mesh,
        in_specs=(P("gz", "gx", "gy"),),
        out_specs=(P("gz", "gx", "gy"), P("gz", "gx", "gy")),
        check_vma=False,
    )
```

time: 532 us -> 37.5 us (0.07); the launches traced: 522 us -> 37.1 us
  other arithmetic: 244 us -> 0 us
  local copies, waits for them, and re-layouts: 198 us -> 8.03 us
  starting transfers between devices: 41 us -> 9.9 us
  waiting for transfers between devices: 23.7 us -> 3.46 us
  Pallas kernels: 0 us -> 14.9 us
  between operations: 12.5 us -> 0.75 us
    slice x56 -> x0, local copies, waits for them, and re-layouts: 93.2 us -> none  [the longest x2 21.3 us: restrict_rim(): right_side = lax.slice_in_dim(weighted, 2, count_all, stride=2, axis=along)]
    sub x266 -> x0, other arithmetic: 91.9 us -> none  [the longest x265 90.8 us: solve_lines(): lax.linalg.tridiagonal_solve(below_diag, middle, above_diag, rotated)]
    while x990 -> x0, other arithmetic: 82 us -> none
    broadcast_in_dim x831 -> x0, local copies, waits for them, and re-layouts: 76.5 us -> none  [the longest x829 76.5 us: solve_lines(): lax.linalg.tridiagonal_solve(below_diag, middle, above_diag, rotated)]
    div x48 -> x0, other arithmetic: 26.3 us -> none  [solve_lines(): lax.linalg.tridiagonal_solve(below_diag, middle, above_diag, rotated)]
    unnamed x49 -> x0, other arithmetic: 25.6 us -> none
    all_to_all x6 -> x1, starting transfers between devices: 26.2 us -> 4.9 us  [on_device(): lax.all_to_all(send, axes, 0, 0, tiled=True).reshape(count * 4, my)]
    all_to_all x6 -> x1, waiting for transfers between devices: 17.8 us -> 0.76 us  [on_device(): lax.all_to_all(send, axes, 0, 0, tiled=True).reshape(count * 4, my)]
  transfers between devices with their start and end apart: 12 -> 4, of which waited for: 7 -> 2; matrix products, arithmetic and copies ran while one was open for 4% -> 0% of each run, Pallas kernels for 0% -> 18%
where the time goes in v1:
time: 37.5 us; the launch traced here: 37.1 us
  Pallas kernels  14.9 us (40%)
  starting transfers between devices  9.9 us (26%)
  local copies, waits for them, and re-layouts  8.03 us (21%)
  waiting for transfers between devices  3.46 us (9%)
  between operations  0.75 us (2%)
    unnamed x36, local copies, waits for them, and re-layouts  8.03 us
    ppermute x3, starting transfers between devices, on_device(): lax.ppermute(pay, 'gz', [(i, i ^ hop) for i in range(gz)])  4.99 us
    all_to_all x1, starting transfers between devices, on_device(): lax.all_to_all(send, axes, 0, 0, tiled=True).reshape(count * 4, my)  4.9 us
    pallas_call x1, Pallas kernels, on_device(): pl.pallas_call(functools.partial(edges_kernel, sizes), out_shape=jax.Shap...  4.8 us
    pallas_call x1, Pallas kernels, on_device(): pl.pallas_call(functools.partial(bulk_kernel, sizes, hops), out_shape=[ja...  4.63 us
    pallas_call x1, Pallas kernels, on_device(): pl.pallas_call(functools.partial(finish_kernel, sizes), out_shape=[jax.Sh...  3.42 us
    ppermute x3, waiting for transfers between devices, on_device(): lax.ppermute(pay, 'gz', [(i, i ^ hop) for i in range(gz)])  2.7 us
    pallas_call x1, Pallas kernels, on_device(): pl.pallas_call(functools.partial(inner_kernel, hops), out_shape=[jax.Shap...  2.06 us
  transfers between devices with their start and end apart: 4, of which 2 were waited for; matrix products, arithmetic and copies ran while one was open for 0% of the time, Pallas kernels for 18%

profile of v1, /device:TPU:0, one launch (start us, length us, event | category | flops | bytes accessed | tf_op | source)
XLA Modules:
  0.0 37.1 jit_solution(16252907191433983533)
XLA Ops:
  0.6 0.0 copy-start
  0.6 1.2 %copy-done = f32[4,256,256]{2,1,0:T(8,128)S(1)} copy-done((f32[4,256,256]{2,1,0:T(8,128)S(1)}, f32[4,256,256]{2,1,0:T(8,128)}, u32[]{:S(2)}) %copy-start) | copy-done | bytes 1048600
  1.9 0.8 %copy-done.4 = f32[4,16,256]{2,1,0:T(8,128)S(1)} copy-done((f32[4,16,256]{2,1,0:T(8,128)S(1)}, f32[4,16,256]{2,1,0:T(8,128)}, u32[]{:S(2)}) %copy-start.4) | copy-done | bytes 65560
  2.7 1.0 %copy-done.7 = f32[4,256,128]{2,1,0:T(8,128)S(1)} copy-done((f32[4,256,128]{2,1,0:T(8,128)S(1)}, f32[4,256,128]{2,1,0:T(8,128)}, u32[]{:S(2)}) %copy-start.7) | copy-done | bytes 524312
  3.7 0.8 %copy-done.8 = f32[2,16,256]{2,1,0:T(8,128)S(1)} copy-done((f32[2,16,256]{2,1,0:T(8,128)S(1)}, f32[2,16,256]{2,1,0:T(8,128)}, u32[]{:S(2)}) %copy-start.8) | copy-done | bytes 32792
  4.5 0.9 %copy-done.10 = f32[2,128,256]{2,1,0:T(8,128)S(1)} copy-done((f32[2,128,256]{2,1,0:T(8,128)S(1)}, f32[2,128,256]{2,1,0:T(8,128)}, u32[]{:S(2)}) %copy-start.10) | copy-done | bytes 262168
  5.5 0.9 %copy-done.11 = f32[256,128]{1,0:T(8,128)S(1)} copy-done((f32[256,128]{1,0:T(8,128)S(1)}, f32[256,128]{1,0:T(8,128)}, u32[]{:S(2)}) %copy-start.11) | copy-done | bytes 131096
  6.4 0.7 %copy-done.15 = f32[6,36]{1,0:T(8,128)S(1)} copy-done((f32[6,36]{1,0:T(8,128)S(1)}, f32[6,36]{1,0:T(8,128)}, u32[]{:S(2)}) %copy-start.15) | copy-done | bytes 888
  7.1 4.6 %bulk.1 = (f32[2,128,128]{2,1,0:T(8,128)S(1)}, f32[2,128,128]{2,1,0:T(8,128)S(1)}, f32[2,128,128]{2,1,0:T(8,128)S(1)}, f32[1,128,128]{2,1,0:T(8,128)S(1)}, f32[2,128,128]{2,1,0:T(8,128)S(1)}) custom-call(f32[6,36]{1,0:T(8,128)S(1)} %copy-done.15, f32[4,256,256]{2,1,0:T(8,128)S(1)} %copy-done, f32[2,128,256]{2,1,0:T(8,128)S(1)} %copy-done.10, ...), custom_call_target="tpu_custom_call" | custom-call | tf_op jit(solution)/shard_map/bulk/pallas_call | solution.py:447
  11.7 0.0 copy-start.1
  11.7 0.5 %collective-permute-start = (f32[2,128,128]{2,1,0:T(8,128)S(1)}, f32[2,128,128]{2,1,0:T(8,128)S(1)}, u32[]{:S(2)}, u32[]{:S(2)}) collective-permute-start(f32[2,128,128]{2,1,0:T(8,128)S(1)} %get-tuple-element.11), channel_id=1, source_target_pairs={{0,1},{1,0},{2,3},{3,2},{4,5},{5,4},{6,7},{7,6},{8,9},{9,8},{10,11... | collective-permute-start | bytes 393224 | tf_op jit(solution)/shard_map/ppermute | solution.py:465
  12.2 2.6 %collective-permute-start.2 = (f32[2,128,128]{2,1,0:T(8,128)S(1)}, f32[2,128,128]{2,1,0:T(8,128)S(1)}, u32[]{:S(2)}, u32[]{:S(2)}) collective-permute-start(f32[2,128,128]{2,1,0:T(8,128)S(1)} %get-tuple-element.13), channel_id=1, source_target_pairs={{0,3},{1,2},{2,1},{3,0},{4,7},{5,6},{6,5},{7,4},{8,11},{9,10},{10,... | collective-permute-start | bytes 393224 | tf_op jit(solution)/shard_map/ppermute | solution.py:465
  14.9 0.0 copy-done.6
  14.9 1.6 %copy-done.2 = f32[4,256,512]{2,1,0:T(8,128)S(1)} copy-done((f32[4,256,512]{2,1,0:T(8,128)S(1)}, f32[4,256,512]{2,1,0:T(8,128)}, u32[]{:S(2)}) %copy-start.2) | copy-done | bytes 2097176
  16.5 0.0 copy-start.17
  16.5 4.8 %edges.1 = f32[32,4,128]{2,1,0:T(4,128)} custom-call(f32[6,36]{1,0:T(8,128)S(1)} %copy-done.15, f32[4,256,256]{2,1,0:T(8,128)S(1)} %copy-done, f32[2,16,256]{2,1,0:T(8,128)S(1)} %copy-done.8, f32[4,16,256]{2,1,0:T(8,128)S(1)} %copy-done.4, f32[4,256,512]{2,1,0:T(8,128)S(1)} %copy-done.2, f32[2,256,256]{2,1,0:T(8,128)S(1)} %copy-done.6), custom_call_target="tpu_custom_call" | custom-call | tf_op jit(solution)/shard_map/edges/pallas_call | solution.py:425
  21.3 4.9 %all-to-all-start = ((f32[32,4,128]{2,1,0:T(4,128)}), f32[32,4,128]{2,1,0:T(4,128)S(1)}, u32[]{:S(2)}, u32[]{:S(2)}) async-start(f32[32,4,128]{2,1,0:T(4,128)} %edges.1), calls=%async_computation | async-start | bytes 131072 | tf_op jit(solution)/shard_map/all_to_all | solution.py:442
  26.2 1.8 %collective-permute-start.1 = (f32[1,128,128]{2,1,0:T(8,128)S(1)}, f32[1,128,128]{2,1,0:T(8,128)S(1)}, u32[]{:S(2)}, u32[]{:S(2)}) collective-permute-start(f32[1,128,128]{2,1,0:T(8,128)S(1)} %get-tuple-element.12), channel_id=1, source_target_pairs={{0,2},{1,3},{2,0},{3,1},{4,6},{5,7},{6,4},{7,5},{8,10},{9,11},{10,... | collective-permute-start | bytes 196616 | tf_op jit(solution)/shard_map/ppermute | solution.py:465
  28.0 2.7 %collective-permute-done.1.rest_1_ = f32[1,128,128]{2,1,0:T(8,128)S(1)} collective-permute-done((f32[1,128,128]{2,1,0:T(8,128)S(1)}, f32[1,128,128]{2,1,0:T(8,128)S(1)}, u32[]{:S(2)}, u32[]{:S(2)}) %collective-permute-start.1) | collective-permute-done | bytes 65568 | tf_op jit(solution)/shard_map/ppermute | solution.py:465
  30.7 0.0 collective-permute-done.rest_0_
  30.7 0.0 collective-permute-done.2.rest_2_
  30.7 0.0 copy-done.3
  30.7 0.0 copy-done.12
  30.8 0.0 copy-done.16
  30.8 0.0 copy-done.1
  30.8 2.1 %inner.1 = (f32[4,256,256]{2,1,0:T(8,128)S(1)}, f32[2,128,128]{2,1,0:T(8,128)S(1)}) custom-call(f32[6,36]{1,0:T(8,128)S(1)} %copy-done.16, f32[4,256,256]{2,1,0:T(8,128)S(1)} %copy-done.1, f32[2,128,128]{2,1,0:T(8,128)S(1)} %get-tuple-element.9.even, f32[2,128,128]{2,1,0:T(8,128)S(1)} %get-tuple-element.10.own, f32[256,128]{1,0:T(8,128)S(1)} %copy-done.12, ...), custom_call_target="tpu_custom_call" | custom-call | tf_op jit(solution)/shard_map/inner/pallas_call | solution.py:468
  32.8 0.8 %all-to-all-done = f32[32,4,128]{2,1,0:T(4,128)S(1)} async-done(((f32[32,4,128]{2,1,0:T(4,128)}), f32[32,4,128]{2,1,0:T(4,128)S(1)}, u32[]{:S(2)}, u32[]{:S(2)}) %all-to-all-start) | async-done | bytes 65568 | tf_op jit(solution)/shard_map/all_to_all | solution.py:442
  33.6 0.0 copy-done.5
  33.6 0.0 copy-done.9
  33.6 0.0 copy-done.13
  33.6 0.0 copy-done.14
  33.6 3.4 %finish.1 = (f32[4,256,256]{2,1,0:T(8,128)}, f32[2,128,128]{2,1,0:T(8,128)}) custom-call(f32[128,128]{1,0:T(8,128)S(1)} %bitcast.1, f32[2,32,128]{2,1,0:T(8,128)S(1)} %copy-done.17, f32[4,32,128]{2,1,0:T(8,128)S(1)} %copy-done.14, f32[4,32,128]{2,1,0:T(8,128)S(1)} %copy-done.13, f32[2,16,256]{2,1,0:T(8,128)S(1)} %copy-done.9, f32[4,16,256]{2,1,0:T(8,128)S(1)} %copy-done.5, ...), custom_call_target="tpu_custom_call" | custom-call | tf_op jit(solution)/shard_map/finish/pallas_call | solution.py:478
  (16 shorter events, 0.0 us)
Async XLA Ops:
  0.6 1.2 %copy-start = (f32[4,256,256]{2,1,0:T(8,128)S(1)}, f32[4,256,256]{2,1,0:T(8,128)}, u32[]{:S(2)}) copy-start(f32[4,256,256]{2,1,0:T(8,128)} %field.5) | copy-start | bytes 3145732
  1.9 0.8 %copy-start.4 = (f32[4,16,256]{2,1,0:T(8,128)S(1)}, f32[4,16,256]{2,1,0:T(8,128)}, u32[]{:S(2)}) copy-start(f32[4,16,256]{2,1,0:T(8,128)} %constant.28.clone.row_y) | copy-start | bytes 196612
  2.7 1.0 %copy-start.7 = (f32[4,256,128]{2,1,0:T(8,128)S(1)}, f32[4,256,128]{2,1,0:T(8,128)}, u32[]{:S(2)}) copy-start(f32[4,256,128]{2,1,0:T(8,128)} %constant.32.clone.sy_all) | copy-start | bytes 1572868
  3.7 0.8 %copy-start.8 = (f32[2,16,256]{2,1,0:T(8,128)S(1)}, f32[2,16,256]{2,1,0:T(8,128)}, u32[]{:S(2)}) copy-start(f32[2,16,256]{2,1,0:T(8,128)} %constant.27.clone.row_x) | copy-start | bytes 98308
  4.5 0.9 %copy-start.10 = (f32[2,128,256]{2,1,0:T(8,128)S(1)}, f32[2,128,256]{2,1,0:T(8,128)}, u32[]{:S(2)}) copy-start(f32[2,128,256]{2,1,0:T(8,128)} %constant.31.clone.sx_all) | copy-start | bytes 786436
  5.4 0.9 %copy-start.11 = (f32[256,128]{1,0:T(8,128)S(1)}, f32[256,128]{1,0:T(8,128)}, u32[]{:S(2)}) copy-start(f32[256,128]{1,0:T(8,128)} %constant.33.clone.pick) | copy-start | bytes 393220
  6.4 0.7 %copy-start.15 = (f32[6,36]{1,0:T(8,128)S(1)}, f32[6,36]{1,0:T(8,128)}, u32[]{:S(2)}) copy-start(f32[6,36]{1,0:T(8,128)} %constant.26.clone.scalars) | copy-start | bytes 2596
  7.0 7.8 %copy-start.6 = (f32[2,256,256]{2,1,0:T(8,128)S(1)}, f32[2,256,256]{2,1,0:T(8,128)}, u32[]{:S(2)}) copy-start(f32[2,256,256]{2,1,0:T(8,128)} %constant.30.clone.right_x) | copy-start | bytes 1572868
  7.0 23.7 %copy-start.3 = (f32[128,256]{1,0:T(8,128)S(1)}, f32[128,256]{1,0:T(8,128)}, u32[]{:S(2)}) copy-start(f32[128,256]{1,0:T(8,128)} %constant.35.clone.up_y.up_x) | copy-start | bytes 393220
  7.0 23.7 %copy-start.12 = (f32[256,128]{1,0:T(8,128)S(1)}, f32[256,128]{1,0:T(8,128)}, u32[]{:S(2)}) copy-start(f32[256,128]{1,0:T(8,128)} %constant.34.clone.up_x) | copy-start | bytes 393220
  7.0 23.7 %copy-start.16 = (f32[6,36]{1,0:T(8,128)S(1)}, f32[6,36]{1,0:T(8,128)}, u32[]{:S(2)}) copy-start(f32[6,36]{1,0:T(8,128)} %constant.26.clone.scalars) | copy-start | bytes 2596
  11.7 19.1 %copy-start.1 = (f32[4,256,256]{2,1,0:T(8,128)S(1)}, f32[4,256,256]{2,1,0:T(8,128)}, u32[]{:S(2)}) copy-start(f32[4,256,256]{2,1,0:T(8,128)} %field.5) | copy-start | bytes 3145732
  11.7 19.0 %collective-permute-start = (f32[2,128,128]{2,1,0:T(8,128)S(1)}, f32[2,128,128]{2,1,0:T(8,128)S(1)}, u32[]{:S(2)}, u32[]{:S(2)}) collective-permute-start(f32[2,128,128]{2,1,0:T(8,128)S(1)} %get-tuple-element.11), channel_id=1, source_target_pairs={{0,1},{1,0},{2,3},{3,2},{4,5},{5,4},{6,7},{7,6},{8,9},{9,8},{10,11... | collective-permute-start | bytes 393224 | tf_op jit(solution)/shard_map/ppermute | solution.py:465
  12.2 18.5 %collective-permute-start.2 = (f32[2,128,128]{2,1,0:T(8,128)S(1)}, f32[2,128,128]{2,1,0:T(8,128)S(1)}, u32[]{:S(2)}, u32[]{:S(2)}) collective-permute-start(f32[2,128,128]{2,1,0:T(8,128)S(1)} %get-tuple-element.13), channel_id=1, source_target_pairs={{0,3},{1,2},{2,1},{3,0},{4,7},{5,6},{6,5},{7,4},{8,11},{9,10},{10,... | collective-permute-start | bytes 393224 | tf_op jit(solution)/shard_map/ppermute | solution.py:465
  14.9 1.6 %copy-start.2 = (f32[4,256,512]{2,1,0:T(8,128)S(1)}, f32[4,256,512]{2,1,0:T(8,128)}, u32[]{:S(2)}) copy-start(f32[4,256,512]{2,1,0:T(8,128)} %constant.29.clone.right_y) | copy-start | bytes 6291460
  16.5 17.1 %copy-start.5 = (f32[4,16,256]{2,1,0:T(8,128)S(1)}, f32[4,16,256]{2,1,0:T(8,128)}, u32[]{:S(2)}) copy-start(f32[4,16,256]{2,1,0:T(8,128)} %constant.28.clone.row_y) | copy-start | bytes 196612
  16.5 17.2 %copy-start.9 = (f32[2,16,256]{2,1,0:T(8,128)S(1)}, f32[2,16,256]{2,1,0:T(8,128)}, u32[]{:S(2)}) copy-start(f32[2,16,256]{2,1,0:T(8,128)} %constant.27.clone.row_x) | copy-start | bytes 98308
  16.5 17.2 %copy-start.13 = (f32[4,32,128]{2,1,0:T(8,128)S(1)}, f32[4,32,128]{2,1,0:T(8,128)}, u32[]{:S(2)}) copy-start(f32[4,32,128]{2,1,0:T(8,128)} %constant.38.clone.wz) | copy-start | bytes 196612
  16.5 17.2 %copy-start.14 = (f32[4,32,128]{2,1,0:T(8,128)S(1)}, f32[4,32,128]{2,1,0:T(8,128)}, u32[]{:S(2)}) copy-start(f32[4,32,128]{2,1,0:T(8,128)} %constant.37.clone.wy) | copy-start | bytes 196612
  16.5 17.2 %copy-start.17 = (f32[2,32,128]{2,1,0:T(8,128)S(1)}, f32[2,32,128]{2,1,0:T(8,128)}, u32[]{:S(2)}) copy-start(f32[2,32,128]{2,1,0:T(8,128)} %constant.36.clone.wx) | copy-start | bytes 98308
  21.3 12.3 %all-to-all-start = ((f32[32,4,128]{2,1,0:T(4,128)}), f32[32,4,128]{2,1,0:T(4,128)S(1)}, u32[]{:S(2)}, u32[]{:S(2)}) async-start(f32[32,4,128]{2,1,0:T(4,128)} %edges.1), calls=%async_computation | async-start | bytes 131072 | tf_op jit(solution)/shard_map/all_to_all | solution.py:442
  26.2 4.5 %collective-permute-start.1 = (f32[1,128,128]{2,1,0:T(8,128)S(1)}, f32[1,128,128]{2,1,0:T(8,128)S(1)}, u32[]{:S(2)}, u32[]{:S(2)}) collective-permute-start(f32[1,128,128]{2,1,0:T(8,128)S(1)} %get-tuple-element.12), channel_id=1, source_target_pairs={{0,2},{1,3},{2,0},{3,1},{4,6},{5,7},{6,4},{7,5},{8,10},{9,11},{10,... | collective-permute-start | bytes 196616 | tf_op jit(solution)/shard_map/ppermute | solution.py:465

commit v2 on v1

v2 whole, which is shorter than its diff:
```python
import functools

import jax
import jax.numpy as jnp
import numpy as np
from jax import lax
from jax.experimental import pallas as pl
from jax.experimental.pallas import tpu as pltpu
from jax.sharding import PartitionSpec as P

RATIO = 2.0 - np.sqrt(3.0)
VMEM_LIMIT = 48 * 1024 * 1024


def inverse_mass(i, j, n):
    low, high = np.minimum(i, j), np.maximum(i, j)
    sign = np.where((high - low) % 2 == 0, 1.0, -1.0)
    value = RATIO ** (high - low + 1.0) * (1.0 - RATIO ** (2.0 * (low + 1))) * (1.0 - RATIO ** (2.0 * (n - high)))
    return 3.0 * sign * value / ((1.0 - RATIO**2) * (1.0 - RATIO ** (2.0 * (n + 1))))


def line_operator(i, k, n):
    a = k // 2
    odd = k % 2 == 1

    def at(j):
        inside = (j >= 0) & (j < n)
        return np.where(inside, inverse_mass(i, np.clip(j, 0, n - 1), n), 0.0)

    even_part = np.where(a == 0, 9.0, 10.0) * at(a) + at(a - 1) + at(a + 1)
    odd_part = 6.0 * at(a) + 6.0 * at(a + 1)
    return np.where(odd, odd_part, even_part) / 12.0


def line_tables(parts, m):
    n = parts * m
    node, fine = np.arange(m), np.arange(2 * m)
    block = np.zeros((parts, m, 2 * m))
    to_right, to_left = np.zeros((parts, 2 * m)), np.zeros((parts, 2 * m))
    from_left, from_right = np.zeros((parts, m)), np.zeros((parts, m))
    weight_left, weight_right = np.zeros((parts, parts)), np.zeros((parts, parts))
    first = np.zeros((parts, m))
    first_right = np.zeros((parts,))
    for p in range(parts):
        k = p * 2 * m + fine
        block[p] = line_operator((p * m + node)[:, None], k[None, :], n)
        if p + 1 < parts:
            to_right[p] = line_operator(np.full_like(k, (p + 1) * m), k, n)
        if p > 0:
            to_left[p] = line_operator(np.full_like(k, p * m - 1), k, n)
        from_left[p] = (-RATIO) ** node * (1 - RATIO ** (2.0 * (n - p * m - node))) / (1 - RATIO ** (2.0 * (n - p * m)))
        from_right[p] = (
            (-RATIO) ** (m - 1 - node) * (1 - RATIO ** (2.0 * (p * m + node + 1))) / (1 - RATIO ** (2.0 * (p + 1) * m))
        )
        for q in range(parts):
            if q < p:
                weight_left[p, q] = (
                    (-RATIO) ** ((p - q - 1) * m)
                    * (1 - RATIO ** (2.0 * (n - p * m)))
                    / (1 - RATIO ** (2.0 * (n - (q + 1) * m)))
                )
            if q > p:
                weight_right[p, q] = (
                    (-RATIO) ** ((q - p - 1) * m) * (1 - RATIO ** (2.0 * (p + 1) * m)) / (1 - RATIO ** (2.0 * q * m))
                )
    first[0] = inverse_mass(node, np.zeros_like(node), n) / 3.0
    if parts > 1:
        first_right[0] = -inverse_mass(np.array(m), np.array(0), n) / 3.0
    return {
        "block": block,
        "to_right": to_right,
        "to_left": to_left,
        "from_left": from_left,
        "from_right": from_right,
        "weight_left": weight_left,
        "weight_right": weight_right,
        "first": first,
        "first_right": first_right,
    }


def even_selector(m):
    pick = np.zeros((2 * m, m))
    pick[2 * np.arange(m), np.arange(m)] = 1.0
    return pick


def lift_matrix(m):
    up = np.zeros((2 * m, m + 1))
    up[2 * np.arange(m), np.arange(m)] = 1.0
    up[2 * np.arange(m) + 1, np.arange(m)] = 0.5
    up[2 * np.arange(m) + 1, np.arange(m) + 1] = 0.5
    return up


def f32(values):
    return np.asarray(values, np.float32)


def combine_tables(sizes, tx, ty, tz, mz):
    gx, gy, gz = sizes
    count = gx * gy * gz
    sender = np.arange(count)
    qx, qy, qz = sender // (gy * gz), (sender // gz) % gy, sender % gz
    rows = 32
    wx, wy, wz = (np.zeros((parts, rows, count, 4)) for parts in sizes)

    def side(t, p, q, which):
        if which == 0:
            return (q == p) * 1.0
        return (t["weight_left"] if which == 1 else t["weight_right"])[p][q]

    for sx in range(3):
        for sy in range(3):
            if sx == 0 and sy == 0:
                continue
            for z in range(mz):
                row = (sx * 3 + sy) * mz + z
                for p in range(gx):
                    wx[p, row] = side(tx, p, qx, sx)[:, None]
                for p in range(gy):
                    wy[p, row] = side(ty, p, qy, sy)[:, None]
                for p in range(gz):
                    wz[p, row, :, z] += qz == p
                    wz[p, row, :, 0] += tz["weight_left"][p][qz] * tz["from_left"][p, z]
                    wz[p, row, :, 0] += tz["weight_right"][p][qz] * tz["from_right"][p, z]
    for case, (ox, oy) in enumerate(((1, 0), (0, 1), (1, 1))):
        for layer in range(mz + 1):
            row = 9 * mz + case * (mz + 1) + layer
            for p in range(gx):
                wx[p, row] = (qx == p + ox)[:, None]
            for p in range(gy):
                wy[p, row] = (qy == p + oy)[:, None]
            for p in range(gz):
                if layer < mz:
                    wz[p, row, :, mz + layer] = qz == p
                else:
                    wz[p, row, :, mz] = qz == p + 1
    return tuple(f32(w.reshape(w.shape[0], rows, count * 4)) for w in (wx, wy, wz))


def split(values):
    high = values.astype(jnp.bfloat16)
    return high, (values - high.astype(jnp.float32)).astype(jnp.bfloat16)


def one_pass(a, b, contract=((1,), (0,))):
    return lax.dot_general(a, b, (contract, ((), ())), preferred_element_type=jnp.float32)


def three_pass(a, b, contract=((1,), (0,))):
    return one_pass(a[0], b[0], contract) + one_pass(a[0], b[1], contract) + one_pass(a[1], b[0], contract)


def exact_left(a, b):
    high, low = split(b)
    return one_pass(a, high) + one_pass(a, low)


def split_exact(values):
    return values.astype(jnp.bfloat16)


def exact_right(a, b):
    high, low = split(a)
    return one_pass(high, b) + one_pass(low, b)


def start_all(copies):
    for copy in copies:
        copy.start()


def local_kernel(sizes, *refs):
    numbers, field, sum_x, sum_y, fold_z, row_y, row_x, line_y, line_x, block_x, pick = refs[:11]
    send, own, even, near, far, first = refs[11:17]
    f, ax, ay, az, vy, vx, ry, rx, bx, sel, kinds, scalars, sem = refs[17:]
    gx, gy, gz = sizes
    px, py, pz = lax.axis_index("gx"), lax.axis_index("gy"), lax.axis_index("gz")
    depth, height, _ = field.shape
    mz, mx, my = own.shape
    planes = []
    for z in range(depth):
        halves = [
            pltpu.make_async_copy(field.at[z, :, pl.ds(h * my, my)], f.at[h, z], sem.at[2 * z + h]) for h in range(2)
        ]
        planes.append(halves)
    sources = [(line_y.at[py], ry), (sum_y.at[py], ay), (fold_z.at[pz], az), (sum_x.at[px], ax), (numbers, scalars)]
    sources += [(row_y.at[py], vy), (row_x.at[px], vx), (block_x.at[px], bx), (pick, sel), (line_x.at[px], rx)]
    tables = [pltpu.make_async_copy(src, dst, sem.at[2 * depth + i]) for i, (src, dst) in enumerate(sources)]
    start_all(tables[:3] + planes[0] + planes[1] + tables[3:] + planes[2] + planes[3])
    for table in tables[:3]:
        table.wait()
    kinds[...] = jnp.zeros_like(kinds)
    solve_y = split(ry[...])
    by_y, along_x = [], None
    for z in range(depth):
        sum_z = split(ay[...] * az[z : z + 1, :])
        weights = tuple(jnp.concatenate([a, b], axis=1) for a, b in zip(solve_y, sum_z, strict=True))
        for half in planes[z]:
            half.wait()
        both = three_pass(split(jnp.concatenate([f[0, z], f[1, z]], axis=1)), weights)
        by_y.append(both[:, :my])
        along_x = both[:, my:] if along_x is None else along_x + both[:, my:]
    for table in tables[3:]:
        table.wait()

    by_x = three_pass(split(jnp.transpose(along_x)[:16, :]), split(rx[...]))
    sums = [[jnp.sum(by_y[z] * ax[ab], axis=0, keepdims=True) for ab in range(2)] for z in range(depth)]
    corners = [jnp.sum(along_x * ax[ab], axis=0, keepdims=True) for ab in range(2)]
    pick_y = split_exact(sel[...])
    evens = []
    for j in range(mz):
        rows = jnp.concatenate([f[h, 2 * j, pl.ds(0, mx, stride=2), :] for h in range(2)], axis=1)
        evens.append(exact_right(rows, pick_y))
        even[j] = evens[j]
    first_y, first_x = vy[8:9, :my], vx[8:9, :mx]
    kappa_x, kappa_y = scalars[gz, px], scalars[gz + 1, py]
    ends = 2 * (mz + 2)
    first_rows = [evens[j][0:1, :] for j in range(mz)]
    first_cols = [by_x[ends + j : ends + j + 1, mx:] for j in range(mz)]
    for out in range(mz + 2):
        base = (mz + 2) * depth + out * mz
        first_row = sum(scalars[pz, base + j] * first_rows[j] for j in range(mz))
        first_col = sum(scalars[pz, base + j] * first_cols[j] for j in range(mz))
        corner = first_row[:, 0:1]
        right_row, left_row = (sum(scalars[pz, out * depth + z] * sums[z][ab] for z in range(depth)) for ab in range(2))
        r, l = slice(2 * out, 2 * out + 1), slice(2 * out + 1, 2 * out + 2)
        spread = jnp.zeros((1, my), jnp.float32)
        chunks = {
            (1, 0): right_row - kappa_x * (first_row - first_y * corner),
            (2, 0): left_row,
            (0, 1): by_x[r, :mx] - kappa_y * (first_col - first_x * corner),
            (0, 2): by_x[l, :mx],
            (1, 1): spread + (corners[0][:, r] - kappa_x * kappa_y * corner),
            (1, 2): spread + corners[0][:, l],
            (2, 1): spread + corners[1][:, r],
            (2, 2): spread + corners[1][:, l],
        }
        for (sx, sy), row in chunks.items():
            kind = (sx * 3 + sy) * 3
            if out < mz:
                kinds[kind, out : out + 1, :] = row
            else:
                kinds[kind + out - mz + 1, 0:1, :] = row
    for sx in range(3):
        for sy in range(3):
            halo = jnp.concatenate(first_cols if sx == 0 else first_rows, axis=0)
            for sz in range(3):
                kinds[(sx * 3 + sy) * 3 + sz, mz : 2 * mz, :] = halo

    def side(there, here):
        return jnp.where(there == here, 0, jnp.where(there > here, 1, 2))

    def scatter(tx, ty, tz, at):
        send[pl.ds(at, 1)] = kinds[pl.ds((side(tx, px) * 3 + side(ty, py)) * 3 + side(tz, pz), 1)]

    if gx * gy * gz <= 32:
        for at in range(gx * gy * gz):
            scatter(at // (gy * gz), (at // gz) % gy, at % gz, at)
    else:

        @pl.loop(0, gx * gy * gz)
        def _(at):
            scatter(at // (gy * gz), (at // gz) % gy, at % gz, at)

    solve_x = split(bx[...])
    solved = [three_pass(solve_x, split(by_y[z])) for z in range(depth)]
    first_x = jnp.transpose(jnp.broadcast_to(first_x, (8, mx)))[:, 0:1]
    outs = []
    for out in range(mz + 2):
        value = sum(scalars[pz, out * depth + z] * solved[z] for z in range(depth))
        base = (mz + 2) * depth + out * mz
        part = sum(scalars[pz, base + j] * evens[j] for j in range(mz))
        part = part - first_x * part[0:1, :]
        part = part - part[:, 0:1] * first_y
        outs.append(value - part)
    for j in range(mz):
        own[j] = evens[j] + outs[j]
    near[...] = jnp.where(pz % 2 == 0, outs[mz], outs[mz + 1])
    far[...] = jnp.where(pz % 4 < 2, outs[mz], outs[mz + 1])
    first[...] = evens[0]


def inner_kernel(field, even, up_x, up_y, c, top):
    depth = field.shape[0]
    mz = even.shape[0]
    up_x, up_y = up_x[...].astype(jnp.bfloat16), up_y[...].astype(jnp.bfloat16)
    lifted = [exact_right(exact_left(up_x, even[j]), up_y) for j in range(mz)]
    for z in range(depth - 1):
        j = z // 2
        c[z] = field[z] - (lifted[j] if z % 2 == 0 else 0.5 * (lifted[j] + lifted[j + 1]))
    top[...] = field[depth - 1] - 0.5 * lifted[mz - 1]


def upper_kernel(scalars, top, own, up_x, up_y, one, two, three, first_one, first_three, last, coarse):
    gz = lax.axis_size("gz")
    pz = lax.axis_index("gz")
    mz = own.shape[0]
    base = (mz + 2) * (2 * mz + mz)
    left, right = jnp.zeros(own.shape[1:], jnp.float32), jnp.zeros(own.shape[1:], jnp.float32)
    for plane, hop in ((one, 1), (two, 2), (three, 3)):
        left = left + scalars[pz, base + (pz ^ hop)] * plane[...]
        right = right + scalars[pz, base + gz + (pz ^ hop)] * plane[...]
    ahead = jnp.where(pz ^ 1 == pz + 1, 1.0, 0.0) * first_one[...]
    ahead = ahead + jnp.where(pz ^ 3 == pz + 1, 1.0, 0.0) * first_three[...]
    up_x, up_y = up_x[...].astype(jnp.bfloat16), up_y[...].astype(jnp.bfloat16)
    last[...] = top[...] - 0.5 * exact_right(exact_left(up_x, ahead), up_y)
    base = base + 2 * gz
    for j in range(mz):
        coarse[j] = own[j] + scalars[pz, base + j] * left + scalars[pz, base + mz + j] * right


def finish_kernel(
    sizes,
    received,
    wx,
    wy,
    wz,
    row_x,
    row_y,
    up_x,
    up_y,
    inner,
    top,
    before,
    coefficients,
    coarse,
    rim,
    foot,
    values,
    sem,
):
    px, py, pz = lax.axis_index("gx"), lax.axis_index("gy"), lax.axis_index("gz")
    mz, mx, my = before.shape
    depth, height, breadth = 2 * mz, 2 * mx, 2 * my
    split_at = breadth - 128
    body = (pl.ds(0, height - 8), pl.ds(0, split_at))
    copies = [
        pltpu.make_async_copy(inner.at[:, *body], coefficients.at[pl.ds(0, depth - 1), *body], sem.at[0]),
        pltpu.make_async_copy(top.at[body], coefficients.at[depth - 1, *body], sem.at[1]),
    ]
    start_all(copies)
    weights = wx[px] * wy[py] * wz[pz]
    got = three_pass(split(weights), split(received[...]))

    base = 9 * mz
    layers = mz + 1
    halo_x, halo_y, halo_xy = (got[base + i * layers : base + (i + 1) * layers] for i in range(3))
    pad = jnp.zeros((8 - layers, halo_x.shape[1]), jnp.float32)
    row = exact_right(jnp.concatenate([halo_x, pad], axis=0), up_y[...].astype(jnp.bfloat16))
    tall = jnp.concatenate([halo_y, jnp.zeros((128 - layers, halo_y.shape[1]), jnp.float32)], axis=0)
    col = exact_left(up_x[...].astype(jnp.bfloat16), jnp.transpose(tall))
    lane = lax.broadcasted_iota(jnp.int32, (1, 128), 1)
    last = lane == 127
    for z in range(depth):
        j = z // 2
        if z % 2 == 0:
            r, s, k = row[j : j + 1], 0.5 * col[:, j : j + 1], halo_xy[j : j + 1, 0:1]
        else:
            r = 0.5 * (row[j : j + 1] + row[j + 1 : j + 2])
            s = 0.25 * (col[:, j : j + 1] + col[:, j + 1 : j + 2])
            k = 0.5 * (halo_xy[j : j + 1, 0:1] + halo_xy[j + 1 : j + 2, 0:1])
        old = inner[z] if z < depth - 1 else top[...]
        rim[z] = old[:, split_at:] - jnp.where(last, s, 0.0)
        end = 0.5 * r[:, split_at:] + jnp.where(last, 0.25 * k, 0.0)
        rim[z, height - 1 : height, :] = rim[z, height - 1 : height, :] - end
        foot[z] = old[height - 8 :, :split_at]
        foot[z, 7:8, :] = old[height - 1 :, :split_at] - 0.5 * r[:, :split_at]
    copies.append(pltpu.make_async_copy(rim, coefficients.at[:, :, pl.ds(split_at, 128)], sem.at[2]))
    copies.append(pltpu.make_async_copy(foot, coefficients.at[:, pl.ds(height - 8, 8), pl.ds(0, split_at)], sem.at[3]))
    start_all(copies[2:])

    ux, vx = row_x[px, 9:10, :mx], row_x[px, 10:11, :mx]
    uy, vy = row_y[py, 9:10, :my], row_y[py, 10:11, :my]

    def part(sx, sy, z):
        at = (sx * 3 + sy) * mz + z
        return got[at : at + 1]

    for z in range(mz):
        a, b = [], []
        for sy, end in ((1, uy), (2, vy)):
            a.append(part(0, sy, z) + ux * part(1, sy, z)[:, 0:1] + vx * part(2, sy, z)[:, 0:1])
            b.append(end)
        for sx, end in ((1, ux), (2, vx)):
            a.append(end)
            b.append(part(sx, 0, z))
        zero = [jnp.zeros((4, mx), jnp.float32)]
        a, b = split(jnp.concatenate(a + zero, axis=0)), split(jnp.concatenate(b + zero, axis=0))
        values[z] = before[z] + three_pass(a, b, ((0,), (0,)))
    copies.append(pltpu.make_async_copy(values, coarse, sem.at[4]))
    copies[4].start()
    for copy in copies:
        copy.wait()


def call(kernel, name, out_shape, in_specs, out_specs, scratch=(), aliases=None, flops=1, size=1):
    return pl.pallas_call(
        kernel,
        out_shape=out_shape,
        in_specs=in_specs,
        out_specs=out_specs,
        scratch_shapes=list(scratch),
        input_output_aliases=aliases or {},
        compiler_params=pltpu.CompilerParams(vmem_limit_bytes=VMEM_LIMIT),
        cost_estimate=pl.CostEstimate(flops=flops, bytes_accessed=size, transcendentals=0),
        name=name,
    )


ANY = pl.BlockSpec(memory_space=pl.ANY)
HBM = pl.BlockSpec(memory_space=pltpu.HBM)
SMEM = pl.BlockSpec(memory_space=pltpu.SMEM)
VMEM = pl.BlockSpec(memory_space=pltpu.VMEM)


def shape(*dims):
    return jax.ShapeDtypeStruct(dims, jnp.float32)


def on_device(sizes, field):
    gx, gy, gz = sizes
    depth, height, breadth = field.shape
    mz, mx, my = depth // 2, height // 2, breadth // 2
    count = gx * gy * gz
    axes = ("gx", "gy", "gz")
    tx, ty, tz = line_tables(gx, mx), line_tables(gy, my), line_tables(gz, mz)

    def rows(t, parts, m):
        table = np.zeros((parts, 16, 2 * m))
        table[:, 0], table[:, 1] = t["to_right"], t["to_left"]
        table[:, 8, :m], table[:, 9, :m], table[:, 10, :m] = t["first"], t["from_left"], t["from_right"]
        return f32(table)

    def right_side(t, parts, m):
        table = np.zeros((parts, 2 * m, 2 * m))
        table[:, :, :m] = t["block"].transpose(0, 2, 1)
        table[:, :, m:] = even_selector(m)
        return f32(table)

    row_x, row_y = rows(tx, gx, mx), rows(ty, gy, my)
    right_x, right_y = right_side(tx, gx, mx), f32(ty["block"].transpose(0, 2, 1))
    sum_x = f32(np.repeat(np.stack([tx["to_right"], tx["to_left"]], axis=1)[..., None], 128, axis=3))
    sum_y, fold_z = np.zeros((gy, breadth, 128)), np.zeros((gz, 8, 128))
    for out in range(mz + 2):
        sum_y[:, :, 2 * out], sum_y[:, :, 2 * out + 1] = ty["to_right"], ty["to_left"]
    sum_y[:, 0, 2 * (mz + 2) : 2 * (mz + 2) + mz] = 1.0

    width = max((mz + 2) * (depth + mz) + 2 * gz + 2 * mz, gx, gy)
    scalars = np.zeros((8 * ((gz + 2 + 7) // 8), 128 * ((width + 127) // 128)))
    for p in range(gz):
        full = np.concatenate([tz["block"][p], tz["to_right"][p : p + 1], tz["to_left"][p : p + 1]], axis=0)
        nodes = np.zeros((mz + 2, mz))
        nodes[:mz] = np.eye(mz)
        nodes[:mz, 0] -= tz["first"][p]
        nodes[mz, 0] = tz["first_right"][p]
        ends = [tz[key][p] for key in ("weight_left", "weight_right", "from_left", "from_right")]
        line = np.concatenate([full.reshape(-1), nodes.reshape(-1)] + ends)
        scalars[p, : line.size] = line
        fold_z[p, :depth, : 2 * (mz + 2)] = np.repeat(full.T, 2, axis=1)
        for j in range(mz):
            fold_z[p, 2 * j, 2 * (mz + 2) + j] = 1.0
    scalars[gz, :gx], scalars[gz + 1, :gy] = tx["first_right"], ty["first_right"]
    scalars = f32(scalars)

    vmem = pltpu.VMEM
    operands = (scalars, field, sum_x, f32(sum_y), f32(fold_z), row_y, row_x, right_y, right_x, f32(tx["block"]))
    operands += (f32(even_selector(my)),)
    send, own, even, near, far, first = call(
        functools.partial(local_kernel, sizes),
        "local",
        [shape(count, 4, my), shape(mz, mx, my), shape(mz, mx, my)] + [shape(mx, my)] * 3,
        [HBM] * 11,
        [VMEM] * 6,
        [
            vmem((2, depth, height, my), jnp.float32),
            vmem(sum_x.shape[1:], jnp.float32),
            vmem(sum_y.shape[1:], jnp.float32),
            vmem(fold_z.shape[1:], jnp.float32),
            vmem(row_y.shape[1:], jnp.float32),
            vmem(row_x.shape[1:], jnp.float32),
            vmem(right_y.shape[1:], jnp.float32),
            vmem(right_x.shape[1:], jnp.float32),
            vmem((mx, height), jnp.float32),
            vmem((breadth, my), jnp.float32),
            vmem((27, 4, my), jnp.float32),
            pltpu.SMEM(scalars.shape, jnp.float32),
            pltpu.SemaphoreType.DMA((2 * depth + 10,)),
        ],
    )(*(pltpu.with_memory_space_constraint(jnp.asarray(value), pltpu.HBM) for value in operands))
    received = lax.all_to_all(send, axes, 0, 0, tiled=True).reshape(count * 4, my)

    assert gz == 4
    plans = ((near, 1), (far, 2), (far, 3), (first, 1), (first, 3))
    gets = [lax.ppermute(plane, "gz", [(i, i ^ hop) for i in range(gz)]) for plane, hop in plans]

    up_x, up_y = f32(lift_matrix(mx)[:, :mx]), f32(lift_matrix(my)[:, :my].T)
    inner, top = call(
        inner_kernel,
        "inner",
        [shape(depth - 1, height, breadth), shape(height, breadth)],
        [VMEM] * 4,
        [VMEM] * 2,
    )(field, even, up_x, up_y)
    last, before = call(
        upper_kernel,
        "upper",
        [shape(height, breadth), shape(mz, mx, my)],
        [SMEM] + [VMEM] * 9,
        [VMEM] * 2,
    )(scalars, top, own, up_x, up_y, *gets)

    wx, wy, wz = combine_tables(sizes, tx, ty, tz, mz)
    return call(
        functools.partial(finish_kernel, sizes),
        "finish",
        [shape(*field.shape), shape(mz, mx, my)],
        [VMEM] * 11,
        [HBM, HBM],
        [
            vmem((depth, height, 128), jnp.float32),
            vmem((depth, 8, breadth - 128), jnp.float32),
            vmem((mz, mx, my), jnp.float32),
            pltpu.SemaphoreType.DMA((5,)),
        ],
    )(received, wx, wy, wz, row_x, row_y, up_x, up_y, inner, last, before)


def solution(mesh):
    sizes = tuple(mesh.shape[axis] for axis in ("gx", "gy", "gz"))
    return jax.shard_map(
        functools.partial(on_device, sizes),
        mesh=mesh,
        in_specs=(P("gz", "gx", "gy"),),
        out_specs=(P("gz", "gx", "gy"), P("gz", "gx", "gy")),
        check_vma=False,
    )
```

time: 37.5 us -> 22.9 us (0.61)
  local copies, waits for them, and re-layouts: 8.03 us -> 0.05 us
  Pallas kernels: 14.9 us -> 7.29 us
  starting transfers between devices: 9.9 us -> 11.4 us
    unnamed x36 -> x18, local copies, waits for them, and re-layouts: 8.03 us -> 0.05 us
    pallas_call x4, Pallas kernels: 14.9 us -> 7.29 us  [the longest x1 4.09 us: on_device(): call(functools.partial(local_kernel, sizes), 'local', [shape(count, 4, my...]
    all_to_all x1, starting transfers between devices: 4.9 us -> 7.3 us  [on_device(): lax.all_to_all(send, axes, 0, 0, tiled=True).reshape(count * 4, my)]
    ppermute x3 -> x5, starting transfers between devices: 4.99 us -> 4.09 us  [on_device(): lax.ppermute(plane, 'gz', [(i, i ^ hop) for i in range(gz)])]
    all_to_all x1, waiting for transfers between devices: 0.76 us -> 0.01 us  [on_device(): lax.all_to_all(send, axes, 0, 0, tiled=True).reshape(count * 4, my)]
    ppermute x3 -> x5, waiting for transfers between devices: 2.7 us -> 3.16 us  [on_device(): lax.ppermute(plane, 'gz', [(i, i ^ hop) for i in range(gz)])]
  transfers between devices with their start and end apart: 4 -> 6, of which waited for: 2 -> 2; matrix products, arithmetic and copies ran while one was open for 0% -> 0% of each run, Pallas kernels for 18% -> 7%
where the time goes in v2:
time: 22.9 us; the launch traced here: 22.7 us
  starting transfers between devices  11.4 us (50%)
  Pallas kernels  7.29 us (32%)
  waiting for transfers between devices  3.17 us (14%)
  between operations  0.79 us (3%)
    all_to_all x1, starting transfers between devices, on_device(): lax.all_to_all(send, axes, 0, 0, tiled=True).reshape(count * 4, my)  7.3 us
    pallas_call x1, Pallas kernels, on_device(): call(functools.partial(local_kernel, sizes), 'local', [shape(count, 4, my...  4.09 us
    ppermute x5, starting transfers between devices, on_device(): lax.ppermute(plane, 'gz', [(i, i ^ hop) for i in range(gz)])  4.09 us
    ppermute x5, waiting for transfers between devices, on_device(): lax.ppermute(plane, 'gz', [(i, i ^ hop) for i in range(gz)])  3.16 us
    pallas_call x1, Pallas kernels, on_device(): call(functools.partial(finish_kernel, sizes), 'finish', [shape(*field.sha...  1.61 us
    pallas_call x1, Pallas kernels, on_device(): call(upper_kernel, 'upper', [shape(height, breadth), shape(mz, mx, my)],...  1.08 us
    pallas_call x1, Pallas kernels, on_device(): call(inner_kernel, 'inner', [shape(depth - 1, height, breadth), shape(hei...  0.5 us
  transfers between devices with their start and end apart: 6, of which 2 were waited for; matrix products, arithmetic and copies ran while one was open for 0% of the time, Pallas kernels for 7%

profile of v2, /device:TPU:0, one launch (start us, length us, event | category | flops | bytes accessed | tf_op | source)
XLA Modules:
  0.0 22.7 jit_solution(6193689189990380158)
XLA Ops:
  0.6 0.0 copy-start
  0.6 0.0 copy-start.2
  0.7 4.1 %local.1 = (f32[32,4,128]{2,1,0:T(4,128)}, f32[2,128,128]{2,1,0:T(8,128)S(1)}, f32[2,128,128]{2,1,0:T(8,128)S(1)}, f32[128,128]{1,0:T(8,128)S(1)}, f32[128,128]{1,0:T(8,128)S(1)}, /*index=5*/f32[128,128]{1,0:T(8,128)S(1)}) custom-call(f32[8,128]{1,0:T(8,128)} %constant.30.clone.refs_0_.scalars, f32[4,256,256]{2,1,0:T(8,128)} %field.1, ...), custom_call_target="tpu_custom_call" | custom-call | flops 1 | bytes 1 | tf_op jit(solution)/shard_map/local/pallas_call | solution.py:470
  4.7 0.0 copy-start.1
  4.8 7.3 %all-to-all-start = ((f32[32,4,128]{2,1,0:T(4,128)}), f32[32,4,128]{2,1,0:T(4,128)S(1)}, u32[]{:S(2)}, u32[]{:S(2)}) async-start(f32[32,4,128]{2,1,0:T(4,128)} %get-tuple-element.12), calls=%async_computation | async-start | bytes 131072 | tf_op jit(solution)/shard_map/all_to_all | solution.py:492
  12.1 0.3 %collective-permute-start = (f32[128,128]{1,0:T(8,128)S(1)}, f32[128,128]{1,0:T(8,128)S(1)}, u32[]{:S(2)}, u32[]{:S(2)}) collective-permute-start(f32[128,128]{1,0:T(8,128)S(1)} %get-tuple-element.17), channel_id=1, source_target_pairs={{0,1},{1,0},{2,3},{3,2},{4,5},{5,4},{6,7},{7,6},{8,9},{9,8},{10,11... | collective-permute-start | bytes 196616 | tf_op jit(solution)/shard_map/ppermute | solution.py:496
  12.4 1.6 %collective-permute-start.2 = (f32[128,128]{1,0:T(8,128)S(1)}, f32[128,128]{1,0:T(8,128)S(1)}, u32[]{:S(2)}, u32[]{:S(2)}) collective-permute-start(f32[128,128]{1,0:T(8,128)S(1)} %get-tuple-element.18), channel_id=1, source_target_pairs={{0,3},{1,2},{2,1},{3,0},{4,7},{5,6},{6,5},{7,4},{8,11},{9,10},{10,... | collective-permute-start | bytes 196616 | tf_op jit(solution)/shard_map/ppermute | solution.py:496
  14.0 0.3 %collective-permute-start.1 = (f32[128,128]{1,0:T(8,128)S(1)}, f32[128,128]{1,0:T(8,128)S(1)}, u32[]{:S(2)}, u32[]{:S(2)}) collective-permute-start(f32[128,128]{1,0:T(8,128)S(1)} %get-tuple-element.18), channel_id=1, source_target_pairs={{0,2},{1,3},{2,0},{3,1},{4,6},{5,7},{6,4},{7,5},{8,10},{9,11},{10,... | collective-permute-start | bytes 196616 | tf_op jit(solution)/shard_map/ppermute | solution.py:496
  14.3 1.3 %collective-permute-start.4 = (f32[128,128]{1,0:T(8,128)S(1)}, f32[128,128]{1,0:T(8,128)S(1)}, u32[]{:S(2)}, u32[]{:S(2)}) collective-permute-start(f32[128,128]{1,0:T(8,128)S(1)} %get-tuple-element.19), channel_id=1, source_target_pairs={{0,3},{1,2},{2,1},{3,0},{4,7},{5,6},{6,5},{7,4},{8,11},{9,10},{10,... | collective-permute-start | bytes 196616 | tf_op jit(solution)/shard_map/ppermute | solution.py:496
  15.5 0.6 %collective-permute-start.3 = (f32[128,128]{1,0:T(8,128)S(1)}, f32[128,128]{1,0:T(8,128)S(1)}, u32[]{:S(2)}, u32[]{:S(2)}) collective-permute-start(f32[128,128]{1,0:T(8,128)S(1)} %get-tuple-element.19), channel_id=1, source_target_pairs={{0,1},{1,0},{2,3},{3,2},{4,5},{5,4},{6,7},{7,6},{8,9},{9,8},{10,11... | collective-permute-start | bytes 196616 | tf_op jit(solution)/shard_map/ppermute | solution.py:496
  16.2 0.0 copy-done
  16.2 0.0 copy-done.2
  16.2 0.0 copy-done.1
  16.2 0.5 %inner.1 = (f32[3,256,256]{2,1,0:T(8,128)S(1)}, f32[256,256]{1,0:T(8,128)S(1)}) custom-call(f32[4,256,256]{2,1,0:T(8,128)S(1)} %copy-done, f32[2,128,128]{2,1,0:T(8,128)S(1)} %get-tuple-element.13.even, f32[256,128]{1,0:T(8,128)S(1)} %copy-done.2, f32[128,256]{1,0:T(8,128)S(1)} %copy-done.1), custom_call_target="tpu_custom_call" | custom-call | flops 1 | bytes 1 | tf_op jit(solution)/shard_map/inner/pallas_call | solution.py:499
  16.7 0.0 collective-permute-done.one
  16.7 0.0 collective-permute-done.2.three
  16.7 2.5 %collective-permute-done.1.two = f32[128,128]{1,0:T(8,128)S(1)} collective-permute-done((f32[128,128]{1,0:T(8,128)S(1)}, f32[128,128]{1,0:T(8,128)S(1)}, u32[]{:S(2)}, u32[]{:S(2)}) %collective-permute-start.1) | collective-permute-done | bytes 65568 | tf_op jit(solution)/shard_map/ppermute | solution.py:496
  19.2 0.7 %collective-permute-done.4.first_three = f32[128,128]{1,0:T(8,128)S(1)} collective-permute-done((f32[128,128]{1,0:T(8,128)S(1)}, f32[128,128]{1,0:T(8,128)S(1)}, u32[]{:S(2)}, u32[]{:S(2)}) %collective-permute-start.4) | collective-permute-done | bytes 65568 | tf_op jit(solution)/shard_map/ppermute | solution.py:496
  19.9 0.0 collective-permute-done.3.first_one
  19.9 0.0 copy-done.8
  19.9 0.0 copy-start.4
  19.9 0.0 copy-start.5
  19.9 0.0 copy-start.6
  19.9 0.0 copy-start.7
  19.9 1.1 %upper.1 = (f32[256,256]{1,0:T(8,128)S(1)}, f32[2,128,128]{2,1,0:T(8,128)S(1)}) custom-call(f32[8,128]{1,0:T(8,128)S(1)} %copy-done.8, f32[256,256]{1,0:T(8,128)S(1)} %get-tuple-element.15.top, f32[2,128,128]{2,1,0:T(8,128)S(1)} %get-tuple-element.16.own, f32[256,128]{1,0:T(8,128)S(1)} %copy-done.2, f32[128,256]{1,0:T(8,128)S(1)} %copy-done.1, ...), custom_call_target="tpu_custom_call" | custom-call | flops 1 | bytes 1 | tf_op jit(solution)/shard_map/upper/pallas_call | solution.py:506
  21.0 0.0 all-to-all-done
  21.0 0.0 copy-done.3
  21.0 0.0 copy-done.4
  21.0 0.0 copy-done.5
  21.1 0.0 copy-done.6
  21.1 0.0 copy-done.7
  21.1 1.6 %finish.1 = (f32[4,256,256]{2,1,0:T(8,128)}, f32[2,128,128]{2,1,0:T(8,128)}) custom-call(f32[128,128]{1,0:T(8,128)S(1)} %bitcast.1, f32[2,32,128]{2,1,0:T(8,128)S(1)} %copy-done.7, f32[4,32,128]{2,1,0:T(8,128)S(1)} %copy-done.6, f32[4,32,128]{2,1,0:T(8,128)S(1)} %copy-done.5, f32[2,16,256]{2,1,0:T(8,128)S(1)} %copy-done.4, f32[4,16,256]{2,1,0:T(8,128)S(1)} %copy-done.3, ...), custom_call_target="tpu_custom_call" | custom-call | flops 1 | bytes 1 | tf_op jit(solution)/shard_map/finish/pallas_call | solution.py:515
  (2 shorter events, 0.0 us)
Async XLA Ops:
  0.6 15.5 %copy-start = (f32[4,256,256]{2,1,0:T(8,128)S(1)}, f32[4,256,256]{2,1,0:T(8,128)}, u32[]{:S(2)}) copy-start(f32[4,256,256]{2,1,0:T(8,128)} %field.1) | copy-start | bytes 3145732
  0.6 15.5 %copy-start.2 = (f32[256,128]{1,0:T(8,128)S(1)}, f32[256,128]{1,0:T(8,128)}, u32[]{:S(2)}) copy-start(f32[256,128]{1,0:T(8,128)} %constant.40.clone.up_x) | copy-start | bytes 393220
  4.7 11.4 %copy-start.1 = (f32[128,256]{1,0:T(8,128)S(1)}, f32[128,256]{1,0:T(8,128)}, u32[]{:S(2)}) copy-start(f32[128,256]{1,0:T(8,128)} %constant.41.clone.up_y) | copy-start | bytes 393220
  4.8 16.3 %all-to-all-start = ((f32[32,4,128]{2,1,0:T(4,128)}), f32[32,4,128]{2,1,0:T(4,128)S(1)}, u32[]{:S(2)}, u32[]{:S(2)}) async-start(f32[32,4,128]{2,1,0:T(4,128)} %get-tuple-element.12), calls=%async_computation | async-start | bytes 131072 | tf_op jit(solution)/shard_map/all_to_all | solution.py:492
  12.1 4.6 %collective-permute-start = (f32[128,128]{1,0:T(8,128)S(1)}, f32[128,128]{1,0:T(8,128)S(1)}, u32[]{:S(2)}, u32[]{:S(2)}) collective-permute-start(f32[128,128]{1,0:T(8,128)S(1)} %get-tuple-element.17), channel_id=1, source_target_pairs={{0,1},{1,0},{2,3},{3,2},{4,5},{5,4},{6,7},{7,6},{8,9},{9,8},{10,11... | collective-permute-start | bytes 196616 | tf_op jit(solution)/shard_map/ppermute | solution.py:496
  12.4 4.3 %collective-permute-start.2 = (f32[128,128]{1,0:T(8,128)S(1)}, f32[128,128]{1,0:T(8,128)S(1)}, u32[]{:S(2)}, u32[]{:S(2)}) collective-permute-start(f32[128,128]{1,0:T(8,128)S(1)} %get-tuple-element.18), channel_id=1, source_target_pairs={{0,3},{1,2},{2,1},{3,0},{4,7},{5,6},{6,5},{7,4},{8,11},{9,10},{10,... | collective-permute-start | bytes 196616 | tf_op jit(solution)/shard_map/ppermute | solution.py:496
  14.0 5.2 %collective-permute-start.1 = (f32[128,128]{1,0:T(8,128)S(1)}, f32[128,128]{1,0:T(8,128)S(1)}, u32[]{:S(2)}, u32[]{:S(2)}) collective-permute-start(f32[128,128]{1,0:T(8,128)S(1)} %get-tuple-element.18), channel_id=1, source_target_pairs={{0,2},{1,3},{2,0},{3,1},{4,6},{5,7},{6,4},{7,5},{8,10},{9,11},{10,... | collective-permute-start | bytes 196616 | tf_op jit(solution)/shard_map/ppermute | solution.py:496
  14.3 5.6 %collective-permute-start.4 = (f32[128,128]{1,0:T(8,128)S(1)}, f32[128,128]{1,0:T(8,128)S(1)}, u32[]{:S(2)}, u32[]{:S(2)}) collective-permute-start(f32[128,128]{1,0:T(8,128)S(1)} %get-tuple-element.19), channel_id=1, source_target_pairs={{0,3},{1,2},{2,1},{3,0},{4,7},{5,6},{6,5},{7,4},{8,11},{9,10},{10,... | collective-permute-start | bytes 196616 | tf_op jit(solution)/shard_map/ppermute | solution.py:496
  15.5 4.3 %collective-permute-start.3 = (f32[128,128]{1,0:T(8,128)S(1)}, f32[128,128]{1,0:T(8,128)S(1)}, u32[]{:S(2)}, u32[]{:S(2)}) collective-permute-start(f32[128,128]{1,0:T(8,128)S(1)} %get-tuple-element.19), channel_id=1, source_target_pairs={{0,1},{1,0},{2,3},{3,2},{4,5},{5,4},{6,7},{7,6},{8,9},{9,8},{10,11... | collective-permute-start | bytes 196616 | tf_op jit(solution)/shard_map/ppermute | solution.py:496
  16.2 3.7 %copy-start.8 = (f32[8,128]{1,0:T(8,128)S(1)}, f32[8,128]{1,0:T(8,128)}, u32[]{:S(2)}) copy-start(f32[8,128]{1,0:T(8,128)} %constant.30.clone.refs_0_.scalars) | copy-start | bytes 12292
  19.9 1.2 %copy-start.3 = (f32[4,16,256]{2,1,0:T(8,128)S(1)}, f32[4,16,256]{2,1,0:T(8,128)}, u32[]{:S(2)}) copy-start(f32[4,16,256]{2,1,0:T(8,128)} %constant.34.clone.refs_5_.row_y) | copy-start | bytes 196612
  19.9 1.2 %copy-start.4 = (f32[2,16,256]{2,1,0:T(8,128)S(1)}, f32[2,16,256]{2,1,0:T(8,128)}, u32[]{:S(2)}) copy-start(f32[2,16,256]{2,1,0:T(8,128)} %constant.35.clone.refs_6_.row_x) | copy-start | bytes 98308
  19.9 1.2 %copy-start.5 = (f32[4,32,128]{2,1,0:T(8,128)S(1)}, f32[4,32,128]{2,1,0:T(8,128)}, u32[]{:S(2)}) copy-start(f32[4,32,128]{2,1,0:T(8,128)} %constant.44.clone.wz) | copy-start | bytes 196612
  19.9 1.2 %copy-start.6 = (f32[4,32,128]{2,1,0:T(8,128)S(1)}, f32[4,32,128]{2,1,0:T(8,128)}, u32[]{:S(2)}) copy-start(f32[4,32,128]{2,1,0:T(8,128)} %constant.43.clone.wy) | copy-start | bytes 196612
  19.9 1.2 %copy-start.7 = (f32[2,32,128]{2,1,0:T(8,128)S(1)}, f32[2,32,128]{2,1,0:T(8,128)}, u32[]{:S(2)}) copy-start(f32[2,32,128]{2,1,0:T(8,128)} %constant.42.clone.wx) | copy-start | bytes 98308

commit v3 on v2

--- a/solution.py
+++ b/solution.py
@@ -173,8 +173,8 @@
 
 def local_kernel(sizes, *refs):
     numbers, field, sum_x, sum_y, fold_z, row_y, row_x, line_y, line_x, block_x, pick = refs[:11]
-    send, own, even, near, far, first = refs[11:17]
-    f, ax, ay, az, vy, vx, ry, rx, bx, sel, kinds, scalars, sem = refs[17:]
+    send, own, even, near, far, first, both_far = refs[11:18]
+    f, ax, ay, az, vy, vx, ry, rx, bx, sel, kinds, scalars, sem = refs[18:]
     gx, gy, gz = sizes
     px, py, pz = lax.axis_index("gx"), lax.axis_index("gy"), lax.axis_index("gz")
     depth, height, _ = field.shape
@@ -279,6 +279,8 @@
         own[j] = evens[j] + outs[j]
     near[...] = jnp.where(pz % 2 == 0, outs[mz], outs[mz + 1])
     far[...] = jnp.where(pz % 4 < 2, outs[mz], outs[mz + 1])
+    both_far[0] = jnp.where(pz % 4 < 2, outs[mz], outs[mz + 1])
+    both_far[1] = evens[0]
     first[...] = evens[0]
 
 
@@ -293,17 +295,17 @@
     top[...] = field[depth - 1] - 0.5 * lifted[mz - 1]
 
 
-def upper_kernel(scalars, top, own, up_x, up_y, one, two, three, first_one, first_three, last, coarse):
+def upper_kernel(scalars, top, own, up_x, up_y, one, two, three, first, last, coarse):
     gz = lax.axis_size("gz")
     pz = lax.axis_index("gz")
     mz = own.shape[0]
     base = (mz + 2) * (2 * mz + mz)
     left, right = jnp.zeros(own.shape[1:], jnp.float32), jnp.zeros(own.shape[1:], jnp.float32)
-    for plane, hop in ((one, 1), (two, 2), (three, 3)):
-        left = left + scalars[pz, base + (pz ^ hop)] * plane[...]
-        right = right + scalars[pz, base + gz + (pz ^ hop)] * plane[...]
-    ahead = jnp.where(pz ^ 1 == pz + 1, 1.0, 0.0) * first_one[...]
-    ahead = ahead + jnp.where(pz ^ 3 == pz + 1, 1.0, 0.0) * first_three[...]
+    for plane, hop in ((one[...], 1), (two[...], 2), (three[0], 3)):
+        left = left + scalars[pz, base + (pz ^ hop)] * plane
+        right = right + scalars[pz, base + gz + (pz ^ hop)] * plane
+    ahead = jnp.where(pz ^ 1 == pz + 1, 1.0, 0.0) * first[...]
+    ahead = ahead + jnp.where(pz ^ 3 == pz + 1, 1.0, 0.0) * three[1]
     up_x, up_y = up_x[...].astype(jnp.bfloat16), up_y[...].astype(jnp.bfloat16)
     last[...] = top[...] - 0.5 * exact_right(exact_left(up_x, ahead), up_y)
     base = base + 2 * gz
@@ -467,12 +469,12 @@
     vmem = pltpu.VMEM
     operands = (scalars, field, sum_x, f32(sum_y), f32(fold_z), row_y, row_x, right_y, right_x, f32(tx["block"]))
     operands += (f32(even_selector(my)),)
-    send, own, even, near, far, first = call(
+    send, own, even, near, far, first, both_far = call(
         functools.partial(local_kernel, sizes),
         "local",
-        [shape(count, 4, my), shape(mz, mx, my), shape(mz, mx, my)] + [shape(mx, my)] * 3,
+        [shape(count, 4, my), shape(mz, mx, my), shape(mz, mx, my)] + [shape(mx, my)] * 3 + [shape(2, mx, my)],
         [HBM] * 11,
-        [VMEM] * 6,
+        [VMEM] * 7,
         [
             vmem((2, depth, height, my), jnp.float32),
             vmem(sum_x.shape[1:], jnp.float32),
@@ -492,7 +494,7 @@
     received = lax.all_to_all(send, axes, 0, 0, tiled=True).reshape(count * 4, my)
 
     assert gz == 4
-    plans = ((near, 1), (far, 2), (far, 3), (first, 1), (first, 3))
+    plans = ((near, 1), (far, 2), (both_far, 3), (first, 1))
     gets = [lax.ppermute(plane, "gz", [(i, i ^ hop) for i in range(gz)]) for plane, hop in plans]
 
     up_x, up_y = f32(lift_matrix(mx)[:, :mx]), f32(lift_matrix(my)[:, :my].T)
@@ -507,7 +509,7 @@
         upper_kernel,
         "upper",
         [shape(height, breadth), shape(mz, mx, my)],
-        [SMEM] + [VMEM] * 9,
+        [SMEM] + [VMEM] * 8,
         [VMEM] * 2,
     )(scalars, top, own, up_x, up_y, *gets)
 

time: 22.9 us -> 21.7 us (0.948)
  starting transfers between devices: 11.4 us -> 9.71 us
  waiting for transfers between devices: 3.17 us -> 3.65 us
    all_to_all x1, starting transfers between devices: 7.3 us -> 5.18 us  [on_device(): lax.all_to_all(send, axes, 0, 0, tiled=True).reshape(count * 4, my)]
    all_to_all x1, waiting for transfers between devices: 0.01 us -> 1.36 us  [on_device(): lax.all_to_all(send, axes, 0, 0, tiled=True).reshape(count * 4, my)]
    ppermute x5 -> x4, waiting for transfers between devices: 3.16 us -> 2.29 us  [on_device(): lax.ppermute(plane, 'gz', [(i, i ^ hop) for i in range(gz)])]
    ppermute x5 -> x4, starting transfers between devices: 4.09 us -> 4.53 us  [on_device(): lax.ppermute(plane, 'gz', [(i, i ^ hop) for i in range(gz)])]
  transfers between devices with their start and end apart: 6 -> 5, of which waited for: 2 -> 2; matrix products, arithmetic and copies ran while one was open for 0% -> 0% of each run, Pallas kernels for 7% -> 7%
where the time goes in v3:
time: 21.7 us; the launch traced here: 21.5 us
  starting transfers between devices  9.71 us (45%)
  Pallas kernels  7.29 us (34%)
  waiting for transfers between devices  3.65 us (17%)
  between operations  0.77 us (4%)
    all_to_all x1, starting transfers between devices, on_device(): lax.all_to_all(send, axes, 0, 0, tiled=True).reshape(count * 4, my)  5.18 us
    ppermute x4, starting transfers between devices, on_device(): lax.ppermute(plane, 'gz', [(i, i ^ hop) for i in range(gz)])  4.53 us
    pallas_call x1, Pallas kernels, on_device(): call(functools.partial(local_kernel, sizes), 'local', [shape(count, 4, my...  4.09 us
    ppermute x4, waiting for transfers between devices, on_device(): lax.ppermute(plane, 'gz', [(i, i ^ hop) for i in range(gz)])  2.29 us
    pallas_call x1, Pallas kernels, on_device(): call(functools.partial(finish_kernel, sizes), 'finish', [shape(*field.sha...  1.61 us
    all_to_all x1, waiting for transfers between devices, on_device(): lax.all_to_all(send, axes, 0, 0, tiled=True).reshape(count * 4, my)  1.36 us
    pallas_call x1, Pallas kernels, on_device(): call(upper_kernel, 'upper', [shape(height, breadth), shape(mz, mx, my)],...  1.08 us
    pallas_call x1, Pallas kernels, on_device(): call(inner_kernel, 'inner', [shape(depth - 1, height, breadth), shape(hei...  0.5 us
  transfers between devices with their start and end apart: 5, of which 2 were waited for; matrix products, arithmetic and copies ran while one was open for 0% of the time, Pallas kernels for 7%

profile of v3, /device:TPU:0, one launch (start us, length us, event | category | flops | bytes accessed | tf_op | source)
XLA Modules:
  0.0 21.5 jit_solution(15604568497792123686)
XLA Ops:
  0.6 0.0 copy-start
  0.6 0.0 copy-start.2
  0.7 4.1 %local.1 = (f32[32,4,128]{2,1,0:T(4,128)}, f32[2,128,128]{2,1,0:T(8,128)S(1)}, f32[2,128,128]{2,1,0:T(8,128)S(1)}, f32[128,128]{1,0:T(8,128)S(1)}, f32[128,128]{...) custom-call(f32[8,128]{1,0:T(8,128)} %constant.30.clone.refs_0_.scalars, f32[4,256,256]{2,1,0:T(8,128)} %field.1, ...), custom_call_target="tpu_custom_call" | custom-call | flops 1 | bytes 1 | tf_op jit(solution)/shard_map/local/pallas_call | solution.py:472
  4.8 0.0 copy-start.1
  4.8 2.5 %collective-permute-start.2 = (f32[2,128,128]{2,1,0:T(8,128)S(1)}, f32[2,128,128]{2,1,0:T(8,128)S(1)}, u32[]{:S(2)}, u32[]{:S(2)}) collective-permute-start(f32[2,128,128]{2,1,0:T(8,128)S(1)} %get-tuple-element.20), channel_id=1, source_target_pairs={{0,3},{1,2},{2,1},{3,0},{4,7},{5,6},{6,5},{7,4},{8,11},{9,10},{10,... | collective-permute-start | bytes 393224 | tf_op jit(solution)/shard_map/ppermute | solution.py:498
  7.2 5.2 %all-to-all-start = ((f32[32,4,128]{2,1,0:T(4,128)}), f32[32,4,128]{2,1,0:T(4,128)S(1)}, u32[]{:S(2)}, u32[]{:S(2)}) async-start(f32[32,4,128]{2,1,0:T(4,128)} %get-tuple-element.13), calls=%async_computation | async-start | bytes 131072 | tf_op jit(solution)/shard_map/all_to_all | solution.py:494
  12.4 0.3 %collective-permute-start = (f32[128,128]{1,0:T(8,128)S(1)}, f32[128,128]{1,0:T(8,128)S(1)}, u32[]{:S(2)}, u32[]{:S(2)}) collective-permute-start(f32[128,128]{1,0:T(8,128)S(1)} %get-tuple-element.18), channel_id=1, source_target_pairs={{0,1},{1,0},{2,3},{3,2},{4,5},{5,4},{6,7},{7,6},{8,9},{9,8},{10,11... | collective-permute-start | bytes 196616 | tf_op jit(solution)/shard_map/ppermute | solution.py:498
  12.7 1.7 %collective-permute-start.1 = (f32[128,128]{1,0:T(8,128)S(1)}, f32[128,128]{1,0:T(8,128)S(1)}, u32[]{:S(2)}, u32[]{:S(2)}) collective-permute-start(f32[128,128]{1,0:T(8,128)S(1)} %get-tuple-element.19), channel_id=1, source_target_pairs={{0,2},{1,3},{2,0},{3,1},{4,6},{5,7},{6,4},{7,5},{8,10},{9,11},{10,... | collective-permute-start | bytes 196616 | tf_op jit(solution)/shard_map/ppermute | solution.py:498
  14.4 0.1 collective-permute-start.3
  14.5 0.0 copy-done
  14.5 0.0 copy-done.2
  14.5 0.0 copy-done.1
  14.5 0.0 copy-start.8
  14.5 0.5 %inner.1 = (f32[3,256,256]{2,1,0:T(8,128)S(1)}, f32[256,256]{1,0:T(8,128)S(1)}) custom-call(f32[4,256,256]{2,1,0:T(8,128)S(1)} %copy-done, f32[2,128,128]{2,1,0:T(8,128)S(1)} %get-tuple-element.14.even, f32[256,128]{1,0:T(8,128)S(1)} %copy-done.2, f32[128,256]{1,0:T(8,128)S(1)} %copy-done.1), custom_call_target="tpu_custom_call" | custom-call | flops 1 | bytes 1 | tf_op jit(solution)/shard_map/inner/pallas_call | solution.py:501
  15.0 0.0 collective-permute-done.one
  15.0 2.3 %collective-permute-done.1.two = f32[128,128]{1,0:T(8,128)S(1)} collective-permute-done((f32[128,128]{1,0:T(8,128)S(1)}, f32[128,128]{1,0:T(8,128)S(1)}, u32[]{:S(2)}, u32[]{:S(2)}) %collective-permute-start.1) | collective-permute-done | bytes 65568 | tf_op jit(solution)/shard_map/ppermute | solution.py:498
  17.3 0.0 collective-permute-done.3.first
  17.3 0.0 collective-permute-done.2.three
  17.3 0.0 copy-done.8
  17.3 0.0 copy-start.3
  17.3 0.0 copy-start.4
  17.3 0.0 copy-start.5
  17.4 0.0 copy-start.6
  17.4 0.0 copy-start.7
  17.4 1.1 %upper.1 = (f32[256,256]{1,0:T(8,128)S(1)}, f32[2,128,128]{2,1,0:T(8,128)S(1)}) custom-call(f32[8,128]{1,0:T(8,128)S(1)} %copy-done.8, f32[256,256]{1,0:T(8,128)S(1)} %get-tuple-element.16.top, f32[2,128,128]{2,1,0:T(8,128)S(1)} %get-tuple-element.17.own, f32[256,128]{1,0:T(8,128)S(1)} %copy-done.2, f32[128,256]{1,0:T(8,128)S(1)} %copy-done.1, ...), custom_call_target="tpu_custom_call" | custom-call | flops 1 | bytes 1 | tf_op jit(solution)/shard_map/upper/pallas_call | solution.py:508
  18.5 1.4 %all-to-all-done = f32[32,4,128]{2,1,0:T(4,128)S(1)} async-done(((f32[32,4,128]{2,1,0:T(4,128)}), f32[32,4,128]{2,1,0:T(4,128)S(1)}, u32[]{:S(2)}, u32[]{:S(2)}) %all-to-all-start) | async-done | bytes 65568 | tf_op jit(solution)/shard_map/all_to_all | solution.py:494
  19.8 0.0 copy-done.3
  19.8 0.0 copy-done.4
  19.8 0.0 copy-done.5
  19.8 0.0 copy-done.6
  19.8 0.0 copy-done.7
  19.9 1.6 %finish.1 = (f32[4,256,256]{2,1,0:T(8,128)}, f32[2,128,128]{2,1,0:T(8,128)}) custom-call(f32[128,128]{1,0:T(8,128)S(1)} %bitcast.1, f32[2,32,128]{2,1,0:T(8,128)S(1)} %copy-done.7, f32[4,32,128]{2,1,0:T(8,128)S(1)} %copy-done.6, f32[4,32,128]{2,1,0:T(8,128)S(1)} %copy-done.5, f32[2,16,256]{2,1,0:T(8,128)S(1)} %copy-done.4, f32[4,16,256]{2,1,0:T(8,128)S(1)} %copy-done.3, ...), custom_call_target="tpu_custom_call" | custom-call | flops 1 | bytes 1 | tf_op jit(solution)/shard_map/finish/pallas_call | solution.py:517
Async XLA Ops:
  0.6 13.9 %copy-start = (f32[4,256,256]{2,1,0:T(8,128)S(1)}, f32[4,256,256]{2,1,0:T(8,128)}, u32[]{:S(2)}) copy-start(f32[4,256,256]{2,1,0:T(8,128)} %field.1) | copy-start | bytes 3145732
  0.6 13.8 %copy-start.2 = (f32[256,128]{1,0:T(8,128)S(1)}, f32[256,128]{1,0:T(8,128)}, u32[]{:S(2)}) copy-start(f32[256,128]{1,0:T(8,128)} %constant.40.clone.up_x) | copy-start | bytes 393220
  4.8 9.7 %copy-start.1 = (f32[128,256]{1,0:T(8,128)S(1)}, f32[128,256]{1,0:T(8,128)}, u32[]{:S(2)}) copy-start(f32[128,256]{1,0:T(8,128)} %constant.41.clone.up_y) | copy-start | bytes 393220
  4.8 12.5 %collective-permute-start.2 = (f32[2,128,128]{2,1,0:T(8,128)S(1)}, f32[2,128,128]{2,1,0:T(8,128)S(1)}, u32[]{:S(2)}, u32[]{:S(2)}) collective-permute-start(f32[2,128,128]{2,1,0:T(8,128)S(1)} %get-tuple-element.20), channel_id=1, source_target_pairs={{0,3},{1,2},{2,1},{3,0},{4,7},{5,6},{6,5},{7,4},{8,11},{9,10},{10,... | collective-permute-start | bytes 393224 | tf_op jit(solution)/shard_map/ppermute | solution.py:498
  7.2 12.6 %all-to-all-start = ((f32[32,4,128]{2,1,0:T(4,128)}), f32[32,4,128]{2,1,0:T(4,128)S(1)}, u32[]{:S(2)}, u32[]{:S(2)}) async-start(f32[32,4,128]{2,1,0:T(4,128)} %get-tuple-element.13), calls=%async_computation | async-start | bytes 131072 | tf_op jit(solution)/shard_map/all_to_all | solution.py:494
  12.4 2.6 %collective-permute-start = (f32[128,128]{1,0:T(8,128)S(1)}, f32[128,128]{1,0:T(8,128)S(1)}, u32[]{:S(2)}, u32[]{:S(2)}) collective-permute-start(f32[128,128]{1,0:T(8,128)S(1)} %get-tuple-element.18), channel_id=1, source_target_pairs={{0,1},{1,0},{2,3},{3,2},{4,5},{5,4},{6,7},{7,6},{8,9},{9,8},{10,11... | collective-permute-start | bytes 196616 | tf_op jit(solution)/shard_map/ppermute | solution.py:498
  12.7 4.6 %collective-permute-start.1 = (f32[128,128]{1,0:T(8,128)S(1)}, f32[128,128]{1,0:T(8,128)S(1)}, u32[]{:S(2)}, u32[]{:S(2)}) collective-permute-start(f32[128,128]{1,0:T(8,128)S(1)} %get-tuple-element.19), channel_id=1, source_target_pairs={{0,2},{1,3},{2,0},{3,1},{4,6},{5,7},{6,4},{7,5},{8,10},{9,11},{10,... | collective-permute-start | bytes 196616 | tf_op jit(solution)/shard_map/ppermute | solution.py:498
  14.4 2.9 %collective-permute-start.3 = (f32[128,128]{1,0:T(8,128)S(1)}, f32[128,128]{1,0:T(8,128)S(1)}, u32[]{:S(2)}, u32[]{:S(2)}) collective-permute-start(f32[128,128]{1,0:T(8,128)S(1)} %get-tuple-element.21), channel_id=1, source_target_pairs={{0,1},{1,0},{2,3},{3,2},{4,5},{5,4},{6,7},{7,6},{8,9},{9,8},{10,11... | collective-permute-start | bytes 196616 | tf_op jit(solution)/shard_map/ppermute | solution.py:498
  14.5 2.8 %copy-start.8 = (f32[8,128]{1,0:T(8,128)S(1)}, f32[8,128]{1,0:T(8,128)}, u32[]{:S(2)}) copy-start(f32[8,128]{1,0:T(8,128)} %constant.30.clone.refs_0_.scalars) | copy-start | bytes 12292
  17.3 2.5 %copy-start.3 = (f32[4,16,256]{2,1,0:T(8,128)S(1)}, f32[4,16,256]{2,1,0:T(8,128)}, u32[]{:S(2)}) copy-start(f32[4,16,256]{2,1,0:T(8,128)} %constant.34.clone.refs_5_.row_y) | copy-start | bytes 196612
  17.3 2.5 %copy-start.4 = (f32[2,16,256]{2,1,0:T(8,128)S(1)}, f32[2,16,256]{2,1,0:T(8,128)}, u32[]{:S(2)}) copy-start(f32[2,16,256]{2,1,0:T(8,128)} %constant.35.clone.refs_6_.row_x) | copy-start | bytes 98308
  17.3 2.5 %copy-start.5 = (f32[4,32,128]{2,1,0:T(8,128)S(1)}, f32[4,32,128]{2,1,0:T(8,128)}, u32[]{:S(2)}) copy-start(f32[4,32,128]{2,1,0:T(8,128)} %constant.44.clone.wz) | copy-start | bytes 196612
  17.4 2.5 %copy-start.6 = (f32[4,32,128]{2,1,0:T(8,128)S(1)}, f32[4,32,128]{2,1,0:T(8,128)}, u32[]{:S(2)}) copy-start(f32[4,32,128]{2,1,0:T(8,128)} %constant.43.clone.wy) | copy-start | bytes 196612
  17.4 2.5 %copy-start.7 = (f32[2,32,128]{2,1,0:T(8,128)S(1)}, f32[2,32,128]{2,1,0:T(8,128)}, u32[]{:S(2)}) copy-start(f32[2,32,128]{2,1,0:T(8,128)} %constant.42.clone.wx) | copy-start | bytes 98308

commit v4 on v3

--- a/solution.py
+++ b/solution.py
@@ -85,14 +85,6 @@
     return pick
 
 
-def lift_matrix(m):
-    up = np.zeros((2 * m, m + 1))
-    up[2 * np.arange(m), np.arange(m)] = 1.0
-    up[2 * np.arange(m) + 1, np.arange(m)] = 0.5
-    up[2 * np.arange(m) + 1, np.arange(m) + 1] = 0.5
-    return up
-
-
 def f32(values):
     return np.asarray(values, np.float32)
 
@@ -152,15 +144,15 @@
     return one_pass(a[0], b[0], contract) + one_pass(a[0], b[1], contract) + one_pass(a[1], b[0], contract)
 
 
+def two_pass(a, b):
+    return one_pass(a[0], b) + one_pass(a[1], b)
+
+
 def exact_left(a, b):
     high, low = split(b)
     return one_pass(a, high) + one_pass(a, low)
 
 
-def split_exact(values):
-    return values.astype(jnp.bfloat16)
-
-
 def exact_right(a, b):
     high, low = split(a)
     return one_pass(high, b) + one_pass(low, b)
@@ -172,53 +164,58 @@
 
 
 def local_kernel(sizes, *refs):
-    numbers, field, sum_x, sum_y, fold_z, row_y, row_x, line_y, line_x, block_x, pick = refs[:11]
-    send, own, even, near, far, first, both_far = refs[11:18]
-    f, ax, ay, az, vy, vx, ry, rx, bx, sel, kinds, scalars, sem = refs[18:]
+    numbers, field, fold_z, line_y, line_x = refs[:5]
+    send, own, even, near, far, first, both_far, f = refs[5:13]
+    ry, bx, az, picked, column, kinds, scalars, sem = refs[13:]
     gx, gy, gz = sizes
     px, py, pz = lax.axis_index("gx"), lax.axis_index("gy"), lax.axis_index("gz")
-    depth, height, _ = field.shape
+    depth, height, breadth = field.shape
     mz, mx, my = own.shape
-    planes = []
-    for z in range(depth):
-        halves = [
-            pltpu.make_async_copy(field.at[z, :, pl.ds(h * my, my)], f.at[h, z], sem.at[2 * z + h]) for h in range(2)
-        ]
-        planes.append(halves)
-    sources = [(line_y.at[py], ry), (sum_y.at[py], ay), (fold_z.at[pz], az), (sum_x.at[px], ax), (numbers, scalars)]
-    sources += [(row_y.at[py], vy), (row_x.at[px], vx), (block_x.at[px], bx), (pick, sel), (line_x.at[px], rx)]
-    tables = [pltpu.make_async_copy(src, dst, sem.at[2 * depth + i]) for i, (src, dst) in enumerate(sources)]
-    start_all(tables[:3] + planes[0] + planes[1] + tables[3:] + planes[2] + planes[3])
-    for table in tables[:3]:
+    planes = [pltpu.make_async_copy(field.at[z], f.at[z], sem.at[z]) for z in range(depth)]
+    sources = [(fold_z.at[pz], az), (line_y.at[py], ry), (line_x.at[px], bx), (numbers, scalars)]
+    tables = [pltpu.make_async_copy(src, dst, sem.at[depth + i]) for i, (src, dst) in enumerate(sources)]
+    start_all(tables[:2] + planes + tables[2:])
+    kinds[...] = jnp.zeros_like(kinds)
+    fine = lax.broadcasted_iota(jnp.int32, (breadth, my), 0)
+    node = lax.broadcasted_iota(jnp.int32, (breadth, my), 1)
+    pick_y = jnp.where(fine == 2 * node, 1.0, 0.0).astype(jnp.bfloat16)
+    tables[0].wait()
+    tables[1].wait()
+    weights = split(ry[:breadth])
+    by_y, evens, along_x = [], [], None
+    step = 2
+    for start in range(0, depth, step):
+        for z in range(start, start + step):
+            planes[z].wait()
+        part = split(f[start : start + step].reshape(step * height, breadth))
+        result = three_pass(part, weights)
+        for z in range(start, start + step):
+            rows = slice((z - start) * height, (z - start + 1) * height)
+            by_y.append(result[rows, :my])
+            folded = result[rows, my:] * az[z : z + 1, :]
+            along_x = folded if along_x is None else along_x + folded
+            if z % 2 == 0:
+                j = z // 2
+                picked[j] = two_pass((part[0][rows], part[1][rows]), pick_y)
+                evens.append(picked[j, pl.ds(0, mx, stride=2), :])
+                even[j] = evens[j]
+    column[...] = along_x
+    edge = jnp.transpose(column[pl.ds(0, mx, stride=2), :])[:16, :]
+    for table in tables[2:]:
         table.wait()
-    kinds[...] = jnp.zeros_like(kinds)
-    solve_y = split(ry[...])
-    by_y, along_x = [], None
-    for z in range(depth):
-        sum_z = split(ay[...] * az[z : z + 1, :])
-        weights = tuple(jnp.concatenate([a, b], axis=1) for a, b in zip(solve_y, sum_z, strict=True))
-        for half in planes[z]:
-            half.wait()
-        both = three_pass(split(jnp.concatenate([f[0, z], f[1, z]], axis=1)), weights)
-        by_y.append(both[:, :my])
-        along_x = both[:, my:] if along_x is None else along_x + both[:, my:]
-    for table in tables[3:]:
-        table.wait()
-
-    by_x = three_pass(split(jnp.transpose(along_x)[:16, :]), split(rx[...]))
-    sums = [[jnp.sum(by_y[z] * ax[ab], axis=0, keepdims=True) for ab in range(2)] for z in range(depth)]
-    corners = [jnp.sum(along_x * ax[ab], axis=0, keepdims=True) for ab in range(2)]
-    pick_y = split_exact(sel[...])
-    evens = []
-    for j in range(mz):
-        rows = jnp.concatenate([f[h, 2 * j, pl.ds(0, mx, stride=2), :] for h in range(2)], axis=1)
-        evens.append(exact_right(rows, pick_y))
-        even[j] = evens[j]
-    first_y, first_x = vy[8:9, :my], vx[8:9, :mx]
+    solve_x = split(bx[: mx + 8])
+    faces = three_pass(solve_x, split(along_x))
+    by_x = jnp.transpose(faces[:mx])[:16, :]
+    corners = [faces[mx + ab : mx + ab + 1] for ab in range(2)]
+    by_split = split(jnp.concatenate(by_y, axis=1))
+    ends_x = three_pass(tuple(half[mx:] for half in solve_x), by_split)
+    sums = [[ends_x[ab : ab + 1, z * my : (z + 1) * my] for ab in range(2)] for z in range(depth)]
+
+    first_y, first_x = ry[breadth : breadth + 1, :my], bx[mx + 8 : mx + 9, :mx]
     kappa_x, kappa_y = scalars[gz, px], scalars[gz + 1, py]
     ends = 2 * (mz + 2)
     first_rows = [evens[j][0:1, :] for j in range(mz)]
-    first_cols = [by_x[ends + j : ends + j + 1, mx:] for j in range(mz)]
+    first_cols = [edge[ends + j : ends + j + 1, :] for j in range(mz)]
     for out in range(mz + 2):
         base = (mz + 2) * depth + out * mz
         first_row = sum(scalars[pz, base + j] * first_rows[j] for j in range(mz))
@@ -230,8 +227,8 @@
         chunks = {
             (1, 0): right_row - kappa_x * (first_row - first_y * corner),
             (2, 0): left_row,
-            (0, 1): by_x[r, :mx] - kappa_y * (first_col - first_x * corner),
-            (0, 2): by_x[l, :mx],
+            (0, 1): by_x[r] - kappa_y * (first_col - first_x * corner),
+            (0, 2): by_x[l],
             (1, 1): spread + (corners[0][:, r] - kappa_x * kappa_y * corner),
             (1, 2): spread + corners[0][:, l],
             (2, 1): spread + corners[1][:, r],
@@ -264,8 +261,8 @@
         def _(at):
             scatter(at // (gy * gz), (at // gz) % gy, at % gz, at)
 
-    solve_x = split(bx[...])
-    solved = [three_pass(solve_x, split(by_y[z])) for z in range(depth)]
+    by_all = three_pass(tuple(half[:mx] for half in solve_x), by_split)
+    solved = [by_all[:, z * my : (z + 1) * my] for z in range(depth)]
     first_x = jnp.transpose(jnp.broadcast_to(first_x, (8, mx)))[:, 0:1]
     outs = []
     for out in range(mz + 2):
@@ -284,75 +281,71 @@
     first[...] = evens[0]
 
 
-def inner_kernel(field, even, up_x, up_y, c, top):
-    depth = field.shape[0]
+def inner_kernel(field, even, *refs):
+    tables, (coefficients, c, top, rows, weights, up_x, up_y), (parts, sem) = refs[:6], refs[6:13], refs[13:]
+    px, py, pz = lax.axis_index("gx"), lax.axis_index("gy"), lax.axis_index("gz")
+    depth, height, breadth = field.shape
     mz = even.shape[0]
-    up_x, up_y = up_x[...].astype(jnp.bfloat16), up_y[...].astype(jnp.bfloat16)
-    lifted = [exact_right(exact_left(up_x, even[j]), up_y) for j in range(mz)]
+    goals = (rows.at[0:8], rows.at[8:16], rows.at[16:32], parts.at[0], parts.at[1], parts.at[2])
+    fetches = [
+        pltpu.make_async_copy(table.at[at], goal, sem.at[depth + i])
+        for i, (table, at, goal) in enumerate(zip(tables, (px, py, pz) * 2, goals, strict=True))
+    ]
+    start_all(fetches)
+    for up, node_axis in ((up_x, 1), (up_y, 0)):
+        node = lax.broadcasted_iota(jnp.int32, up.shape, node_axis)
+        away = jnp.abs(lax.broadcasted_iota(jnp.int32, up.shape, 1 - node_axis) - 2 * node)
+        up[...] = jnp.where(away == 0, 1.0, jnp.where(away == 1, 0.5, 0.0))
+    body = (pl.ds(0, height - 8), pl.ds(0, breadth - 128))
+    up_left, up_right = up_x[...].astype(jnp.bfloat16), up_y[...].astype(jnp.bfloat16)
+    lifted = [exact_right(exact_left(up_left, even[j]), up_right) for j in range(mz)]
+    copies = []
     for z in range(depth - 1):
         j = z // 2
         c[z] = field[z] - (lifted[j] if z % 2 == 0 else 0.5 * (lifted[j] + lifted[j + 1]))
+        copies.append(pltpu.make_async_copy(c.at[z, *body], coefficients.at[z, *body], sem.at[z]))
+        copies[z].start()
     top[...] = field[depth - 1] - 0.5 * lifted[mz - 1]
-
-
-def upper_kernel(scalars, top, own, up_x, up_y, one, two, three, first, last, coarse):
-    gz = lax.axis_size("gz")
-    pz = lax.axis_index("gz")
-    mz = own.shape[0]
-    base = (mz + 2) * (2 * mz + mz)
-    left, right = jnp.zeros(own.shape[1:], jnp.float32), jnp.zeros(own.shape[1:], jnp.float32)
-    for plane, hop in ((one[...], 1), (two[...], 2), (three[0], 3)):
-        left = left + scalars[pz, base + (pz ^ hop)] * plane
-        right = right + scalars[pz, base + gz + (pz ^ hop)] * plane
-    ahead = jnp.where(pz ^ 1 == pz + 1, 1.0, 0.0) * first[...]
-    ahead = ahead + jnp.where(pz ^ 3 == pz + 1, 1.0, 0.0) * three[1]
-    up_x, up_y = up_x[...].astype(jnp.bfloat16), up_y[...].astype(jnp.bfloat16)
-    last[...] = top[...] - 0.5 * exact_right(exact_left(up_x, ahead), up_y)
-    base = base + 2 * gz
-    for j in range(mz):
-        coarse[j] = own[j] + scalars[pz, base + j] * left + scalars[pz, base + mz + j] * right
-
-
-def finish_kernel(
-    sizes,
-    received,
-    wx,
-    wy,
-    wz,
-    row_x,
-    row_y,
-    up_x,
-    up_y,
-    inner,
-    top,
-    before,
-    coefficients,
-    coarse,
-    rim,
-    foot,
-    values,
-    sem,
-):
-    px, py, pz = lax.axis_index("gx"), lax.axis_index("gy"), lax.axis_index("gz")
-    mz, mx, my = before.shape
+    for copy in fetches:
+        copy.wait()
+    weights[...] = parts[0] * parts[1] * parts[2]
+    for copy in copies:
+        copy.wait()
+
+
+def gather_kernel(received, weights, got):
+    got[...] = three_pass(split(weights[...]), split(received[...]))
+
+
+def finish_kernel(*refs):
+    got, rows, up_x, up_y, inner, top, own, one, two, three, first, partial = refs[:12]
+    coefficients, coarse, last_plane, rim, foot, values, sem = refs[12:]
+    del partial
+    mz, mx, my = own.shape
     depth, height, breadth = 2 * mz, 2 * mx, 2 * my
     split_at = breadth - 128
     body = (pl.ds(0, height - 8), pl.ds(0, split_at))
-    copies = [
-        pltpu.make_async_copy(inner.at[:, *body], coefficients.at[pl.ds(0, depth - 1), *body], sem.at[0]),
-        pltpu.make_async_copy(top.at[body], coefficients.at[depth - 1, *body], sem.at[1]),
-    ]
-    start_all(copies)
-    weights = wx[px] * wy[py] * wz[pz]
-    got = three_pass(split(weights), split(received[...]))
+
+    def row_at(i):
+        return rows[16 + i : 17 + i, :]
+
+    planes = (one[...], two[...], three[0])
+    left = sum(row_at(i) * plane for i, plane in enumerate(planes))
+    right = sum(row_at(3 + i) * plane for i, plane in enumerate(planes))
+    ahead = row_at(6) * first[...] + row_at(7) * three[1]
+    up_left, up_right = up_x[...].astype(jnp.bfloat16), up_y[...].astype(jnp.bfloat16)
+    last_plane[...] = top[...] - 0.5 * exact_right(exact_left(up_left, ahead), up_right)
+    copies = [pltpu.make_async_copy(last_plane.at[body], coefficients.at[depth - 1, *body], sem.at[0])]
+    copies[0].start()
+    before = [own[j] + row_at(8 + j) * left + row_at(8 + mz + j) * right for j in range(mz)]
 
     base = 9 * mz
     layers = mz + 1
     halo_x, halo_y, halo_xy = (got[base + i * layers : base + (i + 1) * layers] for i in range(3))
     pad = jnp.zeros((8 - layers, halo_x.shape[1]), jnp.float32)
-    row = exact_right(jnp.concatenate([halo_x, pad], axis=0), up_y[...].astype(jnp.bfloat16))
+    row = exact_right(jnp.concatenate([halo_x, pad], axis=0), up_right)
     tall = jnp.concatenate([halo_y, jnp.zeros((128 - layers, halo_y.shape[1]), jnp.float32)], axis=0)
-    col = exact_left(up_x[...].astype(jnp.bfloat16), jnp.transpose(tall))
+    col = exact_left(up_left, jnp.transpose(tall))
     lane = lax.broadcasted_iota(jnp.int32, (1, 128), 1)
     last = lane == 127
     for z in range(depth):
@@ -363,18 +356,19 @@
             r = 0.5 * (row[j : j + 1] + row[j + 1 : j + 2])
             s = 0.25 * (col[:, j : j + 1] + col[:, j + 1 : j + 2])
             k = 0.5 * (halo_xy[j : j + 1, 0:1] + halo_xy[j + 1 : j + 2, 0:1])
-        old = inner[z] if z < depth - 1 else top[...]
+        old = inner[z] if z < depth - 1 else last_plane[...]
         rim[z] = old[:, split_at:] - jnp.where(last, s, 0.0)
         end = 0.5 * r[:, split_at:] + jnp.where(last, 0.25 * k, 0.0)
         rim[z, height - 1 : height, :] = rim[z, height - 1 : height, :] - end
         foot[z] = old[height - 8 :, :split_at]
         foot[z, 7:8, :] = old[height - 1 :, :split_at] - 0.5 * r[:, :split_at]
-    copies.append(pltpu.make_async_copy(rim, coefficients.at[:, :, pl.ds(split_at, 128)], sem.at[2]))
-    copies.append(pltpu.make_async_copy(foot, coefficients.at[:, pl.ds(height - 8, 8), pl.ds(0, split_at)], sem.at[3]))
-    start_all(copies[2:])
-
-    ux, vx = row_x[px, 9:10, :mx], row_x[px, 10:11, :mx]
-    uy, vy = row_y[py, 9:10, :my], row_y[py, 10:11, :my]
+        goal = coefficients.at[z, :, pl.ds(split_at, 128)]
+        copies.append(pltpu.make_async_copy(rim.at[z], goal, sem.at[3 + 2 * z]))
+        goal = coefficients.at[z, pl.ds(height - 8, 8), pl.ds(0, split_at)]
+        copies.append(pltpu.make_async_copy(foot.at[z], goal, sem.at[4 + 2 * z]))
+        start_all(copies[-2:])
+
+    ux, vx, uy, vy = rows[0:1], rows[1:2], rows[8:9], rows[9:10]
 
     def part(sx, sy, z):
         at = (sx * 3 + sy) * mz + z
@@ -391,8 +385,8 @@
         zero = [jnp.zeros((4, mx), jnp.float32)]
         a, b = split(jnp.concatenate(a + zero, axis=0)), split(jnp.concatenate(b + zero, axis=0))
         values[z] = before[z] + three_pass(a, b, ((0,), (0,)))
-    copies.append(pltpu.make_async_copy(values, coarse, sem.at[4]))
-    copies[4].start()
+    copies.append(pltpu.make_async_copy(values, coarse, sem.at[2]))
+    copies[-1].start()
     for copy in copies:
         copy.wait()
 
@@ -417,6 +411,10 @@
 VMEM = pl.BlockSpec(memory_space=pltpu.VMEM)
 
 
+def in_hbm(values):
+    return pltpu.with_memory_space_constraint(jnp.asarray(values), pltpu.HBM)
+
+
 def shape(*dims):
     return jax.ShapeDtypeStruct(dims, jnp.float32)
 
@@ -429,25 +427,21 @@
     axes = ("gx", "gy", "gz")
     tx, ty, tz = line_tables(gx, mx), line_tables(gy, my), line_tables(gz, mz)
 
-    def rows(t, parts, m):
-        table = np.zeros((parts, 16, 2 * m))
-        table[:, 0], table[:, 1] = t["to_right"], t["to_left"]
-        table[:, 8, :m], table[:, 9, :m], table[:, 10, :m] = t["first"], t["from_left"], t["from_right"]
+    def vectors(t, parts, m):
+        table = np.zeros((parts, 8, m))
+        table[:, 0], table[:, 1] = t["from_left"], t["from_right"]
         return f32(table)
 
-    def right_side(t, parts, m):
-        table = np.zeros((parts, 2 * m, 2 * m))
-        table[:, :, :m] = t["block"].transpose(0, 2, 1)
-        table[:, :, m:] = even_selector(m)
-        return f32(table)
-
-    row_x, row_y = rows(tx, gx, mx), rows(ty, gy, my)
-    right_x, right_y = right_side(tx, gx, mx), f32(ty["block"].transpose(0, 2, 1))
-    sum_x = f32(np.repeat(np.stack([tx["to_right"], tx["to_left"]], axis=1)[..., None], 128, axis=3))
-    sum_y, fold_z = np.zeros((gy, breadth, 128)), np.zeros((gz, 8, 128))
+    row_x, row_y = vectors(tx, gx, mx), vectors(ty, gy, my)
+    line_y, line_x = np.zeros((gy, breadth + 8, 2 * my)), np.zeros((gx, mx + 16, height))
+    line_y[:, :breadth, :my] = ty["block"].transpose(0, 2, 1)
     for out in range(mz + 2):
-        sum_y[:, :, 2 * out], sum_y[:, :, 2 * out + 1] = ty["to_right"], ty["to_left"]
-    sum_y[:, 0, 2 * (mz + 2) : 2 * (mz + 2) + mz] = 1.0
+        line_y[:, :breadth, my + 2 * out], line_y[:, :breadth, my + 2 * out + 1] = ty["to_right"], ty["to_left"]
+    line_y[:, 0, my + 2 * (mz + 2) : my + 2 * (mz + 2) + mz] = 1.0
+    line_y[:, breadth, :my] = ty["first"]
+    line_x[:, :mx], line_x[:, mx], line_x[:, mx + 1] = tx["block"], tx["to_right"], tx["to_left"]
+    line_x[:, mx + 8, :mx] = tx["first"]
+    fold_z = np.zeros((gz, 8, 128))
 
     width = max((mz + 2) * (depth + mz) + 2 * gz + 2 * mz, gx, gy)
     scalars = np.zeros((8 * ((gz + 2 + 7) // 8), 128 * ((width + 127) // 128)))
@@ -467,66 +461,72 @@
     scalars = f32(scalars)
 
     vmem = pltpu.VMEM
-    operands = (scalars, field, sum_x, f32(sum_y), f32(fold_z), row_y, row_x, right_y, right_x, f32(tx["block"]))
-    operands += (f32(even_selector(my)),)
-    send, own, even, near, far, first, both_far = call(
+    operands = (scalars, field, f32(fold_z), f32(line_y), f32(line_x))
+    send, own, even, near, far, first, both_far, kept = call(
         functools.partial(local_kernel, sizes),
         "local",
-        [shape(count, 4, my), shape(mz, mx, my), shape(mz, mx, my)] + [shape(mx, my)] * 3 + [shape(2, mx, my)],
-        [HBM] * 11,
-        [VMEM] * 7,
+        [shape(count, 4, my), shape(mz, mx, my), shape(mz, mx, my)] + [shape(mx, my)] * 3 + [shape(2, mx, my), shape(*field.shape)],
+        [HBM] * 5,
+        [VMEM] * 8,
         [
-            vmem((2, depth, height, my), jnp.float32),
-            vmem(sum_x.shape[1:], jnp.float32),
-            vmem(sum_y.shape[1:], jnp.float32),
+            vmem(line_y.shape[1:], jnp.float32),
+            vmem(line_x.shape[1:], jnp.float32),
             vmem(fold_z.shape[1:], jnp.float32),
-            vmem(row_y.shape[1:], jnp.float32),
-            vmem(row_x.shape[1:], jnp.float32),
-            vmem(right_y.shape[1:], jnp.float32),
-            vmem(right_x.shape[1:], jnp.float32),
-            vmem((mx, height), jnp.float32),
-            vmem((breadth, my), jnp.float32),
+            vmem((mz, height, my), jnp.float32),
+            vmem((height, 128), jnp.float32),
             vmem((27, 4, my), jnp.float32),
             pltpu.SMEM(scalars.shape, jnp.float32),
-            pltpu.SemaphoreType.DMA((2 * depth + 10,)),
+            pltpu.SemaphoreType.DMA((depth + 4,)),
         ],
-    )(*(pltpu.with_memory_space_constraint(jnp.asarray(value), pltpu.HBM) for value in operands))
+    )(*map(in_hbm, operands))
     received = lax.all_to_all(send, axes, 0, 0, tiled=True).reshape(count * 4, my)
 
     assert gz == 4
     plans = ((near, 1), (far, 2), (both_far, 3), (first, 1))
     gets = [lax.ppermute(plane, "gz", [(i, i ^ hop) for i in range(gz)]) for plane, hop in plans]
 
-    up_x, up_y = f32(lift_matrix(mx)[:, :mx]), f32(lift_matrix(my)[:, :my].T)
-    inner, top = call(
+    row_z = np.zeros((gz, 16, my))
+    for p in range(gz):
+        for i, hop in enumerate((1, 2, 3)):
+            row_z[p, i], row_z[p, 3 + i] = tz["weight_left"][p, p ^ hop], tz["weight_right"][p, p ^ hop]
+        row_z[p, 6], row_z[p, 7] = p ^ 1 == p + 1, p ^ 3 == p + 1
+        row_z[p, 8 : 8 + mz] = tz["from_left"][p][:, None]
+        row_z[p, 8 + mz : 8 + 2 * mz] = tz["from_right"][p][:, None]
+    wx, wy, wz = combine_tables(sizes, tx, ty, tz, mz)
+    tables = (row_x, row_y, f32(row_z), wx, wy, wz)
+    partial, inner, top, rows, weights, up_x, up_y = call(
         inner_kernel,
         "inner",
-        [shape(depth - 1, height, breadth), shape(height, breadth)],
-        [VMEM] * 4,
+        [shape(*field.shape), shape(depth - 1, height, breadth), shape(height, breadth), shape(32, my)]
+        + [shape(*wx.shape[1:]), shape(height, mx), shape(my, breadth)],
+        [VMEM] * 2 + [HBM] * len(tables),
+        [HBM] + [VMEM] * 6,
+        [vmem((3, *wx.shape[1:]), jnp.float32), pltpu.SemaphoreType.DMA((depth + len(tables),))],
+    )(kept, even, *map(in_hbm, tables))
+    got = call(
+        gather_kernel,
+        "gather",
+        shape(wx.shape[1], my),
         [VMEM] * 2,
-    )(field, even, up_x, up_y)
-    last, before = call(
-        upper_kernel,
-        "upper",
-        [shape(height, breadth), shape(mz, mx, my)],
-        [SMEM] + [VMEM] * 8,
-        [VMEM] * 2,
-    )(scalars, top, own, up_x, up_y, *gets)
-
-    wx, wy, wz = combine_tables(sizes, tx, ty, tz, mz)
+        VMEM,
+        flops=10**10,
+        size=10**8,
+    )(received, weights)
     return call(
-        functools.partial(finish_kernel, sizes),
+        finish_kernel,
         "finish",
         [shape(*field.shape), shape(mz, mx, my)],
-        [VMEM] * 11,
+        [VMEM] * 11 + [HBM],
         [HBM, HBM],
         [
+            vmem((height, breadth), jnp.float32),
             vmem((depth, height, 128), jnp.float32),
             vmem((depth, 8, breadth - 128), jnp.float32),
             vmem((mz, mx, my), jnp.float32),
-            pltpu.SemaphoreType.DMA((5,)),
+            pltpu.SemaphoreType.DMA((3 + 2 * depth,)),
         ],
-    )(received, wx, wy, wz, row_x, row_y, up_x, up_y, inner, last, before)
+        {11: 0},
+    )(got, rows, up_x, up_y, inner, top, own, *gets, partial)
 
 
 def solution(mesh):

time: 21.7 us -> 20.9 us (0.963)
  Pallas kernels: 7.29 us -> 6.39 us
    all_to_all x1, waiting for transfers between devices: 1.36 us -> 3.76 us  [on_device(): lax.all_to_all(send, axes, 0, 0, tiled=True).reshape(count * 4, my)]
    ppermute x4, waiting for transfers between devices: 2.29 us -> 0.09 us  [on_device(): lax.ppermute(plane, 'gz', [(i, i ^ hop) for i in range(gz)])]
    all_to_all x1, starting transfers between devices: 5.18 us -> 7.3 us  [on_device(): lax.all_to_all(send, axes, 0, 0, tiled=True).reshape(count * 4, my)]
    ppermute x4, starting transfers between devices: 4.53 us -> 2.46 us  [on_device(): lax.ppermute(plane, 'gz', [(i, i ^ hop) for i in range(gz)])]
    pallas_call x1, Pallas kernels: 4.09 us -> 3.49 us  [on_device(): call(functools.partial(local_kernel, sizes), 'local', [shape(count, 4, my...]
    pallas_call x3, Pallas kernels: 3.19 us -> 2.9 us  [the longest x1 1.48 us: on_device(): call(finish_kernel, 'finish', [shape(*field.shape), shape(mz, mx, my)], [...]
where the time goes in v4:
time: 20.9 us; the launch traced here: 20.7 us
  starting transfers between devices  9.76 us (47%)
  Pallas kernels  6.39 us (31%)
  waiting for transfers between devices  3.85 us (18%)
  between operations  0.67 us (3%)
    all_to_all x1, starting transfers between devices, on_device(): lax.all_to_all(send, axes, 0, 0, tiled=True).reshape(count * 4, my)  7.3 us
    all_to_all x1, waiting for transfers between devices, on_device(): lax.all_to_all(send, axes, 0, 0, tiled=True).reshape(count * 4, my)  3.76 us
    pallas_call x1, Pallas kernels, on_device(): call(functools.partial(local_kernel, sizes), 'local', [shape(count, 4, my...  3.49 us
    ppermute x4, starting transfers between devices, on_device(): lax.ppermute(plane, 'gz', [(i, i ^ hop) for i in range(gz)])  2.46 us
    pallas_call x1, Pallas kernels, on_device(): call(finish_kernel, 'finish', [shape(*field.shape), shape(mz, mx, my)], [...  1.48 us
    pallas_call x1, Pallas kernels, on_device(): call(inner_kernel, 'inner', [shape(*field.shape), shape(depth - 1, height...  1.29 us
  transfers between devices with their start and end apart: 5, of which 2 were waited for; matrix products, arithmetic and copies ran while one was open for 0% of the time, Pallas kernels for 7%

profile of v4, /device:TPU:0, one launch (start us, length us, event | category | flops | bytes accessed | tf_op | source)
XLA Modules:
  0.0 20.7 jit_solution(13042676564687336414)
XLA Ops:
  0.6 3.5 %local.1 = (f32[32,4,128]{2,1,0:T(4,128)}, f32[2,128,128]{2,1,0:T(8,128)S(1)}, f32[2,128,128]{2,1,0:T(8,128)S(1)}, f32[128,128]{1,0:T(8,128)S(1)}, f32[128,128]{...) custom-call(f32[8,128]{1,0:T(8,128)} %constant.20.clone.refs_0_, ...), custom_call_target="tpu_custom_call" | custom-call | flops 1 | bytes 1 | tf_op jit(solution)/shard_map/local/pallas_call | solution.py:465
  4.1 7.3 %all-to-all-start = ((f32[32,4,128]{2,1,0:T(4,128)}), f32[32,4,128]{2,1,0:T(4,128)S(1)}, u32[]{:S(2)}, u32[]{:S(2)}) async-start(f32[32,4,128]{2,1,0:T(4,128)} %get-tuple-element.17), calls=%async_computation | async-start | bytes 131072 | tf_op jit(solution)/shard_map/all_to_all | solution.py:482
  11.4 0.3 %collective-permute-start = (f32[128,128]{1,0:T(8,128)S(1)}, f32[128,128]{1,0:T(8,128)S(1)}, u32[]{:S(2)}, u32[]{:S(2)}) collective-permute-start(f32[128,128]{1,0:T(8,128)S(1)} %get-tuple-element.27), channel_id=1, source_target_pairs={{0,1},{1,0},{2,3},{3,2},{4,5},{5,4},{6,7},{7,6},{8,9},{9,8},{10,11... | collective-permute-start | bytes 196616 | tf_op jit(solution)/shard_map/ppermute | solution.py:486
  11.8 1.7 %collective-permute-start.1 = (f32[128,128]{1,0:T(8,128)S(1)}, f32[128,128]{1,0:T(8,128)S(1)}, u32[]{:S(2)}, u32[]{:S(2)}) collective-permute-start(f32[128,128]{1,0:T(8,128)S(1)} %get-tuple-element.28), channel_id=1, source_target_pairs={{0,2},{1,3},{2,0},{3,1},{4,6},{5,7},{6,4},{7,5},{8,10},{9,11},{10,... | collective-permute-start | bytes 196616 | tf_op jit(solution)/shard_map/ppermute | solution.py:486
  13.4 0.1 collective-permute-start.3
  13.5 0.4 %collective-permute-start.2 = (f32[2,128,128]{2,1,0:T(8,128)S(1)}, f32[2,128,128]{2,1,0:T(8,128)S(1)}, u32[]{:S(2)}, u32[]{:S(2)}) collective-permute-start(f32[2,128,128]{2,1,0:T(8,128)S(1)} %get-tuple-element.29), channel_id=1, source_target_pairs={{0,3},{1,2},{2,1},{3,0},{4,7},{5,6},{6,5},{7,4},{8,11},{9,10},{10,... | collective-permute-start | bytes 393224 | tf_op jit(solution)/shard_map/ppermute | solution.py:486
  13.9 1.3 %inner.1 = (f32[4,256,256]{2,1,0:T(8,128)}, f32[3,256,256]{2,1,0:T(8,128)S(1)}, f32[256,256]{1,0:T(8,128)S(1)}, f32[32,128]{1,0:T(8,128)S(1)}, f32[32,128]{1,0:T...) custom-call(f32[4,256,256]{2,1,0:T(8,128)S(1)} %get-tuple-element.18.field, ...), custom_call_target="tpu_custom_call" | custom-call | flops 1 | bytes 1 | tf_op jit(solution)/shard_map/inner/pallas_call | solution.py:497
  15.2 3.8 %all-to-all-done = f32[32,4,128]{2,1,0:T(4,128)S(1)} async-done(((f32[32,4,128]{2,1,0:T(4,128)}), f32[32,4,128]{2,1,0:T(4,128)S(1)}, u32[]{:S(2)}, u32[]{:S(2)}) %all-to-all-start) | async-done | bytes 65568 | tf_op jit(solution)/shard_map/all_to_all | solution.py:482
  19.0 0.1 gather.1.refs_0_
  19.1 0.0 collective-permute-done.refs_7_
  19.1 0.0 collective-permute-done.1.refs_8_
  19.1 0.0 collective-permute-done.3.refs_10_
  19.1 0.1 collective-permute-done.2.refs_9_
  19.2 1.5 %finish.1 = (f32[4,256,256]{2,1,0:T(8,128)}, f32[2,128,128]{2,1,0:T(8,128)}) custom-call(f32[32,128]{1,0:T(8,128)S(1)} %gather.1.refs_0_, f32[32,128]{1,0:T(8,128)S(1)} %get-tuple-element.21.refs_1_, f32[256,128]{1,0:T(8,128)S(1)} %get-tuple-element.22.refs_2_, f32[128,256]{1,0:T(8,128)S(1)} %get-tuple-element.23.refs_3_, ...), custom_call_target="tpu_custom_call", output_to_operand_aliasing={{0}: (11, {})} | custom-call | flops 1 | bytes 1 | tf_op jit(solution)/shard_map/finish/pallas_call | solution.py:515
Async XLA Ops:
  4.1 14.8 %all-to-all-start = ((f32[32,4,128]{2,1,0:T(4,128)}), f32[32,4,128]{2,1,0:T(4,128)S(1)}, u32[]{:S(2)}, u32[]{:S(2)}) async-start(f32[32,4,128]{2,1,0:T(4,128)} %get-tuple-element.17), calls=%async_computation | async-start | bytes 131072 | tf_op jit(solution)/shard_map/all_to_all | solution.py:482
  11.4 7.6 %collective-permute-start = (f32[128,128]{1,0:T(8,128)S(1)}, f32[128,128]{1,0:T(8,128)S(1)}, u32[]{:S(2)}, u32[]{:S(2)}) collective-permute-start(f32[128,128]{1,0:T(8,128)S(1)} %get-tuple-element.27), channel_id=1, source_target_pairs={{0,1},{1,0},{2,3},{3,2},{4,5},{5,4},{6,7},{7,6},{8,9},{9,8},{10,11... | collective-permute-start | bytes 196616 | tf_op jit(solution)/shard_map/ppermute | solution.py:486
  11.8 7.3 %collective-permute-start.1 = (f32[128,128]{1,0:T(8,128)S(1)}, f32[128,128]{1,0:T(8,128)S(1)}, u32[]{:S(2)}, u32[]{:S(2)}) collective-permute-start(f32[128,128]{1,0:T(8,128)S(1)} %get-tuple-element.28), channel_id=1, source_target_pairs={{0,2},{1,3},{2,0},{3,1},{4,6},{5,7},{6,4},{7,5},{8,10},{9,11},{10,... | collective-permute-start | bytes 196616 | tf_op jit(solution)/shard_map/ppermute | solution.py:486
  13.4 5.7 %collective-permute-start.3 = (f32[128,128]{1,0:T(8,128)S(1)}, f32[128,128]{1,0:T(8,128)S(1)}, u32[]{:S(2)}, u32[]{:S(2)}) collective-permute-start(f32[128,128]{1,0:T(8,128)S(1)} %get-tuple-element.30), channel_id=1, source_target_pairs={{0,1},{1,0},{2,3},{3,2},{4,5},{5,4},{6,7},{7,6},{8,9},{9,8},{10,11... | collective-permute-start | bytes 196616 | tf_op jit(solution)/shard_map/ppermute | solution.py:486
  13.5 5.7 %collective-permute-start.2 = (f32[2,128,128]{2,1,0:T(8,128)S(1)}, f32[2,128,128]{2,1,0:T(8,128)S(1)}, u32[]{:S(2)}, u32[]{:S(2)}) collective-permute-start(f32[2,128,128]{2,1,0:T(8,128)S(1)} %get-tuple-element.29), channel_id=1, source_target_pairs={{0,3},{1,2},{2,1},{3,0},{4,7},{5,6},{6,5},{7,4},{8,11},{9,10},{10,... | collective-permute-start | bytes 393224 | tf_op jit(solution)/shard_map/ppermute | solution.py:486

commit v5 on v4

--- a/solution.py
+++ b/solution.py
@@ -164,15 +164,15 @@
 
 
 def local_kernel(sizes, *refs):
-    numbers, field, fold_z, line_y, line_x = refs[:5]
-    send, own, even, near, far, first, both_far, f = refs[5:13]
-    ry, bx, az, picked, column, kinds, scalars, sem = refs[13:]
+    field, fold_z, line_y, line_x = refs[:4]
+    send, own, even, near, far, first, both_far, f = refs[4:12]
+    ry, bx, az, picked, column, kinds, sem = refs[12:]
     gx, gy, gz = sizes
     px, py, pz = lax.axis_index("gx"), lax.axis_index("gy"), lax.axis_index("gz")
     depth, height, breadth = field.shape
     mz, mx, my = own.shape
     planes = [pltpu.make_async_copy(field.at[z], f.at[z], sem.at[z]) for z in range(depth)]
-    sources = [(fold_z.at[pz], az), (line_y.at[py], ry), (line_x.at[px], bx), (numbers, scalars)]
+    sources = [(fold_z.at[pz], az), (line_y.at[py], ry), (line_x.at[px], bx)]
     tables = [pltpu.make_async_copy(src, dst, sem.at[depth + i]) for i, (src, dst) in enumerate(sources)]
     start_all(tables[:2] + planes + tables[2:])
     kinds[...] = jnp.zeros_like(kinds)
@@ -211,40 +211,41 @@
     ends_x = three_pass(tuple(half[mx:] for half in solve_x), by_split)
     sums = [[ends_x[ab : ab + 1, z * my : (z + 1) * my] for ab in range(2)] for z in range(depth)]
 
-    first_y, first_x = ry[breadth : breadth + 1, :my], bx[mx + 8 : mx + 9, :mx]
-    kappa_x, kappa_y = scalars[gz, px], scalars[gz + 1, py]
-    ends = 2 * (mz + 2)
-    first_rows = [evens[j][0:1, :] for j in range(mz)]
-    first_cols = [edge[ends + j : ends + j + 1, :] for j in range(mz)]
-    for out in range(mz + 2):
-        base = (mz + 2) * depth + out * mz
-        first_row = sum(scalars[pz, base + j] * first_rows[j] for j in range(mz))
-        first_col = sum(scalars[pz, base + j] * first_cols[j] for j in range(mz))
-        corner = first_row[:, 0:1]
-        right_row, left_row = (sum(scalars[pz, out * depth + z] * sums[z][ab] for z in range(depth)) for ab in range(2))
-        r, l = slice(2 * out, 2 * out + 1), slice(2 * out + 1, 2 * out + 2)
-        spread = jnp.zeros((1, my), jnp.float32)
-        chunks = {
-            (1, 0): right_row - kappa_x * (first_row - first_y * corner),
-            (2, 0): left_row,
-            (0, 1): by_x[r] - kappa_y * (first_col - first_x * corner),
-            (0, 2): by_x[l],
-            (1, 1): spread + (corners[0][:, r] - kappa_x * kappa_y * corner),
-            (1, 2): spread + corners[0][:, l],
-            (2, 1): spread + corners[1][:, r],
-            (2, 2): spread + corners[1][:, l],
-        }
-        for (sx, sy), row in chunks.items():
-            kind = (sx * 3 + sy) * 3
-            if out < mz:
-                kinds[kind, out : out + 1, :] = row
-            else:
-                kinds[kind + out - mz + 1, 0:1, :] = row
+    first_y, kappa_y = ry[breadth : breadth + 1, :my], ry[breadth + 1 : breadth + 2, :my]
+    first_x, kappa_x = bx[mx + 8 : mx + 9, :mx], bx[mx + 9 : mx + 10, :mx]
+    outs = mz + 2
+    first_rows = jnp.concatenate([evens[j][0:1, :] for j in range(mz)], axis=0)
+    first_cols = edge[2 * outs : 2 * outs + mz, :]
+
+    def over_z(base, rows):
+        return sum(az[base + 8 * j : base + 8 * j + 8, :] * rows[j] for j in range(len(rows)))
+
+    first_row = over_z(8 + 8 * depth, [first_rows[j : j + 1] for j in range(mz)])
+    first_col = over_z(8 + 8 * depth, [first_cols[j : j + 1] for j in range(mz)])
+    corner = first_row[:, 0:1]
+    lane = lax.broadcasted_iota(jnp.int32, (8, my), 1)
+    here = lane == lax.broadcasted_iota(jnp.int32, (8, my), 0)
+    ends = [jnp.sum(jnp.where(here, corners[ab], 0.0), axis=1, keepdims=True) for ab in range(2)]
+    spread = jnp.zeros((outs, my), jnp.float32)
+    chunks = {
+        (1, 0): over_z(8, [sums[z][0] for z in range(depth)]) - kappa_x * (first_row - first_y * corner),
+        (2, 0): over_z(8, [sums[z][1] for z in range(depth)]),
+        (0, 1): by_x[:outs] - (kappa_y * (first_col - first_x * corner))[:outs],
+        (0, 2): by_x[outs : 2 * outs],
+        (1, 1): spread + ends[0][:outs] - kappa_x * kappa_y * corner[:outs],
+        (1, 2): spread + ends[0][outs : 2 * outs],
+        (2, 1): spread + ends[1][:outs],
+        (2, 2): spread + ends[1][outs : 2 * outs],
+    }
+    for (sx, sy), rows in chunks.items():
+        kind = (sx * 3 + sy) * 3
+        kinds[kind, 0:mz, :] = rows[:mz]
+        kinds[kind + 1, 0:1, :] = rows[mz : mz + 1]
+        kinds[kind + 2, 0:1, :] = rows[mz + 1 : mz + 2]
     for sx in range(3):
         for sy in range(3):
-            halo = jnp.concatenate(first_cols if sx == 0 else first_rows, axis=0)
             for sz in range(3):
-                kinds[(sx * 3 + sy) * 3 + sz, mz : 2 * mz, :] = halo
+                kinds[(sx * 3 + sy) * 3 + sz, mz : 2 * mz, :] = first_cols if sx == 0 else first_rows
 
     def side(there, here):
         return jnp.where(there == here, 0, jnp.where(there > here, 1, 2))
@@ -266,9 +267,9 @@
     first_x = jnp.transpose(jnp.broadcast_to(first_x, (8, mx)))[:, 0:1]
     outs = []
     for out in range(mz + 2):
-        value = sum(scalars[pz, out * depth + z] * solved[z] for z in range(depth))
-        base = (mz + 2) * depth + out * mz
-        part = sum(scalars[pz, base + j] * evens[j] for j in range(mz))
+        value = sum(az[8 + 8 * z + out : 9 + 8 * z + out, :] * solved[z] for z in range(depth))
+        base = 8 + 8 * depth + out
+        part = sum(az[base + 8 * j : base + 8 * j + 1, :] * evens[j] for j in range(mz))
         part = part - first_x * part[0:1, :]
         part = part - part[:, 0:1] * first_y
         outs.append(value - part)
@@ -282,7 +283,8 @@
 
 
 def inner_kernel(field, even, *refs):
-    tables, (coefficients, c, top, rows, weights, up_x, up_y), (parts, sem) = refs[:6], refs[6:13], refs[13:]
+    tables, (parts, sem) = refs[:6], refs[14:]
+    coefficients, c, top, rows, weights, columns, up_x, up_y = refs[6:14]
     px, py, pz = lax.axis_index("gx"), lax.axis_index("gy"), lax.axis_index("gz")
     depth, height, breadth = field.shape
     mz = even.shape[0]
@@ -309,17 +311,21 @@
     for copy in fetches:
         copy.wait()
     weights[...] = parts[0] * parts[1] * parts[2]
+    blank = jnp.zeros((columns.shape[1] - weights.shape[0], weights.shape[1]), jnp.float32)
+    columns[...] = jnp.transpose(jnp.concatenate([weights[...], blank], axis=0))
     for copy in copies:
         copy.wait()
 
 
-def gather_kernel(received, weights, got):
-    got[...] = three_pass(split(weights[...]), split(received[...]))
+def gather_kernel(received, weights, columns, got, got_columns):
+    chunks = split(received[...])
+    got_columns[...] = three_pass(chunks, split(columns[...]), ((0,), (0,)))
+    got[...] = three_pass(split(weights[...]), chunks)
 
 
 def finish_kernel(*refs):
-    got, rows, up_x, up_y, inner, top, own, one, two, three, first, partial = refs[:12]
-    coefficients, coarse, last_plane, rim, foot, values, sem = refs[12:]
+    got, got_columns, rows, up_x, up_y, inner, top, own, one, two, three, first, partial = refs[:13]
+    coefficients, coarse, last_plane, rim, foot, values, sem = refs[13:]
     del partial
     mz, mx, my = own.shape
     depth, height, breadth = 2 * mz, 2 * mx, 2 * my
@@ -341,11 +347,10 @@
 
     base = 9 * mz
     layers = mz + 1
-    halo_x, halo_y, halo_xy = (got[base + i * layers : base + (i + 1) * layers] for i in range(3))
+    halo_x, halo_xy = got[base : base + layers], got[base + 2 * layers : base + 3 * layers]
     pad = jnp.zeros((8 - layers, halo_x.shape[1]), jnp.float32)
     row = exact_right(jnp.concatenate([halo_x, pad], axis=0), up_right)
-    tall = jnp.concatenate([halo_y, jnp.zeros((128 - layers, halo_y.shape[1]), jnp.float32)], axis=0)
-    col = exact_left(up_left, jnp.transpose(tall))
+    col = exact_left(up_left, got_columns[...])[:, base + layers : base + 2 * layers]
     lane = lax.broadcasted_iota(jnp.int32, (1, 128), 1)
     last = lane == 127
     for z in range(depth):
@@ -435,38 +440,37 @@
     row_x, row_y = vectors(tx, gx, mx), vectors(ty, gy, my)
     line_y, line_x = np.zeros((gy, breadth + 8, 2 * my)), np.zeros((gx, mx + 16, height))
     line_y[:, :breadth, :my] = ty["block"].transpose(0, 2, 1)
-    for out in range(mz + 2):
-        line_y[:, :breadth, my + 2 * out], line_y[:, :breadth, my + 2 * out + 1] = ty["to_right"], ty["to_left"]
+    outs = mz + 2
+    line_y[:, :breadth, my : my + outs] = ty["to_right"][..., None]
+    line_y[:, :breadth, my + outs : my + 2 * outs] = ty["to_left"][..., None]
     line_y[:, 0, my + 2 * (mz + 2) : my + 2 * (mz + 2) + mz] = 1.0
-    line_y[:, breadth, :my] = ty["first"]
+    line_y[:, breadth, :my], line_y[:, breadth + 1, :my] = ty["first"], ty["first_right"][:, None]
     line_x[:, :mx], line_x[:, mx], line_x[:, mx + 1] = tx["block"], tx["to_right"], tx["to_left"]
-    line_x[:, mx + 8, :mx] = tx["first"]
-    fold_z = np.zeros((gz, 8, 128))
-
-    width = max((mz + 2) * (depth + mz) + 2 * gz + 2 * mz, gx, gy)
-    scalars = np.zeros((8 * ((gz + 2 + 7) // 8), 128 * ((width + 127) // 128)))
+    line_x[:, mx + 8, :mx], line_x[:, mx + 9, :mx] = tx["first"], tx["first_right"][:, None]
+
+    fold_z = np.zeros((gz, 8 + 8 * (depth + mz), my))
     for p in range(gz):
         full = np.concatenate([tz["block"][p], tz["to_right"][p : p + 1], tz["to_left"][p : p + 1]], axis=0)
-        nodes = np.zeros((mz + 2, mz))
+        nodes = np.zeros((outs, mz))
         nodes[:mz] = np.eye(mz)
         nodes[:mz, 0] -= tz["first"][p]
         nodes[mz, 0] = tz["first_right"][p]
-        ends = [tz[key][p] for key in ("weight_left", "weight_right", "from_left", "from_right")]
-        line = np.concatenate([full.reshape(-1), nodes.reshape(-1)] + ends)
-        scalars[p, : line.size] = line
-        fold_z[p, :depth, : 2 * (mz + 2)] = np.repeat(full.T, 2, axis=1)
+        fold_z[p, :depth, : 2 * outs] = np.tile(full.T, 2)
         for j in range(mz):
-            fold_z[p, 2 * j, 2 * (mz + 2) + j] = 1.0
-    scalars[gz, :gx], scalars[gz + 1, :gy] = tx["first_right"], ty["first_right"]
-    scalars = f32(scalars)
+            fold_z[p, 2 * j, 2 * outs + j] = 1.0
+        for z in range(depth):
+            fold_z[p, 8 + 8 * z : 8 + 8 * z + outs] = full[:, z : z + 1]
+        for j in range(mz):
+            base = 8 + 8 * (depth + j)
+            fold_z[p, base : base + outs] = nodes[:, j : j + 1]
 
     vmem = pltpu.VMEM
-    operands = (scalars, field, f32(fold_z), f32(line_y), f32(line_x))
+    operands = (field, f32(fold_z), f32(line_y), f32(line_x))
     send, own, even, near, far, first, both_far, kept = call(
         functools.partial(local_kernel, sizes),
         "local",
         [shape(count, 4, my), shape(mz, mx, my), shape(mz, mx, my)] + [shape(mx, my)] * 3 + [shape(2, mx, my), shape(*field.shape)],
-        [HBM] * 5,
+        [HBM] * 4,
         [VMEM] * 8,
         [
             vmem(line_y.shape[1:], jnp.float32),
@@ -475,8 +479,7 @@
             vmem((mz, height, my), jnp.float32),
             vmem((height, 128), jnp.float32),
             vmem((27, 4, my), jnp.float32),
-            pltpu.SMEM(scalars.shape, jnp.float32),
-            pltpu.SemaphoreType.DMA((depth + 4,)),
+            pltpu.SemaphoreType.DMA((depth + 3,)),
         ],
     )(*map(in_hbm, operands))
     received = lax.all_to_all(send, axes, 0, 0, tiled=True).reshape(count * 4, my)
@@ -494,29 +497,29 @@
         row_z[p, 8 + mz : 8 + 2 * mz] = tz["from_right"][p][:, None]
     wx, wy, wz = combine_tables(sizes, tx, ty, tz, mz)
     tables = (row_x, row_y, f32(row_z), wx, wy, wz)
-    partial, inner, top, rows, weights, up_x, up_y = call(
+    partial, inner, top, rows, weights, columns, up_x, up_y = call(
         inner_kernel,
         "inner",
         [shape(*field.shape), shape(depth - 1, height, breadth), shape(height, breadth), shape(32, my)]
-        + [shape(*wx.shape[1:]), shape(height, mx), shape(my, breadth)],
+        + [shape(*wx.shape[1:]), shape(count * 4, 128), shape(height, mx), shape(my, breadth)],
         [VMEM] * 2 + [HBM] * len(tables),
-        [HBM] + [VMEM] * 6,
+        [HBM] + [VMEM] * 7,
         [vmem((3, *wx.shape[1:]), jnp.float32), pltpu.SemaphoreType.DMA((depth + len(tables),))],
     )(kept, even, *map(in_hbm, tables))
-    got = call(
+    got, got_columns = call(
         gather_kernel,
         "gather",
-        shape(wx.shape[1], my),
+        [shape(wx.shape[1], my), shape(mx, 128)],
+        [VMEM] * 3,
         [VMEM] * 2,
-        VMEM,
         flops=10**10,
         size=10**8,
-    )(received, weights)
+    )(received, weights, columns)
     return call(
         finish_kernel,
         "finish",
         [shape(*field.shape), shape(mz, mx, my)],
-        [VMEM] * 11 + [HBM],
+        [VMEM] * 12 + [HBM],
         [HBM, HBM],
         [
             vmem((height, breadth), jnp.float32),
@@ -525,8 +528,8 @@
             vmem((mz, mx, my), jnp.float32),
             pltpu.SemaphoreType.DMA((3 + 2 * depth,)),
         ],
-        {11: 0},
-    )(got, rows, up_x, up_y, inner, top, own, *gets, partial)
+        {12: 0},
+    )(got, got_columns, rows, up_x, up_y, inner, top, own, *gets, partial)
 
 
 def solution(mesh):

time: 20.9 us -> 20.8 us (level)
  transfers between devices with their start and end apart: 5 -> 5, of which waited for: 2 -> 1; matrix products, arithmetic and copies ran while one was open for 0% -> 0% of each run, Pallas kernels for 7% -> 7%
where the time goes in v5:
time: 20.8 us; the launch traced here: 20.6 us
  starting transfers between devices  9.77 us (47%)
  Pallas kernels  6.38 us (31%)
  waiting for transfers between devices  3.77 us (18%)
  between operations  0.69 us (3%)
    all_to_all x1, starting transfers between devices, on_device(): lax.all_to_all(send, axes, 0, 0, tiled=True).reshape(count * 4, my)  7.31 us
    all_to_all x1, waiting for transfers between devices, on_device(): lax.all_to_all(send, axes, 0, 0, tiled=True).reshape(count * 4, my)  3.75 us
    pallas_call x1, Pallas kernels, on_device(): call(functools.partial(local_kernel, sizes), 'local', [shape(count, 4, my...  3.42 us
    ppermute x4, starting transfers between devices, on_device(): lax.ppermute(plane, 'gz', [(i, i ^ hop) for i in range(gz)])  2.46 us
    pallas_call x1, Pallas kernels, on_device(): call(finish_kernel, 'finish', [shape(*field.shape), shape(mz, mx, my)], [...  1.45 us
    pallas_call x1, Pallas kernels, on_device(): call(inner_kernel, 'inner', [shape(*field.shape), shape(depth - 1, height...  1.29 us
  transfers between devices with their start and end apart: 5, of which 1 were waited for; matrix products, arithmetic and copies ran while one was open for 0% of the time, Pallas kernels for 7%

profile of v5, /device:TPU:0, one launch (start us, length us, event | category | flops | bytes accessed | tf_op | source)
XLA Modules:
  0.0 20.6 jit_solution(17339523322902351359)
XLA Ops:
  0.6 3.4 %local.1 = (f32[32,4,128]{2,1,0:T(4,128)}, f32[2,128,128]{2,1,0:T(8,128)S(1)}, f32[2,128,128]{2,1,0:T(8,128)S(1)}, f32[128,128]{1,0:T(8,128)S(1)}, f32[128,128]{...) custom-call(f32[4,256,256]{2,1,0:T(8,128)} %refs_0_.2, ...), custom_call_target="tpu_custom_call" | custom-call | flops 1 | bytes 1 | tf_op jit(solution)/shard_map/local/pallas_call | solution.py:469
  4.1 7.3 %all-to-all-start = ((f32[32,4,128]{2,1,0:T(4,128)}), f32[32,4,128]{2,1,0:T(4,128)S(1)}, u32[]{:S(2)}, u32[]{:S(2)}) async-start(f32[32,4,128]{2,1,0:T(4,128)} %get-tuple-element.20), calls=%async_computation | async-start | bytes 131072 | tf_op jit(solution)/shard_map/all_to_all | solution.py:485
  11.4 0.3 %collective-permute-start = (f32[128,128]{1,0:T(8,128)S(1)}, f32[128,128]{1,0:T(8,128)S(1)}, u32[]{:S(2)}, u32[]{:S(2)}) collective-permute-start(f32[128,128]{1,0:T(8,128)S(1)} %get-tuple-element.33), channel_id=1, source_target_pairs={{0,1},{1,0},{2,3},{3,2},{4,5},{5,4},{6,7},{7,6},{8,9},{9,8},{10,11... | collective-permute-start | bytes 196616 | tf_op jit(solution)/shard_map/ppermute | solution.py:489
  11.7 1.7 %collective-permute-start.1 = (f32[128,128]{1,0:T(8,128)S(1)}, f32[128,128]{1,0:T(8,128)S(1)}, u32[]{:S(2)}, u32[]{:S(2)}) collective-permute-start(f32[128,128]{1,0:T(8,128)S(1)} %get-tuple-element.34), channel_id=1, source_target_pairs={{0,2},{1,3},{2,0},{3,1},{4,6},{5,7},{6,4},{7,5},{8,10},{9,11},{10,... | collective-permute-start | bytes 196616 | tf_op jit(solution)/shard_map/ppermute | solution.py:489
  13.4 0.1 collective-permute-start.3
  13.4 0.4 %collective-permute-start.2 = (f32[2,128,128]{2,1,0:T(8,128)S(1)}, f32[2,128,128]{2,1,0:T(8,128)S(1)}, u32[]{:S(2)}, u32[]{:S(2)}) collective-permute-start(f32[2,128,128]{2,1,0:T(8,128)S(1)} %get-tuple-element.35), channel_id=1, source_target_pairs={{0,3},{1,2},{2,1},{3,0},{4,7},{5,6},{6,5},{7,4},{8,11},{9,10},{10,... | collective-permute-start | bytes 393224 | tf_op jit(solution)/shard_map/ppermute | solution.py:489
  13.8 1.3 %inner.1 = (f32[4,256,256]{2,1,0:T(8,128)}, f32[3,256,256]{2,1,0:T(8,128)S(1)}, f32[256,256]{1,0:T(8,128)S(1)}, f32[32,128]{1,0:T(8,128)S(1)}, f32[32,128]{1,0:T...) custom-call(f32[4,256,256]{2,1,0:T(8,128)S(1)} %get-tuple-element.21.field, ...), custom_call_target="tpu_custom_call" | custom-call | flops 1 | bytes 1 | tf_op jit(solution)/shard_map/inner/pallas_call | solution.py:500
  15.1 3.8 %all-to-all-done = f32[32,4,128]{2,1,0:T(4,128)S(1)} async-done(((f32[32,4,128]{2,1,0:T(4,128)}), f32[32,4,128]{2,1,0:T(4,128)S(1)}, u32[]{:S(2)}, u32[]{:S(2)}) %all-to-all-start) | async-done | bytes 65568 | tf_op jit(solution)/shard_map/all_to_all | solution.py:485
  18.9 0.2 %gather.1 = (f32[32,128]{1,0:T(8,128)S(1)}, f32[128,128]{1,0:T(8,128)S(1)}) custom-call(f32[128,128]{1,0:T(8,128)S(1)} %bitcast.1, f32[32,128]{1,0:T(8,128)S(1)} %get-tuple-element.23.weights, f32[128,128]{1,0:T(8,128)S(1)} %get-tuple-element.24.columns), custom_call_target="tpu_custom_call" | custom-call | flops 10000000000 | bytes 100000000 | tf_op jit(solution)/shard_map/gather/pallas_call | solution.py:509
  19.1 0.0 collective-permute-done.refs_8_
  19.1 0.0 collective-permute-done.1.refs_9_
  19.1 0.0 collective-permute-done.3.refs_11_
  19.1 0.0 collective-permute-done.2.refs_10_
  19.2 1.5 %finish.1 = (f32[4,256,256]{2,1,0:T(8,128)}, f32[2,128,128]{2,1,0:T(8,128)}) custom-call(f32[32,128]{1,0:T(8,128)S(1)} %get-tuple-element.25.refs_0_, f32[128,128]{1,0:T(8,128)S(1)} %get-tuple-element.26.refs_1_, f32[32,128]{1,0:T(8,128)S(1)} %get-tuple-element.27.refs_2_, ...), custom_call_target="tpu_custom_call", output_to_operand_aliasing={{0}: (12, {})} | custom-call | flops 1 | bytes 1 | tf_op jit(solution)/shard_map/finish/pallas_call | solution.py:518
Async XLA Ops:
  4.1 14.8 %all-to-all-start = ((f32[32,4,128]{2,1,0:T(4,128)}), f32[32,4,128]{2,1,0:T(4,128)S(1)}, u32[]{:S(2)}, u32[]{:S(2)}) async-start(f32[32,4,128]{2,1,0:T(4,128)} %get-tuple-element.20), calls=%async_computation | async-start | bytes 131072 | tf_op jit(solution)/shard_map/all_to_all | solution.py:485
  11.4 7.7 %collective-permute-start = (f32[128,128]{1,0:T(8,128)S(1)}, f32[128,128]{1,0:T(8,128)S(1)}, u32[]{:S(2)}, u32[]{:S(2)}) collective-permute-start(f32[128,128]{1,0:T(8,128)S(1)} %get-tuple-element.33), channel_id=1, source_target_pairs={{0,1},{1,0},{2,3},{3,2},{4,5},{5,4},{6,7},{7,6},{8,9},{9,8},{10,11... | collective-permute-start | bytes 196616 | tf_op jit(solution)/shard_map/ppermute | solution.py:489
  11.7 7.4 %collective-permute-start.1 = (f32[128,128]{1,0:T(8,128)S(1)}, f32[128,128]{1,0:T(8,128)S(1)}, u32[]{:S(2)}, u32[]{:S(2)}) collective-permute-start(f32[128,128]{1,0:T(8,128)S(1)} %get-tuple-element.34), channel_id=1, source_target_pairs={{0,2},{1,3},{2,0},{3,1},{4,6},{5,7},{6,4},{7,5},{8,10},{9,11},{10,... | collective-permute-start | bytes 196616 | tf_op jit(solution)/shard_map/ppermute | solution.py:489
  13.4 5.8 %collective-permute-start.3 = (f32[128,128]{1,0:T(8,128)S(1)}, f32[128,128]{1,0:T(8,128)S(1)}, u32[]{:S(2)}, u32[]{:S(2)}) collective-permute-start(f32[128,128]{1,0:T(8,128)S(1)} %get-tuple-element.36), channel_id=1, source_target_pairs={{0,1},{1,0},{2,3},{3,2},{4,5},{5,4},{6,7},{7,6},{8,9},{9,8},{10,11... | collective-permute-start | bytes 196616 | tf_op jit(solution)/shard_map/ppermute | solution.py:489
  13.4 5.7 %collective-permute-start.2 = (f32[2,128,128]{2,1,0:T(8,128)S(1)}, f32[2,128,128]{2,1,0:T(8,128)S(1)}, u32[]{:S(2)}, u32[]{:S(2)}) collective-permute-start(f32[2,128,128]{2,1,0:T(8,128)S(1)} %get-tuple-element.35), channel_id=1, source_target_pairs={{0,3},{1,2},{2,1},{3,0},{4,7},{5,6},{6,5},{7,4},{8,11},{9,10},{10,... | collective-permute-start | bytes 393224 | tf_op jit(solution)/shard_map/ppermute | solution.py:489

commit v6 on v5

--- a/solution.py
+++ b/solution.py
@@ -165,8 +165,8 @@
 
 def local_kernel(sizes, *refs):
     field, fold_z, line_y, line_x = refs[:4]
-    send, own, even, near, far, first, both_far, f = refs[4:12]
-    ry, bx, az, picked, column, kinds, sem = refs[12:]
+    send, own, even, near, far, first, f = refs[4:11]
+    ry, bx, az, picked, column, kinds, sem = refs[11:]
     gx, gy, gz = sizes
     px, py, pz = lax.axis_index("gx"), lax.axis_index("gy"), lax.axis_index("gz")
     depth, height, breadth = field.shape
@@ -277,8 +277,6 @@
         own[j] = evens[j] + outs[j]
     near[...] = jnp.where(pz % 2 == 0, outs[mz], outs[mz + 1])
     far[...] = jnp.where(pz % 4 < 2, outs[mz], outs[mz + 1])
-    both_far[0] = jnp.where(pz % 4 < 2, outs[mz], outs[mz + 1])
-    both_far[1] = evens[0]
     first[...] = evens[0]
 
 
@@ -324,8 +322,8 @@
 
 
 def finish_kernel(*refs):
-    got, got_columns, rows, up_x, up_y, inner, top, own, one, two, three, first, partial = refs[:13]
-    coefficients, coarse, last_plane, rim, foot, values, sem = refs[13:]
+    got, got_columns, rows, up_x, up_y, inner, top, own, one, two, three, first, first_far, partial = refs[:14]
+    coefficients, coarse, last_plane, rim, foot, values, sem = refs[14:]
     del partial
     mz, mx, my = own.shape
     depth, height, breadth = 2 * mz, 2 * mx, 2 * my
@@ -335,10 +333,10 @@
     def row_at(i):
         return rows[16 + i : 17 + i, :]
 
-    planes = (one[...], two[...], three[0])
+    planes = (one[...], two[...], three[...])
     left = sum(row_at(i) * plane for i, plane in enumerate(planes))
     right = sum(row_at(3 + i) * plane for i, plane in enumerate(planes))
-    ahead = row_at(6) * first[...] + row_at(7) * three[1]
+    ahead = row_at(6) * first[...] + row_at(7) * first_far[...]
     up_left, up_right = up_x[...].astype(jnp.bfloat16), up_y[...].astype(jnp.bfloat16)
     last_plane[...] = top[...] - 0.5 * exact_right(exact_left(up_left, ahead), up_right)
     copies = [pltpu.make_async_copy(last_plane.at[body], coefficients.at[depth - 1, *body], sem.at[0])]
@@ -466,12 +464,12 @@
 
     vmem = pltpu.VMEM
     operands = (field, f32(fold_z), f32(line_y), f32(line_x))
-    send, own, even, near, far, first, both_far, kept = call(
+    send, own, even, near, far, first, kept = call(
         functools.partial(local_kernel, sizes),
         "local",
-        [shape(count, 4, my), shape(mz, mx, my), shape(mz, mx, my)] + [shape(mx, my)] * 3 + [shape(2, mx, my), shape(*field.shape)],
+        [shape(count, 4, my), shape(mz, mx, my), shape(mz, mx, my)] + [shape(mx, my)] * 3 + [shape(*field.shape)],
         [HBM] * 4,
-        [VMEM] * 8,
+        [VMEM] * 7,
         [
             vmem(line_y.shape[1:], jnp.float32),
             vmem(line_x.shape[1:], jnp.float32),
@@ -485,8 +483,12 @@
     received = lax.all_to_all(send, axes, 0, 0, tiled=True).reshape(count * 4, my)
 
     assert gz == 4
-    plans = ((near, 1), (far, 2), (both_far, 3), (first, 1))
-    gets = [lax.ppermute(plane, "gz", [(i, i ^ hop) for i in range(gz)]) for plane, hop in plans]
+
+    def exchange(plane, hop):
+        return lax.ppermute(plane, "gz", [(i, i ^ hop) for i in range(gz)])
+
+    from_far = exchange(far, 3)
+    gets = (exchange(near, 1), exchange(from_far, 1), from_far, exchange(first, 1), exchange(first, 3))
 
     row_z = np.zeros((gz, 16, my))
     for p in range(gz):
@@ -519,7 +521,7 @@
         finish_kernel,
         "finish",
         [shape(*field.shape), shape(mz, mx, my)],
-        [VMEM] * 12 + [HBM],
+        [VMEM] * 13 + [HBM],
         [HBM, HBM],
         [
             vmem((height, breadth), jnp.float32),
@@ -528,7 +530,7 @@
             vmem((mz, mx, my), jnp.float32),
             pltpu.SemaphoreType.DMA((3 + 2 * depth,)),
         ],
-        {12: 0},
+        {13: 0},
     )(got, got_columns, rows, up_x, up_y, inner, top, own, *gets, partial)
 
 

time: 20.8 us -> 20.7 us (level)
  waiting for transfers between devices: 3.77 us -> 3.27 us
  starting transfers between devices: 9.77 us -> 10.2 us
    all_to_all x1, waiting for transfers between devices: 3.75 us -> 2.61 us  [on_device(): lax.all_to_all(send, axes, 0, 0, tiled=True).reshape(count * 4, my)]
    ppermute x4 -> x5, waiting for transfers between devices: 0.01 us -> 0.66 us  [exchange(): return lax.ppermute(plane, 'gz', [(i, i ^ hop) for i in range(gz)])]
    ppermute x4 -> x5, starting transfers between devices: 2.46 us -> 2.85 us  [exchange(): return lax.ppermute(plane, 'gz', [(i, i ^ hop) for i in range(gz)])]
  transfers between devices with their start and end apart: 5 -> 6, of which waited for: 1 -> 2; matrix products, arithmetic and copies ran while one was open for 0% -> 0% of each run, Pallas kernels for 7% -> 7%
where the time goes in v6:
time: 20.7 us; the launch traced here: 20.5 us
  starting transfers between devices  10.2 us (49%)
  Pallas kernels  6.37 us (31%)
  waiting for transfers between devices  3.27 us (16%)
  between operations  0.7 us (3%)
    all_to_all x1, starting transfers between devices, on_device(): lax.all_to_all(send, axes, 0, 0, tiled=True).reshape(count * 4, my)  7.31 us
    pallas_call x1, Pallas kernels, on_device(): call(functools.partial(local_kernel, sizes), 'local', [shape(count, 4, my...  3.42 us
    ppermute x5, starting transfers between devices, exchange(): return lax.ppermute(plane, 'gz', [(i, i ^ hop) for i in range(gz)])  2.85 us
    all_to_all x1, waiting for transfers between devices, on_device(): lax.all_to_all(send, axes, 0, 0, tiled=True).reshape(count * 4, my)  2.61 us
    pallas_call x1, Pallas kernels, on_device(): call(finish_kernel, 'finish', [shape(*field.shape), shape(mz, mx, my)], [...  1.45 us
    pallas_call x1, Pallas kernels, on_device(): call(inner_kernel, 'inner', [shape(*field.shape), shape(depth - 1, height...  1.29 us
    ppermute x5, waiting for transfers between devices, exchange(): return lax.ppermute(plane, 'gz', [(i, i ^ hop) for i in range(gz)])  0.66 us
  transfers between devices with their start and end apart: 6, of which 2 were waited for; matrix products, arithmetic and copies ran while one was open for 0% of the time, Pallas kernels for 7%

profile of v6, /device:TPU:0, one launch (start us, length us, event | category | flops | bytes accessed | tf_op | source)
XLA Modules:
  0.0 20.5 jit_solution(16699281976068771202)
XLA Ops:
  0.6 3.4 %local.1 = (f32[32,4,128]{2,1,0:T(4,128)}, f32[2,128,128]{2,1,0:T(8,128)S(1)}, f32[2,128,128]{2,1,0:T(8,128)S(1)}, f32[128,128]{1,0:T(8,128)S(1)}, f32[128,128]{...) custom-call(f32[4,256,256]{2,1,0:T(8,128)} %refs_0_.2, f32[4,56,128]{2,1,0:T(8,128)} %constant.18.clone.refs_1_, ...), custom_call_target="tpu_custom_call" | custom-call | flops 1 | bytes 1 | tf_op jit(solution)/shard_map/local/pallas_call | solution.py:467
  4.1 7.3 %all-to-all-start = ((f32[32,4,128]{2,1,0:T(4,128)}), f32[32,4,128]{2,1,0:T(4,128)S(1)}, u32[]{:S(2)}, u32[]{:S(2)}) async-start(f32[32,4,128]{2,1,0:T(4,128)} %get-tuple-element.19), calls=%async_computation | async-start | bytes 131072 | tf_op jit(solution)/shard_map/all_to_all | solution.py:483
  11.4 1.6 %collective-permute-start.1 = (f32[128,128]{1,0:T(8,128)S(1)}, f32[128,128]{1,0:T(8,128)S(1)}, u32[]{:S(2)}, u32[]{:S(2)}) collective-permute-start(f32[128,128]{1,0:T(8,128)S(1)} %get-tuple-element.33), channel_id=1, source_target_pairs={{0,3},{1,2},{2,1},{3,0},{4,7},{5,6},{6,5},{7,4},{8,11},{9,10},{10,... | collective-permute-start | bytes 196616 | tf_op jit(solution)/shard_map/ppermute | solution.py:488
  13.0 0.4 %collective-permute-start.3 = (f32[128,128]{1,0:T(8,128)S(1)}, f32[128,128]{1,0:T(8,128)S(1)}, u32[]{:S(2)}, u32[]{:S(2)}) collective-permute-start(f32[128,128]{1,0:T(8,128)S(1)} %get-tuple-element.34), channel_id=1, source_target_pairs={{0,1},{1,0},{2,3},{3,2},{4,5},{5,4},{6,7},{7,6},{8,9},{9,8},{10,11... | collective-permute-start | bytes 196616 | tf_op jit(solution)/shard_map/ppermute | solution.py:488
  13.3 0.1 collective-permute-start.4
  13.4 0.3 %collective-permute-start = (f32[128,128]{1,0:T(8,128)S(1)}, f32[128,128]{1,0:T(8,128)S(1)}, u32[]{:S(2)}, u32[]{:S(2)}) collective-permute-start(f32[128,128]{1,0:T(8,128)S(1)} %get-tuple-element.32), channel_id=1, source_target_pairs={{0,1},{1,0},{2,3},{3,2},{4,5},{5,4},{6,7},{7,6},{8,9},{9,8},{10,11... | collective-permute-start | bytes 196616 | tf_op jit(solution)/shard_map/ppermute | solution.py:488
  13.7 1.3 %inner.1 = (f32[4,256,256]{2,1,0:T(8,128)}, f32[3,256,256]{2,1,0:T(8,128)S(1)}, f32[256,256]{1,0:T(8,128)S(1)}, f32[32,128]{1,0:T(8,128)S(1)}, f32[32,128]{1,0:T...) custom-call(f32[4,256,256]{2,1,0:T(8,128)S(1)} %get-tuple-element.20.field, ...), custom_call_target="tpu_custom_call" | custom-call | flops 1 | bytes 1 | tf_op jit(solution)/shard_map/inner/pallas_call | solution.py:502
  15.0 0.6 %collective-permute-done.1.refs_10_ = f32[128,128]{1,0:T(8,128)S(1)} collective-permute-done((f32[128,128]{1,0:T(8,128)S(1)}, f32[128,128]{1,0:T(8,128)S(1)}, u32[]{:S(2)}, u32[]{:S(2)}) %collective-permute-start.1) | collective-permute-done | bytes 65568 | tf_op jit(solution)/shard_map/ppermute | solution.py:488
  15.6 0.5 %collective-permute-start.2 = (f32[128,128]{1,0:T(8,128)S(1)}, f32[128,128]{1,0:T(8,128)S(1)}, u32[]{:S(2)}, u32[]{:S(2)}) collective-permute-start(f32[128,128]{1,0:T(8,128)S(1)} %collective-permute-done.1.refs_10_), channel_id=1, source_target_pairs={{0,1},{1,0},{2,3},{3,2},{4,5},{5,4},{6,7},{7,6},{8,9},{9,8},{10,11... | collective-permute-start | bytes 196616 | tf_op jit(solution)/shard_map/ppermute | solution.py:488
  16.2 2.6 %all-to-all-done = f32[32,4,128]{2,1,0:T(4,128)S(1)} async-done(((f32[32,4,128]{2,1,0:T(4,128)}), f32[32,4,128]{2,1,0:T(4,128)S(1)}, u32[]{:S(2)}, u32[]{:S(2)}) %all-to-all-start) | async-done | bytes 65568 | tf_op jit(solution)/shard_map/all_to_all | solution.py:483
  18.8 0.2 %gather.1 = (f32[32,128]{1,0:T(8,128)S(1)}, f32[128,128]{1,0:T(8,128)S(1)}) custom-call(f32[128,128]{1,0:T(8,128)S(1)} %bitcast.1, f32[32,128]{1,0:T(8,128)S(1)} %get-tuple-element.22.weights, f32[128,128]{1,0:T(8,128)S(1)} %get-tuple-element.23.columns), custom_call_target="tpu_custom_call" | custom-call | flops 10000000000 | bytes 100000000 | tf_op jit(solution)/shard_map/gather/pallas_call | solution.py:511
  19.0 0.0 collective-permute-done.3.refs_11_
  19.0 0.0 collective-permute-done.4.refs_12_
  19.0 0.0 collective-permute-done.refs_8_
  19.0 0.0 collective-permute-done.2.refs_9_
  19.0 1.5 %finish.1 = (f32[4,256,256]{2,1,0:T(8,128)}, f32[2,128,128]{2,1,0:T(8,128)}) custom-call(f32[32,128]{1,0:T(8,128)S(1)} %get-tuple-element.24.refs_0_, f32[128,128]{1,0:T(8,128)S(1)} %get-tuple-element.25.refs_1_, f32[32,128]{1,0:T(8,128)S(1)} %get-tuple-element.26.refs_2_, ...), custom_call_target="tpu_custom_call", output_to_operand_aliasing={{0}: (13, {})} | custom-call | flops 1 | bytes 1 | tf_op jit(solution)/shard_map/finish/pallas_call | solution.py:520
Async XLA Ops:
  4.1 14.7 %all-to-all-start = ((f32[32,4,128]{2,1,0:T(4,128)}), f32[32,4,128]{2,1,0:T(4,128)S(1)}, u32[]{:S(2)}, u32[]{:S(2)}) async-start(f32[32,4,128]{2,1,0:T(4,128)} %get-tuple-element.19), calls=%async_computation | async-start | bytes 131072 | tf_op jit(solution)/shard_map/all_to_all | solution.py:483
  11.4 4.3 %collective-permute-start.1 = (f32[128,128]{1,0:T(8,128)S(1)}, f32[128,128]{1,0:T(8,128)S(1)}, u32[]{:S(2)}, u32[]{:S(2)}) collective-permute-start(f32[128,128]{1,0:T(8,128)S(1)} %get-tuple-element.33), channel_id=1, source_target_pairs={{0,3},{1,2},{2,1},{3,0},{4,7},{5,6},{6,5},{7,4},{8,11},{9,10},{10,... | collective-permute-start | bytes 196616 | tf_op jit(solution)/shard_map/ppermute | solution.py:488
  13.0 6.0 %collective-permute-start.3 = (f32[128,128]{1,0:T(8,128)S(1)}, f32[128,128]{1,0:T(8,128)S(1)}, u32[]{:S(2)}, u32[]{:S(2)}) collective-permute-start(f32[128,128]{1,0:T(8,128)S(1)} %get-tuple-element.34), channel_id=1, source_target_pairs={{0,1},{1,0},{2,3},{3,2},{4,5},{5,4},{6,7},{7,6},{8,9},{9,8},{10,11... | collective-permute-start | bytes 196616 | tf_op jit(solution)/shard_map/ppermute | solution.py:488
  13.3 5.7 %collective-permute-start.4 = (f32[128,128]{1,0:T(8,128)S(1)}, f32[128,128]{1,0:T(8,128)S(1)}, u32[]{:S(2)}, u32[]{:S(2)}) collective-permute-start(f32[128,128]{1,0:T(8,128)S(1)} %get-tuple-element.34), channel_id=1, source_target_pairs={{0,3},{1,2},{2,1},{3,0},{4,7},{5,6},{6,5},{7,4},{8,11},{9,10},{10,... | collective-permute-start | bytes 196616 | tf_op jit(solution)/shard_map/ppermute | solution.py:488
  13.4 5.6 %collective-permute-start = (f32[128,128]{1,0:T(8,128)S(1)}, f32[128,128]{1,0:T(8,128)S(1)}, u32[]{:S(2)}, u32[]{:S(2)}) collective-permute-start(f32[128,128]{1,0:T(8,128)S(1)} %get-tuple-element.32), channel_id=1, source_target_pairs={{0,1},{1,0},{2,3},{3,2},{4,5},{5,4},{6,7},{7,6},{8,9},{9,8},{10,11... | collective-permute-start | bytes 196616 | tf_op jit(solution)/shard_map/ppermute | solution.py:488
  15.6 3.4 %collective-permute-start.2 = (f32[128,128]{1,0:T(8,128)S(1)}, f32[128,128]{1,0:T(8,128)S(1)}, u32[]{:S(2)}, u32[]{:S(2)}) collective-permute-start(f32[128,128]{1,0:T(8,128)S(1)} %collective-permute-done.1.refs_10_), channel_id=1, source_target_pairs={{0,1},{1,0},{2,3},{3,2},{4,5},{5,4},{6,7},{7,6},{8,9},{9,8},{10,11... | collective-permute-start | bytes 196616 | tf_op jit(solution)/shard_map/ppermute | solution.py:488

commit v7 on v6

--- a/solution.py
+++ b/solution.py
@@ -93,7 +93,7 @@
     gx, gy, gz = sizes
     count = gx * gy * gz
     sender = np.arange(count)
-    qx, qy, qz = sender // (gy * gz), (sender // gz) % gy, sender % gz
+    qx, qy, qz = sender % gx, (sender // gx) % gy, sender // (gy * gx)
     rows = 32
     wx, wy, wz = (np.zeros((parts, rows, count, 4)) for parts in sizes)
 
@@ -255,12 +255,12 @@
 
     if gx * gy * gz <= 32:
         for at in range(gx * gy * gz):
-            scatter(at // (gy * gz), (at // gz) % gy, at % gz, at)
+            scatter(at % gx, (at // gx) % gy, at // (gy * gx), at)
     else:
 
         @pl.loop(0, gx * gy * gz)
         def _(at):
-            scatter(at // (gy * gz), (at // gz) % gy, at % gz, at)
+            scatter(at % gx, (at // gx) % gy, at // (gy * gx), at)
 
     by_all = three_pass(tuple(half[:mx] for half in solve_x), by_split)
     solved = [by_all[:, z * my : (z + 1) * my] for z in range(depth)]
@@ -427,7 +427,7 @@
     depth, height, breadth = field.shape
     mz, mx, my = depth // 2, height // 2, breadth // 2
     count = gx * gy * gz
-    axes = ("gx", "gy", "gz")
+    axes = ("gz", "gy", "gx")
     tx, ty, tz = line_tables(gx, mx), line_tables(gy, my), line_tables(gz, mz)
 
     def vectors(t, parts, m):

time: 20.7 us -> 20.6 us (level)
  no operation moved by 1% of the time
where the time goes in v7:
time: 20.6 us; the launch traced here: 20.4 us
  starting transfers between devices  10.2 us (50%)
  Pallas kernels  6.37 us (31%)
  waiting for transfers between devices  3.08 us (15%)
  between operations  0.7 us (3%)
    all_to_all x1, starting transfers between devices, on_device(): lax.all_to_all(send, axes, 0, 0, tiled=True).reshape(count * 4, my)  7.31 us
    pallas_call x1, Pallas kernels, on_device(): call(functools.partial(local_kernel, sizes), 'local', [shape(count, 4, my...  3.42 us
    ppermute x5, starting transfers between devices, exchange(): return lax.ppermute(plane, 'gz', [(i, i ^ hop) for i in range(gz)])  2.9 us
    all_to_all x1, waiting for transfers between devices, on_device(): lax.all_to_all(send, axes, 0, 0, tiled=True).reshape(count * 4, my)  2.48 us
    pallas_call x1, Pallas kernels, on_device(): call(finish_kernel, 'finish', [shape(*field.shape), shape(mz, mx, my)], [...  1.45 us
    pallas_call x1, Pallas kernels, on_device(): call(inner_kernel, 'inner', [shape(*field.shape), shape(depth - 1, height...  1.29 us
    ppermute x5, waiting for transfers between devices, exchange(): return lax.ppermute(plane, 'gz', [(i, i ^ hop) for i in range(gz)])  0.6 us
  transfers between devices with their start and end apart: 6, of which 2 were waited for; matrix products, arithmetic and copies ran while one was open for 0% of the time, Pallas kernels for 7%

profile of v7, /device:TPU:0, one launch (start us, length us, event | category | flops | bytes accessed | tf_op | source)
XLA Modules:
  0.0 20.4 jit_solution(8085932050265382945)
XLA Ops:
  0.6 3.4 %local.1 = (f32[32,4,128]{2,1,0:T(4,128)}, f32[2,128,128]{2,1,0:T(8,128)S(1)}, f32[2,128,128]{2,1,0:T(8,128)S(1)}, f32[128,128]{1,0:T(8,128)S(1)}, f32[128,128]{...) custom-call(f32[4,256,256]{2,1,0:T(8,128)} %refs_0_.2, f32[4,56,128]{2,1,0:T(8,128)} %constant.18.clone.refs_1_, ...), custom_call_target="tpu_custom_call" | custom-call | flops 1 | bytes 1 | tf_op jit(solution)/shard_map/local/pallas_call | solution.py:467
  4.1 7.3 %all-to-all-start = ((f32[32,4,128]{2,1,0:T(4,128)}), f32[32,4,128]{2,1,0:T(4,128)S(1)}, u32[]{:S(2)}, u32[]{:S(2)}) async-start(f32[32,4,128]{2,1,0:T(4,128)} %get-tuple-element.19), calls=%async_computation | async-start | bytes 131072 | tf_op jit(solution)/shard_map/all_to_all | solution.py:483
  11.4 1.6 %collective-permute-start.1 = (f32[128,128]{1,0:T(8,128)S(1)}, f32[128,128]{1,0:T(8,128)S(1)}, u32[]{:S(2)}, u32[]{:S(2)}) collective-permute-start(f32[128,128]{1,0:T(8,128)S(1)} %get-tuple-element.33), channel_id=1, source_target_pairs={{0,3},{1,2},{2,1},{3,0},{4,7},{5,6},{6,5},{7,4},{8,11},{9,10},{10,... | collective-permute-start | bytes 196616 | tf_op jit(solution)/shard_map/ppermute | solution.py:488
  13.0 0.4 %collective-permute-start.3 = (f32[128,128]{1,0:T(8,128)S(1)}, f32[128,128]{1,0:T(8,128)S(1)}, u32[]{:S(2)}, u32[]{:S(2)}) collective-permute-start(f32[128,128]{1,0:T(8,128)S(1)} %get-tuple-element.34), channel_id=1, source_target_pairs={{0,1},{1,0},{2,3},{3,2},{4,5},{5,4},{6,7},{7,6},{8,9},{9,8},{10,11... | collective-permute-start | bytes 196616 | tf_op jit(solution)/shard_map/ppermute | solution.py:488
  13.3 0.1 collective-permute-start.4
  13.4 0.3 %collective-permute-start = (f32[128,128]{1,0:T(8,128)S(1)}, f32[128,128]{1,0:T(8,128)S(1)}, u32[]{:S(2)}, u32[]{:S(2)}) collective-permute-start(f32[128,128]{1,0:T(8,128)S(1)} %get-tuple-element.32), channel_id=1, source_target_pairs={{0,1},{1,0},{2,3},{3,2},{4,5},{5,4},{6,7},{7,6},{8,9},{9,8},{10,11... | collective-permute-start | bytes 196616 | tf_op jit(solution)/shard_map/ppermute | solution.py:488
  13.7 1.3 %inner.1 = (f32[4,256,256]{2,1,0:T(8,128)}, f32[3,256,256]{2,1,0:T(8,128)S(1)}, f32[256,256]{1,0:T(8,128)S(1)}, f32[32,128]{1,0:T(8,128)S(1)}, f32[32,128]{1,0:T...) custom-call(f32[4,256,256]{2,1,0:T(8,128)S(1)} %get-tuple-element.20.field, ...), custom_call_target="tpu_custom_call" | custom-call | flops 1 | bytes 1 | tf_op jit(solution)/shard_map/inner/pallas_call | solution.py:502
  15.0 0.6 %collective-permute-done.1.refs_10_ = f32[128,128]{1,0:T(8,128)S(1)} collective-permute-done((f32[128,128]{1,0:T(8,128)S(1)}, f32[128,128]{1,0:T(8,128)S(1)}, u32[]{:S(2)}, u32[]{:S(2)}) %collective-permute-start.1) | collective-permute-done | bytes 65568 | tf_op jit(solution)/shard_map/ppermute | solution.py:488
  15.6 0.6 %collective-permute-start.2 = (f32[128,128]{1,0:T(8,128)S(1)}, f32[128,128]{1,0:T(8,128)S(1)}, u32[]{:S(2)}, u32[]{:S(2)}) collective-permute-start(f32[128,128]{1,0:T(8,128)S(1)} %collective-permute-done.1.refs_10_), channel_id=1, source_target_pairs={{0,1},{1,0},{2,3},{3,2},{4,5},{5,4},{6,7},{7,6},{8,9},{9,8},{10,11... | collective-permute-start | bytes 196616 | tf_op jit(solution)/shard_map/ppermute | solution.py:488
  16.2 2.5 %all-to-all-done = f32[32,4,128]{2,1,0:T(4,128)S(1)} async-done(((f32[32,4,128]{2,1,0:T(4,128)}), f32[32,4,128]{2,1,0:T(4,128)S(1)}, u32[]{:S(2)}, u32[]{:S(2)}) %all-to-all-start) | async-done | bytes 65568 | tf_op jit(solution)/shard_map/all_to_all | solution.py:483
  18.7 0.2 %gather.1 = (f32[32,128]{1,0:T(8,128)S(1)}, f32[128,128]{1,0:T(8,128)S(1)}) custom-call(f32[128,128]{1,0:T(8,128)S(1)} %bitcast.1, f32[32,128]{1,0:T(8,128)S(1)} %get-tuple-element.22.weights, f32[128,128]{1,0:T(8,128)S(1)} %get-tuple-element.23.columns), custom_call_target="tpu_custom_call" | custom-call | flops 10000000000 | bytes 100000000 | tf_op jit(solution)/shard_map/gather/pallas_call | solution.py:511
  18.9 0.0 collective-permute-done.3.refs_11_
  18.9 0.0 collective-permute-done.4.refs_12_
  18.9 0.0 collective-permute-done.refs_8_
  18.9 0.0 collective-permute-done.2.refs_9_
  18.9 1.5 %finish.1 = (f32[4,256,256]{2,1,0:T(8,128)}, f32[2,128,128]{2,1,0:T(8,128)}) custom-call(f32[32,128]{1,0:T(8,128)S(1)} %get-tuple-element.24.refs_0_, f32[128,128]{1,0:T(8,128)S(1)} %get-tuple-element.25.refs_1_, f32[32,128]{1,0:T(8,128)S(1)} %get-tuple-element.26.refs_2_, ...), custom_call_target="tpu_custom_call", output_to_operand_aliasing={{0}: (13, {})} | custom-call | flops 1 | bytes 1 | tf_op jit(solution)/shard_map/finish/pallas_call | solution.py:520
Async XLA Ops:
  4.1 14.6 %all-to-all-start = ((f32[32,4,128]{2,1,0:T(4,128)}), f32[32,4,128]{2,1,0:T(4,128)S(1)}, u32[]{:S(2)}, u32[]{:S(2)}) async-start(f32[32,4,128]{2,1,0:T(4,128)} %get-tuple-element.19), calls=%async_computation | async-start | bytes 131072 | tf_op jit(solution)/shard_map/all_to_all | solution.py:483
  11.4 4.2 %collective-permute-start.1 = (f32[128,128]{1,0:T(8,128)S(1)}, f32[128,128]{1,0:T(8,128)S(1)}, u32[]{:S(2)}, u32[]{:S(2)}) collective-permute-start(f32[128,128]{1,0:T(8,128)S(1)} %get-tuple-element.33), channel_id=1, source_target_pairs={{0,3},{1,2},{2,1},{3,0},{4,7},{5,6},{6,5},{7,4},{8,11},{9,10},{10,... | collective-permute-start | bytes 196616 | tf_op jit(solution)/shard_map/ppermute | solution.py:488
  13.0 5.9 %collective-permute-start.3 = (f32[128,128]{1,0:T(8,128)S(1)}, f32[128,128]{1,0:T(8,128)S(1)}, u32[]{:S(2)}, u32[]{:S(2)}) collective-permute-start(f32[128,128]{1,0:T(8,128)S(1)} %get-tuple-element.34), channel_id=1, source_target_pairs={{0,1},{1,0},{2,3},{3,2},{4,5},{5,4},{6,7},{7,6},{8,9},{9,8},{10,11... | collective-permute-start | bytes 196616 | tf_op jit(solution)/shard_map/ppermute | solution.py:488
  13.3 5.6 %collective-permute-start.4 = (f32[128,128]{1,0:T(8,128)S(1)}, f32[128,128]{1,0:T(8,128)S(1)}, u32[]{:S(2)}, u32[]{:S(2)}) collective-permute-start(f32[128,128]{1,0:T(8,128)S(1)} %get-tuple-element.34), channel_id=1, source_target_pairs={{0,3},{1,2},{2,1},{3,0},{4,7},{5,6},{6,5},{7,4},{8,11},{9,10},{10,... | collective-permute-start | bytes 196616 | tf_op jit(solution)/shard_map/ppermute | solution.py:488
  13.4 5.5 %collective-permute-start = (f32[128,128]{1,0:T(8,128)S(1)}, f32[128,128]{1,0:T(8,128)S(1)}, u32[]{:S(2)}, u32[]{:S(2)}) collective-permute-start(f32[128,128]{1,0:T(8,128)S(1)} %get-tuple-element.32), channel_id=1, source_target_pairs={{0,1},{1,0},{2,3},{3,2},{4,5},{5,4},{6,7},{7,6},{8,9},{9,8},{10,11... | collective-permute-start | bytes 196616 | tf_op jit(solution)/shard_map/ppermute | solution.py:488
  15.6 3.3 %collective-permute-start.2 = (f32[128,128]{1,0:T(8,128)S(1)}, f32[128,128]{1,0:T(8,128)S(1)}, u32[]{:S(2)}, u32[]{:S(2)}) collective-permute-start(f32[128,128]{1,0:T(8,128)S(1)} %collective-permute-done.1.refs_10_), channel_id=1, source_target_pairs={{0,1},{1,0},{2,3},{3,2},{4,5},{5,4},{6,7},{7,6},{8,9},{9,8},{10,11... | collective-permute-start | bytes 196616 | tf_op jit(solution)/shard_map/ppermute | solution.py:488

commit v8 on v7

--- a/solution.py
+++ b/solution.py
@@ -79,12 +79,6 @@
     }
 
 
-def even_selector(m):
-    pick = np.zeros((2 * m, m))
-    pick[2 * np.arange(m), np.arange(m)] = 1.0
-    return pick
-
-
 def f32(values):
     return np.asarray(values, np.float32)
 
@@ -163,14 +157,14 @@
         copy.start()
 
 
-def local_kernel(sizes, *refs):
+def faces_kernel(sizes, *refs):
     field, fold_z, line_y, line_x = refs[:4]
-    send, own, even, near, far, first, f = refs[4:11]
-    ry, bx, az, picked, column, kinds, sem = refs[11:]
+    send, f, bx, az, by, head = refs[4:10]
+    ry, column, kinds, sem = refs[10:]
     gx, gy, gz = sizes
     px, py, pz = lax.axis_index("gx"), lax.axis_index("gy"), lax.axis_index("gz")
     depth, height, breadth = field.shape
-    mz, mx, my = own.shape
+    mz, mx, my = depth // 2, height // 2, breadth // 2
     planes = [pltpu.make_async_copy(field.at[z], f.at[z], sem.at[z]) for z in range(depth)]
     sources = [(fold_z.at[pz], az), (line_y.at[py], ry), (line_x.at[px], bx)]
     tables = [pltpu.make_async_copy(src, dst, sem.at[depth + i]) for i, (src, dst) in enumerate(sources)]
@@ -182,7 +176,7 @@
     tables[0].wait()
     tables[1].wait()
     weights = split(ry[:breadth])
-    by_y, evens, along_x = [], [], None
+    by_y, tops, along_x = [], [], None
     step = 2
     for start in range(0, depth, step):
         for z in range(start, start + step):
@@ -195,10 +189,7 @@
             folded = result[rows, my:] * az[z : z + 1, :]
             along_x = folded if along_x is None else along_x + folded
             if z % 2 == 0:
-                j = z // 2
-                picked[j] = two_pass((part[0][rows], part[1][rows]), pick_y)
-                evens.append(picked[j, pl.ds(0, mx, stride=2), :])
-                even[j] = evens[j]
+                tops.append(tuple(half[rows][:16] for half in part))
     column[...] = along_x
     edge = jnp.transpose(column[pl.ds(0, mx, stride=2), :])[:16, :]
     for table in tables[2:]:
@@ -207,14 +198,17 @@
     faces = three_pass(solve_x, split(along_x))
     by_x = jnp.transpose(faces[:mx])[:16, :]
     corners = [faces[mx + ab : mx + ab + 1] for ab in range(2)]
-    by_split = split(jnp.concatenate(by_y, axis=1))
+    by[...] = jnp.concatenate(by_y, axis=1)
+    head[...] = ry[breadth : breadth + 8, :my]
+    by_split = split(by[...])
     ends_x = three_pass(tuple(half[mx:] for half in solve_x), by_split)
     sums = [[ends_x[ab : ab + 1, z * my : (z + 1) * my] for ab in range(2)] for z in range(depth)]
 
     first_y, kappa_y = ry[breadth : breadth + 1, :my], ry[breadth + 1 : breadth + 2, :my]
     first_x, kappa_x = bx[mx + 8 : mx + 9, :mx], bx[mx + 9 : mx + 10, :mx]
     outs = mz + 2
-    first_rows = jnp.concatenate([evens[j][0:1, :] for j in range(mz)], axis=0)
+    heads = two_pass(tuple(jnp.concatenate(halves, axis=0) for halves in zip(*tops, strict=True)), pick_y)
+    first_rows = jnp.concatenate([heads[16 * j : 16 * j + 1, :] for j in range(mz)], axis=0)
     first_cols = edge[2 * outs : 2 * outs + mz, :]
 
     def over_z(base, rows):
@@ -262,7 +256,21 @@
         def _(at):
             scatter(at % gx, (at // gx) % gy, at // (gy * gx), at)
 
-    by_all = three_pass(tuple(half[:mx] for half in solve_x), by_split)
+
+def planes_kernel(f, bx, az, by, head, own, even, near, far, first, picked):
+    pz = lax.axis_index("gz")
+    depth, _, breadth = f.shape
+    mz, mx, my = own.shape
+    fine = lax.broadcasted_iota(jnp.int32, (breadth, my), 0)
+    node = lax.broadcasted_iota(jnp.int32, (breadth, my), 1)
+    pick_y = jnp.where(fine == 2 * node, 1.0, 0.0).astype(jnp.bfloat16)
+    evens = []
+    for j in range(mz):
+        picked[j] = two_pass(split(f[2 * j]), pick_y)
+        evens.append(picked[j, pl.ds(0, mx, stride=2), :])
+        even[j] = evens[j]
+    first_y, first_x = head[0:1], bx[mx + 8 : mx + 9, :mx]
+    by_all = three_pass(split(bx[:mx]), split(by[...]))
     solved = [by_all[:, z * my : (z + 1) * my] for z in range(depth)]
     first_x = jnp.transpose(jnp.broadcast_to(first_x, (8, mx)))[:, 0:1]
     outs = []
@@ -464,22 +472,28 @@
 
     vmem = pltpu.VMEM
     operands = (field, f32(fold_z), f32(line_y), f32(line_x))
-    send, own, even, near, far, first, kept = call(
-        functools.partial(local_kernel, sizes),
-        "local",
-        [shape(count, 4, my), shape(mz, mx, my), shape(mz, mx, my)] + [shape(mx, my)] * 3 + [shape(*field.shape)],
+    bx, az = shape(*line_x.shape[1:]), shape(*fold_z.shape[1:])
+    send, kept, *saved = call(
+        functools.partial(faces_kernel, sizes),
+        "faces",
+        [shape(count, 4, my), shape(*field.shape), bx, az, shape(height, depth * my), shape(8, my)],
         [HBM] * 4,
-        [VMEM] * 7,
+        [VMEM] * 6,
         [
             vmem(line_y.shape[1:], jnp.float32),
-            vmem(line_x.shape[1:], jnp.float32),
-            vmem(fold_z.shape[1:], jnp.float32),
-            vmem((mz, height, my), jnp.float32),
             vmem((height, 128), jnp.float32),
             vmem((27, 4, my), jnp.float32),
             pltpu.SemaphoreType.DMA((depth + 3,)),
         ],
     )(*map(in_hbm, operands))
+    own, even, near, far, first = call(
+        planes_kernel,
+        "planes",
+        [shape(mz, mx, my)] * 2 + [shape(mx, my)] * 3,
+        [VMEM] * 5,
+        [VMEM] * 5,
+        [vmem((mz, height, my), jnp.float32)],
+    )(kept, *saved)
     received = lax.all_to_all(send, axes, 0, 0, tiled=True).reshape(count * 4, my)
 
     assert gz == 4

time: 20.6 us -> 20.6 us (level)
  Pallas kernels: 6.37 us -> 6.85 us
  waiting for transfers between devices: 3.08 us -> 2.77 us
    all_to_all x1, waiting for transfers between devices: 2.48 us -> 1.93 us  [on_device(): lax.all_to_all(send, axes, 0, 0, tiled=True).reshape(count * 4, my)]
    pallas_call x1 -> x2, Pallas kernels: 3.42 us -> 3.9 us  [the longest x1 3.4 us: on_device(): call(functools.partial(faces_kernel, sizes), 'faces', [shape(count, 4, my...]
    ppermute x5, waiting for transfers between devices: 0.6 us -> 0.84 us  [exchange(): return lax.ppermute(plane, 'gz', [(i, i ^ hop) for i in range(gz)])]
  transfers between devices with their start and end apart: 6 -> 6, of which waited for: 2 -> 2; matrix products, arithmetic and copies ran while one was open for 0% -> 0% of each run, Pallas kernels for 7% -> 10%
where the time goes in v8:
time: 20.6 us; the launch traced here: 20.3 us
  starting transfers between devices  10 us (49%)
  Pallas kernels  6.85 us (33%)
  waiting for transfers between devices  2.77 us (13%)
  between operations  0.7 us (3%)
    all_to_all x1, starting transfers between devices, on_device(): lax.all_to_all(send, axes, 0, 0, tiled=True).reshape(count * 4, my)  7.3 us
    pallas_call x1, Pallas kernels, on_device(): call(functools.partial(faces_kernel, sizes), 'faces', [shape(count, 4, my...  3.4 us
    ppermute x5, starting transfers between devices, exchange(): return lax.ppermute(plane, 'gz', [(i, i ^ hop) for i in range(gz)])  2.71 us
    all_to_all x1, waiting for transfers between devices, on_device(): lax.all_to_all(send, axes, 0, 0, tiled=True).reshape(count * 4, my)  1.93 us
    pallas_call x1, Pallas kernels, on_device(): call(finish_kernel, 'finish', [shape(*field.shape), shape(mz, mx, my)], [...  1.45 us
    pallas_call x1, Pallas kernels, on_device(): call(inner_kernel, 'inner', [shape(*field.shape), shape(depth - 1, height...  1.29 us
    ppermute x5, waiting for transfers between devices, exchange(): return lax.ppermute(plane, 'gz', [(i, i ^ hop) for i in range(gz)])  0.84 us
    pallas_call x1, Pallas kernels, on_device(): call(planes_kernel, 'planes', [shape(mz, mx, my)] * 2 + [shape(mx, my)] *...  0.5 us
  transfers between devices with their start and end apart: 6, of which 2 were waited for; matrix products, arithmetic and copies ran while one was open for 0% of the time, Pallas kernels for 10%

profile of v8, /device:TPU:0, one launch (start us, length us, event | category | flops | bytes accessed | tf_op | source)
XLA Modules:
  0.0 20.3 jit_solution(14740992861145729461)
XLA Ops:
  0.6 3.4 %faces.1 = (f32[32,4,128]{2,1,0:T(4,128)}, f32[4,256,256]{2,1,0:T(8,128)S(1)}, f32[144,256]{1,0:T(8,128)S(1)}, f32[56,128]{1,0:T(8,128)S(1)}, f32[256,512]{1,0:T(8,128)S(1)}, /*index=5*/f32[8,128]{1,0:T(8,128)S(1)}) custom-call(f32[4,256,256]{2,1,0:T(8,128)} %refs_0_.2, f32[4,56,128]{2,1,0:T(8,128)} %constant.18.clone.refs_1_, ...), custom_call_target="tpu_custom_call" | custom-call | flops 1 | bytes 1 | tf_op jit(solution)/shard_map/faces/pallas_call | solution.py:476
  4.0 7.3 %all-to-all-start = ((f32[32,4,128]{2,1,0:T(4,128)}), f32[32,4,128]{2,1,0:T(4,128)S(1)}, u32[]{:S(2)}, u32[]{:S(2)}) async-start(f32[32,4,128]{2,1,0:T(4,128)} %get-tuple-element.23), calls=%async_computation | async-start | bytes 131072 | tf_op jit(solution)/shard_map/all_to_all | solution.py:497
  11.3 0.5 %planes.1 = (f32[2,128,128]{2,1,0:T(8,128)S(1)}, f32[2,128,128]{2,1,0:T(8,128)S(1)}, f32[128,128]{1,0:T(8,128)S(1)}, f32[128,128]{1,0:T(8,128)S(1)}, f32[128,128]{1,0:T(8,128)S(1)}) custom-call(f32[4,256,256]{2,1,0:T(8,128)S(1)} %get-tuple-element.24.f.field, f32[144,256]{1,0:T(8,128)S(1)} %get-tuple-element.25.bx, f32[56,128]{1,0:T(8,128)S(1)} %get-tuple-element.26.az, ...), custom_call_target="tpu_custom_call" | custom-call | flops 1 | bytes 1 | tf_op jit(solution)/shard_map/planes/pallas_call | solution.py:489
  11.9 1.6 %collective-permute-start.1 = (f32[128,128]{1,0:T(8,128)S(1)}, f32[128,128]{1,0:T(8,128)S(1)}, u32[]{:S(2)}, u32[]{:S(2)}) collective-permute-start(f32[128,128]{1,0:T(8,128)S(1)} %get-tuple-element.41), channel_id=1, source_target_pairs={{0,3},{1,2},{2,1},{3,0},{4,7},{5,6},{6,5},{7,4},{8,11},{9,10},{10,... | collective-permute-start | bytes 196616 | tf_op jit(solution)/shard_map/ppermute | solution.py:502
  13.4 0.4 %collective-permute-start.3 = (f32[128,128]{1,0:T(8,128)S(1)}, f32[128,128]{1,0:T(8,128)S(1)}, u32[]{:S(2)}, u32[]{:S(2)}) collective-permute-start(f32[128,128]{1,0:T(8,128)S(1)} %get-tuple-element.42), channel_id=1, source_target_pairs={{0,1},{1,0},{2,3},{3,2},{4,5},{5,4},{6,7},{7,6},{8,9},{9,8},{10,11... | collective-permute-start | bytes 196616 | tf_op jit(solution)/shard_map/ppermute | solution.py:502
  13.8 0.1 collective-permute-start.4
  13.9 0.3 %collective-permute-start = (f32[128,128]{1,0:T(8,128)S(1)}, f32[128,128]{1,0:T(8,128)S(1)}, u32[]{:S(2)}, u32[]{:S(2)}) collective-permute-start(f32[128,128]{1,0:T(8,128)S(1)} %get-tuple-element.40), channel_id=1, source_target_pairs={{0,1},{1,0},{2,3},{3,2},{4,5},{5,4},{6,7},{7,6},{8,9},{9,8},{10,11... | collective-permute-start | bytes 196616 | tf_op jit(solution)/shard_map/ppermute | solution.py:502
  14.2 1.3 %inner.1 = (f32[4,256,256]{2,1,0:T(8,128)}, f32[3,256,256]{2,1,0:T(8,128)S(1)}, f32[256,256]{1,0:T(8,128)S(1)}, f32[32,128]{1,0:T(8,128)S(1)}, f32[32,128]{1,0:T...) custom-call(f32[4,256,256]{2,1,0:T(8,128)S(1)} %get-tuple-element.24.f.field, ...), custom_call_target="tpu_custom_call" | custom-call | flops 1 | bytes 1 | tf_op jit(solution)/shard_map/inner/pallas_call | solution.py:516
  15.5 0.8 %collective-permute-done.1.refs_10_ = f32[128,128]{1,0:T(8,128)S(1)} collective-permute-done((f32[128,128]{1,0:T(8,128)S(1)}, f32[128,128]{1,0:T(8,128)S(1)}, u32[]{:S(2)}, u32[]{:S(2)}) %collective-permute-start.1) | collective-permute-done | bytes 65568 | tf_op jit(solution)/shard_map/ppermute | solution.py:502
  16.3 0.4 %collective-permute-start.2 = (f32[128,128]{1,0:T(8,128)S(1)}, f32[128,128]{1,0:T(8,128)S(1)}, u32[]{:S(2)}, u32[]{:S(2)}) collective-permute-start(f32[128,128]{1,0:T(8,128)S(1)} %collective-permute-done.1.refs_10_), channel_id=1, source_target_pairs={{0,1},{1,0},{2,3},{3,2},{4,5},{5,4},{6,7},{7,6},{8,9},{9,8},{10,11... | collective-permute-start | bytes 196616 | tf_op jit(solution)/shard_map/ppermute | solution.py:502
  16.7 1.9 %all-to-all-done = f32[32,4,128]{2,1,0:T(4,128)S(1)} async-done(((f32[32,4,128]{2,1,0:T(4,128)}), f32[32,4,128]{2,1,0:T(4,128)S(1)}, u32[]{:S(2)}, u32[]{:S(2)}) %all-to-all-start) | async-done | bytes 65568 | tf_op jit(solution)/shard_map/all_to_all | solution.py:497
  18.6 0.2 %gather.1 = (f32[32,128]{1,0:T(8,128)S(1)}, f32[128,128]{1,0:T(8,128)S(1)}) custom-call(f32[128,128]{1,0:T(8,128)S(1)} %bitcast.1, f32[32,128]{1,0:T(8,128)S(1)} %get-tuple-element.30.weights, f32[128,128]{1,0:T(8,128)S(1)} %get-tuple-element.31.columns), custom_call_target="tpu_custom_call" | custom-call | flops 10000000000 | bytes 100000000 | tf_op jit(solution)/shard_map/gather/pallas_call | solution.py:525
  18.8 0.0 collective-permute-done.3.refs_11_
  18.8 0.0 collective-permute-done.4.refs_12_
  18.9 0.0 collective-permute-done.refs_8_
  18.9 0.0 collective-permute-done.2.refs_9_
  18.9 1.5 %finish.1 = (f32[4,256,256]{2,1,0:T(8,128)}, f32[2,128,128]{2,1,0:T(8,128)}) custom-call(f32[32,128]{1,0:T(8,128)S(1)} %get-tuple-element.32.refs_0_, f32[128,128]{1,0:T(8,128)S(1)} %get-tuple-element.33.refs_1_, f32[32,128]{1,0:T(8,128)S(1)} %get-tuple-element.34.refs_2_, ...), custom_call_target="tpu_custom_call", output_to_operand_aliasing={{0}: (13, {})} | custom-call | flops 1 | bytes 1 | tf_op jit(solution)/shard_map/finish/pallas_call | solution.py:534
Async XLA Ops:
  4.0 14.6 %all-to-all-start = ((f32[32,4,128]{2,1,0:T(4,128)}), f32[32,4,128]{2,1,0:T(4,128)S(1)}, u32[]{:S(2)}, u32[]{:S(2)}) async-start(f32[32,4,128]{2,1,0:T(4,128)} %get-tuple-element.23), calls=%async_computation | async-start | bytes 131072 | tf_op jit(solution)/shard_map/all_to_all | solution.py:497
  11.9 4.5 %collective-permute-start.1 = (f32[128,128]{1,0:T(8,128)S(1)}, f32[128,128]{1,0:T(8,128)S(1)}, u32[]{:S(2)}, u32[]{:S(2)}) collective-permute-start(f32[128,128]{1,0:T(8,128)S(1)} %get-tuple-element.41), channel_id=1, source_target_pairs={{0,3},{1,2},{2,1},{3,0},{4,7},{5,6},{6,5},{7,4},{8,11},{9,10},{10,... | collective-permute-start | bytes 196616 | tf_op jit(solution)/shard_map/ppermute | solution.py:502
  13.4 5.4 %collective-permute-start.3 = (f32[128,128]{1,0:T(8,128)S(1)}, f32[128,128]{1,0:T(8,128)S(1)}, u32[]{:S(2)}, u32[]{:S(2)}) collective-permute-start(f32[128,128]{1,0:T(8,128)S(1)} %get-tuple-element.42), channel_id=1, source_target_pairs={{0,1},{1,0},{2,3},{3,2},{4,5},{5,4},{6,7},{7,6},{8,9},{9,8},{10,11... | collective-permute-start | bytes 196616 | tf_op jit(solution)/shard_map/ppermute | solution.py:502
  13.8 5.0 %collective-permute-start.4 = (f32[128,128]{1,0:T(8,128)S(1)}, f32[128,128]{1,0:T(8,128)S(1)}, u32[]{:S(2)}, u32[]{:S(2)}) collective-permute-start(f32[128,128]{1,0:T(8,128)S(1)} %get-tuple-element.42), channel_id=1, source_target_pairs={{0,3},{1,2},{2,1},{3,0},{4,7},{5,6},{6,5},{7,4},{8,11},{9,10},{10,... | collective-permute-start | bytes 196616 | tf_op jit(solution)/shard_map/ppermute | solution.py:502
  13.9 4.9 %collective-permute-start = (f32[128,128]{1,0:T(8,128)S(1)}, f32[128,128]{1,0:T(8,128)S(1)}, u32[]{:S(2)}, u32[]{:S(2)}) collective-permute-start(f32[128,128]{1,0:T(8,128)S(1)} %get-tuple-element.40), channel_id=1, source_target_pairs={{0,1},{1,0},{2,3},{3,2},{4,5},{5,4},{6,7},{7,6},{8,9},{9,8},{10,11... | collective-permute-start | bytes 196616 | tf_op jit(solution)/shard_map/ppermute | solution.py:502
  16.3 2.6 %collective-permute-start.2 = (f32[128,128]{1,0:T(8,128)S(1)}, f32[128,128]{1,0:T(8,128)S(1)}, u32[]{:S(2)}, u32[]{:S(2)}) collective-permute-start(f32[128,128]{1,0:T(8,128)S(1)} %collective-permute-done.1.refs_10_), channel_id=1, source_target_pairs={{0,1},{1,0},{2,3},{3,2},{4,5},{5,4},{6,7},{7,6},{8,9},{9,8},{10,11... | collective-permute-start | bytes 196616 | tf_op jit(solution)/shard_map/ppermute | solution.py:502

commit v9 on v7

--- a/solution.py
+++ b/solution.py
@@ -93,7 +93,7 @@
     gx, gy, gz = sizes
     count = gx * gy * gz
     sender = np.arange(count)
-    qx, qy, qz = sender % gx, (sender // gx) % gy, sender // (gy * gx)
+    qx, qy, qz = (sender // gy) % gx, sender % gy, sender // (gx * gy)
     rows = 32
     wx, wy, wz = (np.zeros((parts, rows, count, 4)) for parts in sizes)
 
@@ -255,12 +255,12 @@
 
     if gx * gy * gz <= 32:
         for at in range(gx * gy * gz):
-            scatter(at % gx, (at // gx) % gy, at // (gy * gx), at)
+            scatter((at // gy) % gx, at % gy, at // (gx * gy), at)
     else:
 
         @pl.loop(0, gx * gy * gz)
         def _(at):
-            scatter(at % gx, (at // gx) % gy, at // (gy * gx), at)
+            scatter((at // gy) % gx, at % gy, at // (gx * gy), at)
 
     by_all = three_pass(tuple(half[:mx] for half in solve_x), by_split)
     solved = [by_all[:, z * my : (z + 1) * my] for z in range(depth)]
@@ -427,7 +427,7 @@
     depth, height, breadth = field.shape
     mz, mx, my = depth // 2, height // 2, breadth // 2
     count = gx * gy * gz
-    axes = ("gz", "gy", "gx")
+    axes = ("gz", "gx", "gy")
     tx, ty, tz = line_tables(gx, mx), line_tables(gy, my), line_tables(gz, mz)
 
     def vectors(t, parts, m):

time: 20.6 us -> 20.6 us (level)
  no operation moved by 1% of the time
where the time goes in v9:
time: 20.6 us; the launch traced here: 20.4 us
  starting transfers between devices  10.2 us (50%)
  Pallas kernels  6.38 us (31%)
  waiting for transfers between devices  3.06 us (15%)
  between operations  0.7 us (3%)
    all_to_all x1, starting transfers between devices, on_device(): lax.all_to_all(send, axes, 0, 0, tiled=True).reshape(count * 4, my)  7.31 us
    pallas_call x1, Pallas kernels, on_device(): call(functools.partial(local_kernel, sizes), 'local', [shape(count, 4, my...  3.42 us
    ppermute x5, starting transfers between devices, exchange(): return lax.ppermute(plane, 'gz', [(i, i ^ hop) for i in range(gz)])  2.93 us
    all_to_all x1, waiting for transfers between devices, on_device(): lax.all_to_all(send, axes, 0, 0, tiled=True).reshape(count * 4, my)  2.46 us
    pallas_call x1, Pallas kernels, on_device(): call(finish_kernel, 'finish', [shape(*field.shape), shape(mz, mx, my)], [...  1.46 us
    pallas_call x1, Pallas kernels, on_device(): call(inner_kernel, 'inner', [shape(*field.shape), shape(depth - 1, height...  1.29 us
    ppermute x5, waiting for transfers between devices, exchange(): return lax.ppermute(plane, 'gz', [(i, i ^ hop) for i in range(gz)])  0.6 us
  transfers between devices with their start and end apart: 6, of which 2 were waited for; matrix products, arithmetic and copies ran while one was open for 0% of the time, Pallas kernels for 7%

profile of v9, /device:TPU:0, one launch (start us, length us, event | category | flops | bytes accessed | tf_op | source)
XLA Modules:
  0.0 20.4 jit_solution(16412095983065217873)
XLA Ops:
  0.6 3.4 %local.1 = (f32[32,4,128]{2,1,0:T(4,128)}, f32[2,128,128]{2,1,0:T(8,128)S(1)}, f32[2,128,128]{2,1,0:T(8,128)S(1)}, f32[128,128]{1,0:T(8,128)S(1)}, f32[128,128]{...) custom-call(f32[4,256,256]{2,1,0:T(8,128)} %refs_0_.2, f32[4,56,128]{2,1,0:T(8,128)} %constant.18.clone.refs_1_, ...), custom_call_target="tpu_custom_call" | custom-call | flops 1 | bytes 1 | tf_op jit(solution)/shard_map/local/pallas_call | solution.py:467
  4.1 7.3 %all-to-all-start = ((f32[32,4,128]{2,1,0:T(4,128)}), f32[32,4,128]{2,1,0:T(4,128)S(1)}, u32[]{:S(2)}, u32[]{:S(2)}) async-start(f32[32,4,128]{2,1,0:T(4,128)} %get-tuple-element.19), calls=%async_computation | async-start | bytes 131072 | tf_op jit(solution)/shard_map/all_to_all | solution.py:483
  11.4 1.6 %collective-permute-start.1 = (f32[128,128]{1,0:T(8,128)S(1)}, f32[128,128]{1,0:T(8,128)S(1)}, u32[]{:S(2)}, u32[]{:S(2)}) collective-permute-start(f32[128,128]{1,0:T(8,128)S(1)} %get-tuple-element.33), channel_id=1, source_target_pairs={{0,3},{1,2},{2,1},{3,0},{4,7},{5,6},{6,5},{7,4},{8,11},{9,10},{10,... | collective-permute-start | bytes 196616 | tf_op jit(solution)/shard_map/ppermute | solution.py:488
  13.0 0.4 %collective-permute-start.3 = (f32[128,128]{1,0:T(8,128)S(1)}, f32[128,128]{1,0:T(8,128)S(1)}, u32[]{:S(2)}, u32[]{:S(2)}) collective-permute-start(f32[128,128]{1,0:T(8,128)S(1)} %get-tuple-element.34), channel_id=1, source_target_pairs={{0,1},{1,0},{2,3},{3,2},{4,5},{5,4},{6,7},{7,6},{8,9},{9,8},{10,11... | collective-permute-start | bytes 196616 | tf_op jit(solution)/shard_map/ppermute | solution.py:488
  13.3 0.1 collective-permute-start.4
  13.4 0.3 %collective-permute-start = (f32[128,128]{1,0:T(8,128)S(1)}, f32[128,128]{1,0:T(8,128)S(1)}, u32[]{:S(2)}, u32[]{:S(2)}) collective-permute-start(f32[128,128]{1,0:T(8,128)S(1)} %get-tuple-element.32), channel_id=1, source_target_pairs={{0,1},{1,0},{2,3},{3,2},{4,5},{5,4},{6,7},{7,6},{8,9},{9,8},{10,11... | collective-permute-start | bytes 196616 | tf_op jit(solution)/shard_map/ppermute | solution.py:488
  13.7 1.3 %inner.1 = (f32[4,256,256]{2,1,0:T(8,128)}, f32[3,256,256]{2,1,0:T(8,128)S(1)}, f32[256,256]{1,0:T(8,128)S(1)}, f32[32,128]{1,0:T(8,128)S(1)}, f32[32,128]{1,0:T...) custom-call(f32[4,256,256]{2,1,0:T(8,128)S(1)} %get-tuple-element.20.field, ...), custom_call_target="tpu_custom_call" | custom-call | flops 1 | bytes 1 | tf_op jit(solution)/shard_map/inner/pallas_call | solution.py:502
  15.0 0.6 %collective-permute-done.1.refs_10_ = f32[128,128]{1,0:T(8,128)S(1)} collective-permute-done((f32[128,128]{1,0:T(8,128)S(1)}, f32[128,128]{1,0:T(8,128)S(1)}, u32[]{:S(2)}, u32[]{:S(2)}) %collective-permute-start.1) | collective-permute-done | bytes 65568 | tf_op jit(solution)/shard_map/ppermute | solution.py:488
  15.6 0.6 %collective-permute-start.2 = (f32[128,128]{1,0:T(8,128)S(1)}, f32[128,128]{1,0:T(8,128)S(1)}, u32[]{:S(2)}, u32[]{:S(2)}) collective-permute-start(f32[128,128]{1,0:T(8,128)S(1)} %collective-permute-done.1.refs_10_), channel_id=1, source_target_pairs={{0,1},{1,0},{2,3},{3,2},{4,5},{5,4},{6,7},{7,6},{8,9},{9,8},{10,11... | collective-permute-start | bytes 196616 | tf_op jit(solution)/shard_map/ppermute | solution.py:488
  16.2 2.5 %all-to-all-done = f32[32,4,128]{2,1,0:T(4,128)S(1)} async-done(((f32[32,4,128]{2,1,0:T(4,128)}), f32[32,4,128]{2,1,0:T(4,128)S(1)}, u32[]{:S(2)}, u32[]{:S(2)}) %all-to-all-start) | async-done | bytes 65568 | tf_op jit(solution)/shard_map/all_to_all | solution.py:483
  18.7 0.2 %gather.1 = (f32[32,128]{1,0:T(8,128)S(1)}, f32[128,128]{1,0:T(8,128)S(1)}) custom-call(f32[128,128]{1,0:T(8,128)S(1)} %bitcast.1, f32[32,128]{1,0:T(8,128)S(1)} %get-tuple-element.22.weights, f32[128,128]{1,0:T(8,128)S(1)} %get-tuple-element.23.columns), custom_call_target="tpu_custom_call" | custom-call | flops 10000000000 | bytes 100000000 | tf_op jit(solution)/shard_map/gather/pallas_call | solution.py:511
  18.9 0.0 collective-permute-done.3.refs_11_
  18.9 0.0 collective-permute-done.4.refs_12_
  18.9 0.0 collective-permute-done.refs_8_
  18.9 0.0 collective-permute-done.2.refs_9_
  18.9 1.5 %finish.1 = (f32[4,256,256]{2,1,0:T(8,128)}, f32[2,128,128]{2,1,0:T(8,128)}) custom-call(f32[32,128]{1,0:T(8,128)S(1)} %get-tuple-element.24.refs_0_, f32[128,128]{1,0:T(8,128)S(1)} %get-tuple-element.25.refs_1_, f32[32,128]{1,0:T(8,128)S(1)} %get-tuple-element.26.refs_2_, ...), custom_call_target="tpu_custom_call", output_to_operand_aliasing={{0}: (13, {})} | custom-call | flops 1 | bytes 1 | tf_op jit(solution)/shard_map/finish/pallas_call | solution.py:520
Async XLA Ops:
  4.1 14.6 %all-to-all-start = ((f32[32,4,128]{2,1,0:T(4,128)}), f32[32,4,128]{2,1,0:T(4,128)S(1)}, u32[]{:S(2)}, u32[]{:S(2)}) async-start(f32[32,4,128]{2,1,0:T(4,128)} %get-tuple-element.19), calls=%async_computation | async-start | bytes 131072 | tf_op jit(solution)/shard_map/all_to_all | solution.py:483
  11.4 4.2 %collective-permute-start.1 = (f32[128,128]{1,0:T(8,128)S(1)}, f32[128,128]{1,0:T(8,128)S(1)}, u32[]{:S(2)}, u32[]{:S(2)}) collective-permute-start(f32[128,128]{1,0:T(8,128)S(1)} %get-tuple-element.33), channel_id=1, source_target_pairs={{0,3},{1,2},{2,1},{3,0},{4,7},{5,6},{6,5},{7,4},{8,11},{9,10},{10,... | collective-permute-start | bytes 196616 | tf_op jit(solution)/shard_map/ppermute | solution.py:488
  13.0 5.9 %collective-permute-start.3 = (f32[128,128]{1,0:T(8,128)S(1)}, f32[128,128]{1,0:T(8,128)S(1)}, u32[]{:S(2)}, u32[]{:S(2)}) collective-permute-start(f32[128,128]{1,0:T(8,128)S(1)} %get-tuple-element.34), channel_id=1, source_target_pairs={{0,1},{1,0},{2,3},{3,2},{4,5},{5,4},{6,7},{7,6},{8,9},{9,8},{10,11... | collective-permute-start | bytes 196616 | tf_op jit(solution)/shard_map/ppermute | solution.py:488
  13.3 5.6 %collective-permute-start.4 = (f32[128,128]{1,0:T(8,128)S(1)}, f32[128,128]{1,0:T(8,128)S(1)}, u32[]{:S(2)}, u32[]{:S(2)}) collective-permute-start(f32[128,128]{1,0:T(8,128)S(1)} %get-tuple-element.34), channel_id=1, source_target_pairs={{0,3},{1,2},{2,1},{3,0},{4,7},{5,6},{6,5},{7,4},{8,11},{9,10},{10,... | collective-permute-start | bytes 196616 | tf_op jit(solution)/shard_map/ppermute | solution.py:488
  13.4 5.5 %collective-permute-start = (f32[128,128]{1,0:T(8,128)S(1)}, f32[128,128]{1,0:T(8,128)S(1)}, u32[]{:S(2)}, u32[]{:S(2)}) collective-permute-start(f32[128,128]{1,0:T(8,128)S(1)} %get-tuple-element.32), channel_id=1, source_target_pairs={{0,1},{1,0},{2,3},{3,2},{4,5},{5,4},{6,7},{7,6},{8,9},{9,8},{10,11... | collective-permute-start | bytes 196616 | tf_op jit(solution)/shard_map/ppermute | solution.py:488
  15.6 3.3 %collective-permute-start.2 = (f32[128,128]{1,0:T(8,128)S(1)}, f32[128,128]{1,0:T(8,128)S(1)}, u32[]{:S(2)}, u32[]{:S(2)}) collective-permute-start(f32[128,128]{1,0:T(8,128)S(1)} %collective-permute-done.1.refs_10_), channel_id=1, source_target_pairs={{0,1},{1,0},{2,3},{3,2},{4,5},{5,4},{6,7},{7,6},{8,9},{9,8},{10,11... | collective-permute-start | bytes 196616 | tf_op jit(solution)/shard_map/ppermute | solution.py:488
